TPU v7x, 32 devices: a whole 2x2x4 slice. The times are simulated.
32 devices in a mesh: frame: 16 (over z, x, core), tile: 2 (over y).
Axes of the slice: x: 2, y: 2, z: 4, core: 2. Of those that a mesh axis runs over, the one named last changes fastest.
Arguments:
- queries: bfloat16 [16, 2, 64, 5120], P('frame', 'tile'), may hold values from -6 to 6
- keys: bfloat16 [16, 2, 64, 5120], P('frame', 'tile'), may hold values from -6 to 6
- values: bfloat16 [16, 2, 64, 5120], P('frame', 'tile'), may hold values from -6 to 6
- step_index: int32 [16], P('frame'), may hold values from 0 to 3
- frame_index: int32 [16], P('frame'), may hold values from 0 to 9
- window_mask: int32 [40, 9], replicated, may hold values 0 or 1
- history_mask: int32 [16, 5], P('frame'), may hold values 0 or 1
- step_gain: float32 [4, 40], replicated, may hold values from 0.5 to 2
Outputs:
- output: bfloat16 [16, 2, 64, 5120], P('frame', 'tile')
All inputs are finite; a program needn't handle non-finite values. No bound on the sum of `history_mask` on one device may be relied on, other than what follows from the above.
Results may differ from a plain program's by a relative error of at most 0.0095.
Values may be sent and summed in bfloat16 or wider, within the bound.
No kernel may reach another device: no remote copies, remote signals or barrier semaphores. Data moves between devices by JAX's collectives and lax.ppermute only.
A program may use at most 128 MiB of HBM per device.

v0:
```python
import math

import jax
import jax.numpy as jnp
from jax import lax
from jax.sharding import PartitionSpec as P

HEADS = 40
HD = 128
TH = 8
TW = 8
BLK = 4
WIN = 5
STEPS = 4


NEG_BIG = -1e30


def from_behind(block, axis, distance):
    devices = range(lax.axis_size(axis))
    route = [(i - distance, i) for i in devices if i - distance in devices]
    return lax.ppermute(block, axis, route)


def offset_code(query_row, query_col, key_row, key_col):
    row_step = key_row // BLK - query_row // BLK
    across = key_col // BLK - query_col // BLK
    nearby = (jnp.abs(row_step) <= 1) & (jnp.abs(across) <= 1)
    return jnp.where(nearby, (row_step + 1) * 3 + across + 1, -1)


def window_allow(offset_ids, mask_rows):
    allowed = (offset_ids == 4)[None]
    for offset in range(9):
        allowed = (
            allowed | (offset_ids == offset)[None] & (mask_rows[:, offset] == 1)[:, None, None]
        )
    return allowed


def empty_state(head_count, row_count):
    return (
        jnp.full((head_count, row_count), NEG_BIG, jnp.float32),
        jnp.zeros((head_count, row_count), jnp.float32),
        jnp.zeros((row_count, head_count, HD), jnp.float32),
    )


def blend(carry_state, query_blk, key_blk, value_blk, allowed):
    running_max, normaliser, summed = carry_state
    scale_factor = 1.0 / math.sqrt(HD)
    scores = (
        jnp.einsum("qhd,khd->hqk", query_blk, key_blk, preferred_element_type=jnp.float32)
        * scale_factor
    )
    scores = jnp.where(allowed, scores, NEG_BIG)
    new_max = jnp.maximum(running_max, jnp.max(scores, axis=2))
    weights = jnp.where(allowed, jnp.exp(scores - new_max[:, :, None]), 0.0)
    factor = jnp.exp(running_max - new_max)
    normaliser = normaliser * factor + jnp.sum(weights, axis=2)
    summed = summed * factor.T[:, :, None] + jnp.einsum(
        "hqk,khd->qhd", weights.astype(jnp.bfloat16), value_blk, preferred_element_type=jnp.float32
    )
    return (new_max, normaliser, summed)


def rim_shift(block_data, distance):
    return from_behind(block_data, "tile", distance)


def shards(queries, keys, values, step_index, frame_index, window_mask, history_mask, step_gain):
    tile_count = lax.axis_size("tile")
    tile_cols = min(tile_count, 4)
    tile_rows = tile_count // tile_cols
    tile_id = lax.axis_index("tile")
    group_id = lax.axis_index("frame")
    channels = queries.shape[-1]
    head_share = HEADS // tile_count
    share_width = channels // tile_count
    tile_tok = queries.shape[2]
    frame_tok = tile_tok * tile_count
    own_q = queries[0, 0]
    own_k = keys[0, 0]
    own_v = values[0, 0]
    picker = (jnp.arange(STEPS, dtype=jnp.int32) == step_index[0]).astype(jnp.float32)
    head_gains = jnp.dot(picker, step_gain, precision=lax.Precision.HIGHEST)
    head_layout = lax.all_to_all(
        jnp.stack([own_q, own_k, own_v]), "tile", split_axis=2, concat_axis=1, tiled=True
    )
    head_q = head_layout[0].reshape(frame_tok, head_share, HD)
    head_kv = head_layout[1:]
    past_list = []
    for distance in range(1, WIN + 1):
        arrived = from_behind(head_kv, "frame", distance)
        usable = (
            (history_mask[0, distance - 1] == 1)
            & (distance <= frame_index[0])
            & (group_id - distance >= 0)
        )
        past_list.append((arrived, usable))
    past_keys = jnp.stack([item[0][0] for item in past_list]).reshape(
        WIN, frame_tok, head_share, HD
    )
    past_vals = jnp.stack([item[0][1] for item in past_list]).reshape(
        WIN, frame_tok, head_share, HD
    )
    past_ok = jnp.stack([item[1] for item in past_list])
    block_rows = min(frame_tok, 512)
    block_count = frame_tok // block_rows

    def one_block(start):
        carry_state = empty_state(head_share, block_rows)
        for which in range(WIN):
            carry_state = blend(
                carry_state, head_q, past_keys[which], past_vals[which], past_ok[which]
            )
        return carry_state

    starts = jnp.arange(block_count, dtype=jnp.int32) * block_rows
    block_max, block_norm, block_sum = lax.map(one_block, starts)
    far_max = jnp.transpose(block_max, (1, 0, 2)).reshape(head_share, frame_tok)
    far_norm = jnp.transpose(block_norm, (1, 0, 2)).reshape(head_share, frame_tok)
    far_sum = block_sum.reshape(frame_tok, head_share, HD)
    tile_kv = jnp.concatenate([own_k, own_v], axis=1).reshape(TH, TW, 2 * channels)
    tile_row = tile_id // tile_cols
    tile_col = tile_id % tile_cols
    from_left = rim_shift(tile_kv[:, TW - BLK :], 1)
    from_right = rim_shift(tile_kv[:, :BLK], -1)
    from_left = jnp.where(tile_col > 0, from_left, jnp.zeros_like(from_left))
    from_right = jnp.where(tile_col < tile_cols - 1, from_right, jnp.zeros_like(from_right))
    widened = jnp.concatenate([from_left, tile_kv, from_right], axis=1)
    if tile_rows > 1:
        from_above = rim_shift(widened[TH - BLK :], tile_cols)
        from_below = rim_shift(widened[:BLK], -tile_cols)
    else:
        from_above = jnp.zeros_like(widened[:BLK])
        from_below = jnp.zeros_like(widened[:BLK])
    padded = jnp.concatenate([from_above, widened, from_below], axis=0).reshape(-1, 2 * channels)
    pad_row = tile_row * TH - BLK + jnp.arange(TH + 2 * BLK, dtype=jnp.int32)
    pad_col = tile_col * TW - BLK + jnp.arange(TW + 2 * BLK, dtype=jnp.int32)
    key_row_all = jnp.repeat(pad_row, TW + 2 * BLK)
    key_col_all = jnp.tile(pad_col, TH + 2 * BLK)
    inside = (
        (key_row_all >= 0)
        & (key_row_all < tile_rows * TH)
        & (key_col_all >= 0)
        & (key_col_all < tile_cols * TW)
    )
    query_pos = jnp.arange(tile_tok, dtype=jnp.int32)
    query_row = tile_row * TH + query_pos // TW
    query_col = tile_col * TW + query_pos % TW
    offset_ids = offset_code(
        query_row[:, None], query_col[:, None], key_row_all[None, :], key_col_all[None, :]
    )
    allowed = window_allow(offset_ids, window_mask) & inside[None, None, :]
    near_max, near_norm, near_sum = blend(
        empty_state(HEADS, tile_tok),
        own_q.reshape(tile_tok, HEADS, HD),
        padded[:, :channels].reshape(-1, HEADS, HD),
        padded[:, channels:].reshape(-1, HEADS, HD),
        allowed,
    )
    sent_back = (
        lax.all_to_all(
            far_max.T.astype(jnp.bfloat16), "tile", split_axis=0, concat_axis=1, tiled=True
        ).astype(jnp.float32),
        lax.all_to_all(
            far_norm.T.astype(jnp.bfloat16), "tile", split_axis=0, concat_axis=1, tiled=True
        ).astype(jnp.float32),
        lax.all_to_all(
            far_sum.reshape(frame_tok, share_width).astype(jnp.bfloat16),
            "tile",
            split_axis=0,
            concat_axis=1,
            tiled=True,
        ).astype(jnp.float32),
    )
    hist_max = sent_back[0].T
    hist_norm = sent_back[1].T
    hist_sum = sent_back[2].reshape(tile_tok, HEADS, HD)
    joint_max = jnp.maximum(near_max, hist_max)
    near_factor = jnp.exp(near_max - joint_max)
    hist_factor = jnp.exp(hist_max - joint_max)
    joint_norm = near_norm * near_factor + hist_norm * hist_factor
    joint_sum = near_sum * near_factor.T[:, :, None] + hist_sum * hist_factor.T[:, :, None]
    finished = joint_sum / joint_norm.T[:, :, None] * head_gains[None, :, None]
    return finished.astype(jnp.bfloat16).reshape(1, 1, tile_tok, channels)


def solution(mesh):
    return jax.shard_map(
        shards,
        mesh=mesh,
        in_specs=(
            P("frame", "tile", None, None),
            P("frame", "tile", None, None),
            P("frame", "tile", None, None),
            P("frame"),
            P("frame"),
            P(),
            P("frame", None),
            P(),
        ),
        out_specs=P("frame", "tile", None, None),
        check_vma=False,
    )
```

profile of v0, /device:TPU:16, one launch (start us, length us, event | category | flops | bytes accessed | tf_op | source)
XLA Modules:
  0.0 297.9 jit_solution(18085457742120290374)
XLA Ops:
  1.7 5.2 %copy.137 = bf16[3,64,5120]{1,0,2:T(4,128)(2,1)} copy(bf16[3,64,5120]{2,1,0:T(8,128)(2,1)S(1)} %pad_maximum_fusion.1) | data formatting | bytes 3932160 | tf_op jit(solution)/shard_map/stack | solution.py:89
  6.9 6.2 %reshape.942 = bf16[2,2,245760]{2,1,0:T(2,128)(2,1)} reshape(bf16[5120,3,64]{2,1,0:T(4,128)(2,1)} %bitcast.254) | data formatting | bytes 3932160
  13.1 4.9 %all-to-all-start = ((bf16[2,2,245760]{2,1,0:T(2,128)(2,1)}), bf16[2,2,245760]{2,1,0:T(2,128)(2,1)}, u32[]{:S(2)}, u32[]{:S(2)}) async-start(bf16[2,2,245760]{2,1,0:T(2,128)(2,1)} %reshape.942), calls=%async_computation | async-start | bytes 3932160 | tf_op jit(solution)/shard_map/all_to_all | solution.py:88
  19.9 6.2 %collective-permute-start = (bf16[8,4,10240]{2,1,0:T(4,128)(2,1)S(1)}, bf16[8,4,10240]{2,1,0:T(4,128)(2,1)}, u32[]{:S(2)}, u32[]{:S(2)}) collective-permute-start(bf16[8,4,10240]{2,1,0:T(4,128)(2,1)S(1)} %get-tuple-element.55), channel_id=1, source_target_pairs={{0,1},{2,3},{4,5},{6,7},{8,9},{10,11},{12,13},{14,15},{16,17},{18,... | collective-permute-start | bytes 1966088 | tf_op jit(solution)/shard_map/ppermute | solution.py:23
  33.6 22.2 %collective-permute-done.1 = bf16[8,4,10240]{2,1,0:T(4,128)(2,1)} collective-permute-done((bf16[8,4,10240]{2,1,0:T(4,128)(2,1)S(1)}, bf16[8,4,10240]{2,1,0:T(4,128)(2,1)}, u32[]{:S(2)}, u32[]{:S(2)}) %collective-permute-start.1) | collective-permute-done | bytes 655392 | tf_op jit(solution)/shard_map/ppermute | solution.py:23
  62.0 4.4 %copy.135 = bf16[256,5120]{0,1:T(8,128)(2,1)} copy(bf16[256,5120]{1,0:T(8,128)(2,1)} %get-tuple-element.54) | data formatting | bytes 5242880 | tf_op jit(solution)/shard_map/slice | solution.py:161
  69.1 5.9 %reshape.943 = bf16[5120,3,64]{2,1,0:T(4,128)(2,1)} reshape(bf16[2,2,245760]{2,1,0:T(2,128)(2,1)} %all-to-all-done) | data formatting | bytes 3932160
  75.0 12.1 %copy.184 = bf16[3,64,2,2560]{3,2,1,0:T(2,128)(2,1)S(1)} copy(bf16[3,64,2,2560]{1,0,3,2:T(4,128)(2,1)} %bitcast.255) | data formatting | bytes 3932160 | tf_op jit(solution)/shard_map/all_to_all | solution.py:88
  94.0 2.9 collective-permute-start.5
  97.1 3.6 %fusion.1 = f32[40,64]{1,0:T(8,128)S(1)} fusion(f32[40,256,64]{1,2,0:T(8,128)S(1)} %get-tuple-element.105, f32[40,64]{1,0:T(8,128)S(1)} %broadcast_maximum_fusion, pred[256]{0:T(512)(128)(4,1)S(1)} %compare_and_fusion, pred[40]{0:T(512)(128)(4,1)S(1)} %get-tuple-element.78, pred[64,256]{1,0:T(8,128)(4,1)S(1)} %get-tuple-element.88, ...), kind=kLoop, calls=%fused_computation.6 | loop fusion | flops 15726080 | bytes 2789992 | tf_op jit(solution)/shard_map/reduce_sum | solution.py:61
  103.1 3.4 %collective-permute-start.3 = (bf16[2,128,2560]{2,1,0:T(8,128)(2,1)}, bf16[2,128,2560]{2,1,0:T(8,128)(2,1)}, u32[]{:S(2)}, u32[]{:S(2)}) collective-permute-start(bf16[2,128,2560]{2,1,0:T(8,128)(2,1)} %bitcast.24), channel_id=1, source_target_pairs={{0,4},{2,6},{4,8},{6,10},{8,12},{10,14},{12,16},{14,18},{16,20},{1... | collective-permute-start | bytes 3932168 | tf_op jit(solution)/shard_map/ppermute | solution.py:23
  109.1 15.4 %collective-permute-done.6 = bf16[2,128,2560]{2,1,0:T(8,128)(2,1)} collective-permute-done((bf16[2,128,2560]{2,1,0:T(8,128)(2,1)}, bf16[2,128,2560]{2,1,0:T(8,128)(2,1)}, u32[]{:S(2)}, u32[]{:S(2)}) %collective-permute-start.6) | collective-permute-done | bytes 1310752 | tf_op jit(solution)/shard_map/ppermute | solution.py:23
  127.3 20.7 %collective-permute-done.5 = bf16[2,128,2560]{2,1,0:T(8,128)(2,1)} collective-permute-done((bf16[2,128,2560]{2,1,0:T(8,128)(2,1)}, bf16[2,128,2560]{2,1,0:T(8,128)(2,1)}, u32[]{:S(2)}, u32[]{:S(2)}) %collective-permute-start.5) | collective-permute-done | bytes 1310752 | tf_op jit(solution)/shard_map/ppermute | solution.py:23
  150.5 13.4 %collective-permute-done.4 = bf16[2,128,2560]{2,1,0:T(8,128)(2,1)} collective-permute-done((bf16[2,128,2560]{2,1,0:T(8,128)(2,1)}, bf16[2,128,2560]{2,1,0:T(8,128)(2,1)}, u32[]{:S(2)}, u32[]{:S(2)}) %collective-permute-start.4) | collective-permute-done | bytes 1310752 | tf_op jit(solution)/shard_map/ppermute | solution.py:23
  166.5 52.6 %collective-permute-done.3 = bf16[2,128,2560]{2,1,0:T(8,128)(2,1)} collective-permute-done((bf16[2,128,2560]{2,1,0:T(8,128)(2,1)}, bf16[2,128,2560]{2,1,0:T(8,128)(2,1)}, u32[]{:S(2)}, u32[]{:S(2)}) %collective-permute-start.3) | collective-permute-done | bytes 1310752 | tf_op jit(solution)/shard_map/ppermute | solution.py:23
  222.4 12.7 %collective-permute-done.2 = bf16[2,128,2560]{2,1,0:T(8,128)(2,1)} collective-permute-done((bf16[2,128,2560]{2,1,0:T(8,128)(2,1)}, bf16[2,128,2560]{2,1,0:T(8,128)(2,1)}, u32[]{:S(2)}, u32[]{:S(2)}) %collective-permute-start.2) | collective-permute-done | bytes 1310752 | tf_op jit(solution)/shard_map/ppermute | solution.py:23
  249.9 2.9 convolution_bitcast_fusion.2
  261.8 3.2 %all-to-all-start.3 = ((bf16[2,2,640]{2,1,0:T(2,128)(2,1)}), bf16[2,2,640]{2,1,0:T(2,128)(2,1)S(1)}, u32[]{:S(2)}, u32[]{:S(2)}) async-start(bf16[2,2,640]{2,1,0:T(2,128)(2,1)} %reshape.946), calls=%async_computation.3 | async-start | bytes 10240 | tf_op jit(solution)/shard_map/all_to_all | solution.py:168
  265.0 3.3 %fusion.20 = bf16[128,20,128]{0,2,1:T(8,128)(2,1)S(1)} fusion(f32[128,20,128]{0,2,1:T(8,128)} %convolution_bitcast_fusion.1, f32[128,20,128]{0,2,1:T(8,128)} %convolution_bitcast_fusion.2, f32[128,20,128]{0,2,1:T(8,128)} %convolution_bitcast_fusion.3, f32[128,20,128]{0,2,1:T(8,128)} %convolution_bitcast_fusion.4, bf16[128,20,128]{0,2,1:T(8,128)(2,1)S(1)} %bitcast.265, ...), kind=kOutput, calls=%fused_computation.36 | convolution fusion | flops 88145920 | bytes 7925761 | tf_op jit(solution)/shard_map/while/body/eval_jaxpr/hqk,khd->qhd/dot_general | solution.py:62
  270.7 3.3 %all-to-all-start.1 = ((bf16[2,2,640]{2,1,0:T(2,128)(2,1)}), bf16[2,2,640]{2,1,0:T(2,128)(2,1)S(1)}, u32[]{:S(2)}, u32[]{:S(2)}) async-start(bf16[2,2,640]{2,1,0:T(2,128)(2,1)} %reshape.944), calls=%async_computation.1 | async-start | bytes 10240 | tf_op jit(solution)/shard_map/all_to_all | solution.py:165
  274.1 3.7 %all-to-all-done.1 = bf16[2,2,640]{2,1,0:T(2,128)(2,1)S(1)} async-done(((bf16[2,2,640]{2,1,0:T(2,128)(2,1)}), bf16[2,2,640]{2,1,0:T(2,128)(2,1)S(1)}, u32[]{:S(2)}, u32[]{:S(2)}) %all-to-all-start.1) | async-done | bytes 5152 | tf_op jit(solution)/shard_map/all_to_all | solution.py:165
  277.8 3.5 %all-to-all-start.2 = ((bf16[2,64,2560]{2,1,0:T(8,128)(2,1)}), bf16[2,64,2560]{2,1,0:T(8,128)(2,1)S(1)}, u32[]{:S(2)}, u32[]{:S(2)}) async-start(bf16[2,64,2560]{2,1,0:T(8,128)(2,1)} %convert_element_type.79), calls=%async_computation.2 | async-start | bytes 1310720 | tf_op jit(solution)/shard_map/all_to_all | solution.py:171
  281.5 7.1 %all-to-all-done.2 = bf16[2,64,2560]{2,1,0:T(8,128)(2,1)S(1)} async-done(((bf16[2,64,2560]{2,1,0:T(8,128)(2,1)}), bf16[2,64,2560]{2,1,0:T(8,128)(2,1)S(1)}, u32[]{:S(2)}, u32[]{:S(2)}) %all-to-all-start.2) | async-done | bytes 655392 | tf_op jit(solution)/shard_map/all_to_all | solution.py:171
  291.2 5.1 %multiply_convert_fusion = bf16[64,40,128]{2,0,1:T(8,128)(2,1)S(1)} fusion(f32[64,40,128]{2,1,0:T(8,128)S(1)} %reshape.938, bf16[256,40,128]{0,2,1:T(8,128)(2,1)} %bitcast.266, f32[40,256,64]{1,2,0:T(8,128)} %copy-done.8, f32[40,64]{1,0:T(8,128)S(1)} %broadcast_maximum_fusion, f32[40]{0:T(128)S(1)} %copy-done.53, f32[64,40]{0,1:T(8,128)S(1)} %get-tuple-element.27, ...), kind=kOutput, calls=%fused_computation.41 | convolution fusion | flops 185794560 | bytes 7408392 | tf_op jit(solution)/shard_map/hqk,khd->qhd/dot_general | solution.py:62
  (193 shorter events, 68.4 us)
Async XLA Ops:
  13.1 56.0 %all-to-all-start = ((bf16[2,2,245760]{2,1,0:T(2,128)(2,1)}), bf16[2,2,245760]{2,1,0:T(2,128)(2,1)}, u32[]{:S(2)}, u32[]{:S(2)}) async-start(bf16[2,2,245760]{2,1,0:T(2,128)(2,1)} %reshape.942), calls=%async_computation | async-start | bytes 3932160 | tf_op jit(solution)/shard_map/all_to_all | solution.py:88
  18.6 37.2 %collective-permute-start.1 = (bf16[8,4,10240]{2,1,0:T(4,128)(2,1)S(1)}, bf16[8,4,10240]{2,1,0:T(4,128)(2,1)}, u32[]{:S(2)}, u32[]{:S(2)}) collective-permute-start(bf16[8,4,10240]{2,1,0:T(4,128)(2,1)S(1)} %get-tuple-element.56), channel_id=1, source_target_pairs={{1,0},{3,2},{5,4},{7,6},{9,8},{11,10},{13,12},{15,14},{17,16},{19,... | collective-permute-start | bytes 1966088 | tf_op jit(solution)/shard_map/ppermute | solution.py:23
  19.9 37.2 %collective-permute-start = (bf16[8,4,10240]{2,1,0:T(4,128)(2,1)S(1)}, bf16[8,4,10240]{2,1,0:T(4,128)(2,1)}, u32[]{:S(2)}, u32[]{:S(2)}) collective-permute-start(bf16[8,4,10240]{2,1,0:T(4,128)(2,1)S(1)} %get-tuple-element.55), channel_id=1, source_target_pairs={{0,1},{2,3},{4,5},{6,7},{8,9},{10,11},{12,13},{14,15},{16,17},{18,... | collective-permute-start | bytes 1966088 | tf_op jit(solution)/shard_map/ppermute | solution.py:23
  33.2 63.8 %copy-start.35 = (pred[40]{0:T(512)(128)(4,1)}, pred[40]{0:T(512)(128)(4,1)S(1)}, u32[]{:S(2)}) copy-start(pred[40]{0:T(512)(128)(4,1)S(1)} %get-tuple-element.71) | copy-start | bytes 124
  33.2 63.8 %copy-start.37 = (pred[40]{0:T(512)(128)(4,1)}, pred[40]{0:T(512)(128)(4,1)S(1)}, u32[]{:S(2)}) copy-start(pred[40]{0:T(512)(128)(4,1)S(1)} %get-tuple-element.72) | copy-start | bytes 124
  33.2 63.8 %copy-start.39 = (pred[40]{0:T(512)(128)(4,1)}, pred[40]{0:T(512)(128)(4,1)S(1)}, u32[]{:S(2)}) copy-start(pred[40]{0:T(512)(128)(4,1)S(1)} %get-tuple-element.73) | copy-start | bytes 124
  33.2 63.8 %copy-start.41 = (pred[40]{0:T(512)(128)(4,1)}, pred[40]{0:T(512)(128)(4,1)S(1)}, u32[]{:S(2)}) copy-start(pred[40]{0:T(512)(128)(4,1)S(1)} %get-tuple-element.74) | copy-start | bytes 124
  33.3 63.8 %copy-start.43 = (pred[40]{0:T(512)(128)(4,1)}, pred[40]{0:T(512)(128)(4,1)S(1)}, u32[]{:S(2)}) copy-start(pred[40]{0:T(512)(128)(4,1)S(1)} %get-tuple-element.75) | copy-start | bytes 124
  33.3 63.8 %copy-start.45 = (pred[40]{0:T(512)(128)(4,1)}, pred[40]{0:T(512)(128)(4,1)S(1)}, u32[]{:S(2)}) copy-start(pred[40]{0:T(512)(128)(4,1)S(1)} %get-tuple-element.76) | copy-start | bytes 124
  33.3 63.8 %copy-start.47 = (pred[40]{0:T(512)(128)(4,1)}, pred[40]{0:T(512)(128)(4,1)S(1)}, u32[]{:S(2)}) copy-start(pred[40]{0:T(512)(128)(4,1)S(1)} %get-tuple-element.77) | copy-start | bytes 124
  33.3 63.8 %copy-start.49 = (pred[40]{0:T(512)(128)(4,1)}, pred[40]{0:T(512)(128)(4,1)S(1)}, u32[]{:S(2)}) copy-start(pred[40]{0:T(512)(128)(4,1)S(1)} %get-tuple-element.78) | copy-start | bytes 124
  33.3 63.8 %copy-start.51 = (pred[40]{0:T(512)(128)(4,1)}, pred[40]{0:T(512)(128)(4,1)S(1)}, u32[]{:S(2)}) copy-start(pred[40]{0:T(512)(128)(4,1)S(1)} %get-tuple-element.79) | copy-start | bytes 124
  33.5 63.6 %copy-start.17 = (pred[64,256]{1,0:T(8,128)(4,1)}, pred[64,256]{1,0:T(8,128)(4,1)S(1)}, u32[]{:S(2)}) copy-start(pred[64,256]{1,0:T(8,128)(4,1)S(1)} %get-tuple-element.81) | copy-start | bytes 49156
  33.5 63.6 %copy-start.19 = (pred[64,256]{1,0:T(8,128)(4,1)}, pred[64,256]{1,0:T(8,128)(4,1)S(1)}, u32[]{:S(2)}) copy-start(pred[64,256]{1,0:T(8,128)(4,1)S(1)} %get-tuple-element.82) | copy-start | bytes 49156
  33.5 63.6 %copy-start.21 = (pred[64,256]{1,0:T(8,128)(4,1)}, pred[64,256]{1,0:T(8,128)(4,1)S(1)}, u32[]{:S(2)}) copy-start(pred[64,256]{1,0:T(8,128)(4,1)S(1)} %get-tuple-element.83) | copy-start | bytes 49156
  33.5 63.6 %copy-start.23 = (pred[64,256]{1,0:T(8,128)(4,1)}, pred[64,256]{1,0:T(8,128)(4,1)S(1)}, u32[]{:S(2)}) copy-start(pred[64,256]{1,0:T(8,128)(4,1)S(1)} %get-tuple-element.84) | copy-start | bytes 49156
  89.2 35.3 %collective-permute-start.6 = (bf16[2,128,2560]{2,1,0:T(8,128)(2,1)}, bf16[2,128,2560]{2,1,0:T(8,128)(2,1)}, u32[]{:S(2)}, u32[]{:S(2)}) collective-permute-start(bf16[2,128,2560]{2,1,0:T(8,128)(2,1)} %bitcast.24), channel_id=1, source_target_pairs={{0,10},{2,12},{4,14},{6,16},{8,18},{10,20},{12,22},{14,24},{16,26}... | collective-permute-start | bytes 3932168 | tf_op jit(solution)/shard_map/ppermute | solution.py:23
  94.0 54.0 %collective-permute-start.5 = (bf16[2,128,2560]{2,1,0:T(8,128)(2,1)}, bf16[2,128,2560]{2,1,0:T(8,128)(2,1)}, u32[]{:S(2)}, u32[]{:S(2)}) collective-permute-start(bf16[2,128,2560]{2,1,0:T(8,128)(2,1)} %bitcast.24), channel_id=1, source_target_pairs={{0,8},{2,10},{4,12},{6,14},{8,16},{10,18},{12,20},{14,22},{16,24},... | collective-permute-start | bytes 3932168 | tf_op jit(solution)/shard_map/ppermute | solution.py:23
  101.2 62.7 %collective-permute-start.4 = (bf16[2,128,2560]{2,1,0:T(8,128)(2,1)}, bf16[2,128,2560]{2,1,0:T(8,128)(2,1)}, u32[]{:S(2)}, u32[]{:S(2)}) collective-permute-start(bf16[2,128,2560]{2,1,0:T(8,128)(2,1)} %bitcast.24), channel_id=1, source_target_pairs={{0,6},{2,8},{4,10},{6,12},{8,14},{10,16},{12,18},{14,20},{16,22},{... | collective-permute-start | bytes 3932168 | tf_op jit(solution)/shard_map/ppermute | solution.py:23
  103.1 116.0 %collective-permute-start.3 = (bf16[2,128,2560]{2,1,0:T(8,128)(2,1)}, bf16[2,128,2560]{2,1,0:T(8,128)(2,1)}, u32[]{:S(2)}, u32[]{:S(2)}) collective-permute-start(bf16[2,128,2560]{2,1,0:T(8,128)(2,1)} %bitcast.24), channel_id=1, source_target_pairs={{0,4},{2,6},{4,8},{6,10},{8,12},{10,14},{12,16},{14,18},{16,20},{1... | collective-permute-start | bytes 3932168 | tf_op jit(solution)/shard_map/ppermute | solution.py:23
  106.5 128.5 %collective-permute-start.2 = (bf16[2,128,2560]{2,1,0:T(8,128)(2,1)}, bf16[2,128,2560]{2,1,0:T(8,128)(2,1)}, u32[]{:S(2)}, u32[]{:S(2)}) collective-permute-start(bf16[2,128,2560]{2,1,0:T(8,128)(2,1)} %bitcast.24), channel_id=1, source_target_pairs={{0,2},{2,4},{4,6},{6,8},{8,10},{10,12},{12,14},{14,16},{16,18},{18... | collective-permute-start | bytes 3932168 | tf_op jit(solution)/shard_map/ppermute | solution.py:23
  261.8 8.9 %all-to-all-start.3 = ((bf16[2,2,640]{2,1,0:T(2,128)(2,1)}), bf16[2,2,640]{2,1,0:T(2,128)(2,1)S(1)}, u32[]{:S(2)}, u32[]{:S(2)}) async-start(bf16[2,2,640]{2,1,0:T(2,128)(2,1)} %reshape.946), calls=%async_computation.3 | async-start | bytes 10240 | tf_op jit(solution)/shard_map/all_to_all | solution.py:168
  270.7 7.1 %all-to-all-start.1 = ((bf16[2,2,640]{2,1,0:T(2,128)(2,1)}), bf16[2,2,640]{2,1,0:T(2,128)(2,1)S(1)}, u32[]{:S(2)}, u32[]{:S(2)}) async-start(bf16[2,2,640]{2,1,0:T(2,128)(2,1)} %reshape.944), calls=%async_computation.1 | async-start | bytes 10240 | tf_op jit(solution)/shard_map/all_to_all | solution.py:165
  277.8 10.8 %all-to-all-start.2 = ((bf16[2,64,2560]{2,1,0:T(8,128)(2,1)}), bf16[2,64,2560]{2,1,0:T(8,128)(2,1)S(1)}, u32[]{:S(2)}, u32[]{:S(2)}) async-start(bf16[2,64,2560]{2,1,0:T(8,128)(2,1)} %convert_element_type.79), calls=%async_computation.2 | async-start | bytes 1310720 | tf_op jit(solution)/shard_map/all_to_all | solution.py:171
  (41 other events, 391.7 us)
where the time goes:
time: 299 us; the launch traced here: 298 us
  waiting for transfers between devices  148 us (49%)
  local copies, waits for them, and re-layouts  72.6 us (24%)
  starting transfers between devices  34.9 us (12%)
  matrix products  25.2 us (8%)
  other arithmetic  11.8 us (4%)
  between operations  5.54 us (2%)
    ppermute x7, waiting for transfers between devices, from_behind(): return lax.ppermute(block, axis, route)  137 us
    ppermute x7, starting transfers between devices, from_behind(): return lax.ppermute(block, axis, route)  20 us
    dot_general x6, matrix products, blend(): jnp.einsum('hqk,khd->qhd', weights.astype(jnp.bfloat16), value_blk, prefe...  16.8 us
    unnamed x115, local copies, waits for them, and re-layouts  16.7 us
    slice x9, local copies, waits for them, and re-layouts, shards(): item[0][1]  15.7 us
    all_to_all x1, local copies, waits for them, and re-layouts, shards(): lax.all_to_all(jnp.stack([own_q, own_k, own_v]), 'tile', split_axis=2, co...  12.1 us
    dot_general x6, matrix products, blend(): jnp.einsum('qhd,khd->hqk', query_blk, key_blk, preferred_element_type=jnp...  7.81 us
    all_to_all x1, waiting for transfers between devices, shards(): lax.all_to_all(far_sum.reshape(frame_tok, share_width).astype(jnp.bfloat1...  7.12 us
  transfers between devices with their start and end apart: 11, of which 8 were waited for; matrix products, arithmetic and copies ran while one was open for 14% of the time, Pallas kernels for 0%

commit v1 on v0

v1 whole, which is shorter than its diff:
```python
import functools
import math

import jax
import jax.numpy as jnp
from jax import lax
from jax.experimental import pallas as pl
from jax.experimental.pallas import tpu as pltpu
from jax.sharding import PartitionSpec as P

HEADS = 40
HD = 128
TH = 8
TW = 8
BLK = 4
WIN = 5
STEPS = 4

NEG_BIG = -1e30
CHUNKS = (2, 3)


def group_frames(frame_count, tile_count):
    return max(
        g
        for g in range(1, frame_count + 1)
        if frame_count % g == 0 and HEADS % (g * tile_count) == 0
    )


def first_needed(hop, group):
    return max(0, hop * group - WIN)


def pack(arrays, members, head_share, start, count):
    tokens = arrays[0].shape[0]
    width = count * HD

    def body(*refs):
        out = refs[-1]
        for n in range(members):
            for a, ref in enumerate(refs[:-1]):
                out[n, a] = ref[:, pl.ds((n * head_share + start) * HD, width)]

    vmem = pl.BlockSpec(memory_space=pltpu.VMEM)
    return pl.pallas_call(
        body,
        out_shape=jax.ShapeDtypeStruct((members, len(arrays), tokens, width), jnp.bfloat16),
        in_specs=[vmem] * len(arrays),
        out_specs=vmem,
    )(*arrays)


def unpack(parts, starts, head_share):
    members, tokens = parts[0].shape[:2]

    def body(*refs):
        out = refs[-1]
        for start, ref in zip(starts, refs[:-1]):
            for n in range(members):
                out[:, pl.ds((n * head_share + start) * HD, ref.shape[-1])] = ref[n]

    vmem = pl.BlockSpec(memory_space=pltpu.VMEM)
    return pl.pallas_call(
        body,
        out_shape=jax.ShapeDtypeStruct((tokens, members * head_share * HD), jnp.bfloat16),
        in_specs=[vmem] * len(parts),
        out_specs=vmem,
    )(*parts)


def attend(query, own_kv, hop_kv, bias, past_bias, gains, group):
    members, _, tokens, width = query.shape
    tiles = members // group
    frame_tok = tiles * tokens
    heads = width // HD
    factor = math.log2(math.e) / math.sqrt(HD)
    hops = len(hop_kv)

    def body(*refs):
        past_ref, gain_ref, q_ref, own_ref = refs[:4]
        hop_refs = refs[4 : 4 + hops]
        bias_ref, out_ref = refs[4 + hops :]

        def frame_of(ref, frame, which, lanes):
            return ref[frame * tiles : (frame + 1) * tiles, which, :, lanes].reshape(frame_tok, HD)

        def source(rel):
            if rel >= 0:
                return own_ref, rel
            hop = -(rel // group)
            return hop_refs[hop - 1], rel + hop * group - first_needed(hop, group)

        def one_head(h):
            lanes = pl.ds(h * HD, HD)
            own_bias = bias_ref[h]
            for j in range(group):
                q = frame_of(q_ref, j, 0, lanes)
                scores = []
                for d in range(WIN + 1):
                    ref, frame = source(j - d)
                    k = frame_of(ref, frame, 0, lanes)
                    s = lax.dot_general(
                        q, k, (((1,), (1,)), ((), ())), preferred_element_type=jnp.float32
                    )
                    s = s * factor
                    scores.append(s + own_bias if d == 0 else s + past_ref[j, d - 1])
                top = scores[0]
                for s in scores[1:]:
                    top = jnp.maximum(top, s)
                top = jnp.max(top, axis=1, keepdims=True)
                total = None
                blended = None
                for d in range(WIN + 1):
                    ref, frame = source(j - d)
                    v = frame_of(ref, frame, 1, lanes)
                    p = jnp.exp2(scores[d] - top)
                    total = p if total is None else total + p
                    part = jnp.dot(p.astype(jnp.bfloat16), v, preferred_element_type=jnp.float32)
                    blended = part if blended is None else blended + part
                norm = jnp.sum(total, axis=1, keepdims=True)
                result = (blended * (gain_ref[j, h] / norm)).astype(jnp.bfloat16)
                out_ref[j * tiles : (j + 1) * tiles, :, lanes] = result.reshape(tiles, tokens, HD)

        for h in range(heads):
            one_head(h)

    smem = pl.BlockSpec(memory_space=pltpu.SMEM)
    vmem = pl.BlockSpec(memory_space=pltpu.VMEM)
    keys = frame_tok * (WIN + 1)
    return pl.pallas_call(
        body,
        out_shape=jax.ShapeDtypeStruct((members, tokens, width), jnp.bfloat16),
        in_specs=[smem, smem] + [vmem] * (3 + hops),
        out_specs=vmem,
        cost_estimate=pl.CostEstimate(
            flops=4 * group * heads * frame_tok * keys * HD,
            bytes_accessed=2 * width * tokens * members * 6,
            transcendentals=group * heads * frame_tok * keys,
        ),
        compiler_params=pltpu.CompilerParams(vmem_limit_bytes=48 * 1024 * 1024),
    )(past_bias, gains, query, own_kv, *hop_kv, bias)


def window_bias(mask_rows, tile_count):
    tile_cols = min(tile_count, 4)
    pos = jnp.arange(tile_count * TH * TW, dtype=jnp.int32)
    tile, within = pos // (TH * TW), pos % (TH * TW)
    row = (tile // tile_cols * TH + within // TW) // BLK
    col = (tile % tile_cols * TW + within % TW) // BLK
    down = row[None, :] - row[:, None]
    across = col[None, :] - col[:, None]
    near = (jnp.abs(down) <= 1) & (jnp.abs(across) <= 1)
    code = jnp.where(near, (down + 1) * 3 + across + 1, -1)
    allowed = (code == 4)[None]
    for offset in range(9):
        allowed = allowed | (code == offset)[None] & (mask_rows[:, offset] == 1)[:, None, None]
    return jnp.where(allowed, 0.0, NEG_BIG).astype(jnp.float32)


def shards(queries, keys, values, step_index, frame_index, window_mask, history_mask, step_gain):
    tile_count = lax.axis_size("tile")
    frame_count = lax.axis_size("frame")
    group = group_frames(frame_count, tile_count)
    members = group * tile_count
    head_share = HEADS // members
    frame_id = lax.axis_index("frame")
    member = (frame_id % group) * tile_count + lax.axis_index("tile")
    both = ("frame", "tile")
    teams = [
        [g * members + n for n in range(members)] for g in range(frame_count // group)
    ]
    frame_teams = [[g * group + n for n in range(group)] for g in range(frame_count // group)]

    def exchange(block):
        return lax.all_to_all(block, both, 0, 0, axis_index_groups=teams, tiled=True)

    def from_behind(block, hop):
        step = hop * group
        return lax.ppermute(
            block, "frame", [(i, i + step) for i in range(frame_count) if i + step < frame_count]
        )

    own_q, own_k, own_v = queries[0, 0], keys[0, 0], values[0, 0]

    distance = jnp.arange(1, WIN + 1, dtype=jnp.int32)
    usable = (
        (history_mask[0] == 1) & (distance <= frame_index[0]) & (frame_id - distance >= 0)
    ).astype(jnp.int32)
    facts = jnp.concatenate([usable, step_index])[None]
    if group > 1:
        facts = lax.all_gather(facts, "frame", axis_index_groups=frame_teams, tiled=True)
    past_bias = jnp.where(facts[:, :WIN] == 1, 0.0, NEG_BIG).astype(jnp.float32)
    gains = jnp.zeros((group, head_share), jnp.float32)
    my_gain = lax.dynamic_slice(step_gain, (0, member * head_share), (STEPS, head_share))
    for s in range(STEPS):
        gains = jnp.where(facts[:, WIN:] == s, my_gain[s][None], gains)
    my_mask = lax.dynamic_slice(window_mask, (member * head_share, 0), (head_share, 9))
    bias = window_bias(my_mask, tile_count)

    starts = [sum(CHUNKS[:c]) for c in range(len(CHUNKS))]
    kv = [
        exchange(pack([own_k, own_v], members, head_share, s, n)) for s, n in zip(starts, CHUNKS)
    ]
    q = [exchange(pack([own_q], members, head_share, s, n)) for s, n in zip(starts, CHUNKS)]
    parts = []
    for c, (s, n) in enumerate(zip(starts, CHUNKS)):
        hop_kv, behind, low = [], kv[c], 0
        for hop in range(1, -(-WIN // group) + 1):
            need = first_needed(hop, group)
            behind = from_behind(behind[(need - low) * tile_count :], 1)
            low = need
            hop_kv.append(behind)
        out = attend(
            q[c], kv[c], hop_kv, bias[s : s + n], past_bias, gains[:, s : s + n], group
        )
        parts.append(exchange(out))
    return unpack(parts, starts, head_share)[None, None]


def solution(mesh):
    return jax.shard_map(
        shards,
        mesh=mesh,
        in_specs=(
            P("frame", "tile", None, None),
            P("frame", "tile", None, None),
            P("frame", "tile", None, None),
            P("frame"),
            P("frame"),
            P(),
            P("frame", None),
            P(),
        ),
        out_specs=P("frame", "tile", None, None),
        check_vma=False,
    )
```

time: 299 us -> 93.9 us (0.31)
  the two profiles are of different devices: /device:TPU:16 before, /device:TPU:0 now
where the time goes in v1:
time: 93.9 us; the launch traced here: 93 us
  starting transfers between devices  34.7 us (37%)
  Pallas kernels  20 us (21%)
  blocking collectives  17.6 us (19%)
  waiting for transfers between devices  13.4 us (14%)
  local copies, waits for them, and re-layouts  3.19 us (3%)
  between operations  2.17 us (2%)
  other arithmetic  1.89 us (2%)
    all_to_all x5, starting transfers between devices, exchange(): lax.all_to_all(block, both, 0, 0, axis_index_groups=teams, tiled=True)  19.7 us
    ppermute x4, starting transfers between devices, from_behind(): lax.ppermute(block, 'frame', [(i, i + step) for i in range(frame_count) i...  14.9 us
    all_to_all x1, blocking collectives, exchange(): lax.all_to_all(block, both, 0, 0, axis_index_groups=teams, tiled=True)  11.4 us
    ppermute x4, waiting for transfers between devices, from_behind(): lax.ppermute(block, 'frame', [(i, i + step) for i in range(frame_count) i...  10.5 us
    pallas_call x2, Pallas kernels, attend(): pl.pallas_call(body, out_shape=jax.ShapeDtypeStruct((members, tokens, wid...  10 us
    pallas_call x4, Pallas kernels, pack(): pl.pallas_call(body, out_shape=jax.ShapeDtypeStruct((members, len(arrays)...  8.04 us
    unnamed x1, blocking collectives  6.23 us
    all_to_all x5, waiting for transfers between devices, exchange(): lax.all_to_all(block, both, 0, 0, axis_index_groups=teams, tiled=True)  2.93 us
  transfers between devices with their start and end apart: 9, of which 4 were waited for; matrix products, arithmetic and copies ran while one was open for 5% of the time, Pallas kernels for 17%

profile of v1, /device:TPU:0, one launch (start us, length us, event | category | flops | bytes accessed | tf_op | source)
XLA Modules:
  0.0 93.0 jit_solution(10441151450808095058)
XLA Ops:
  0.0 2.2 %shard_map.86 = bf16[8,2,64,384]{3,2,1,0:T(8,128)(2,1)} custom-call(bf16[64,5120]{1,0:T(8,128)(2,1)} %bitcast.41, bf16[64,5120]{1,0:T(8,128)(2,1)} %bitcast.43), custom_call_target="tpu_custom_call" | custom-call | tf_op jit(solution)/shard_map/pallas_call | solution.py:46
  2.2 5.2 %all-to-all-start.4 = ((bf16[8,2,64,384]{3,2,1,0:T(8,128)(2,1)}), bf16[8,2,64,384]{3,2,1,0:T(8,128)(2,1)S(1)}, u32[]{:S(2)}, u32[]{:S(2)}) async-start(bf16[8,2,64,384]{3,2,1,0:T(8,128)(2,1)} %shard_map.86), calls=%async_computation.4 | async-start | bytes 1572864 | tf_op jit(solution)/shard_map/all_to_all | solution.py:176
  7.4 2.1 %shard_map.83 = bf16[8,2,64,256]{3,2,1,0:T(8,128)(2,1)} custom-call(bf16[64,5120]{1,0:T(8,128)(2,1)} %bitcast.42, bf16[64,5120]{1,0:T(8,128)(2,1)} %bitcast.44), custom_call_target="tpu_custom_call" | custom-call | tf_op jit(solution)/shard_map/pallas_call | solution.py:46
  10.9 0.6 dynamic-slice
  13.0 6.2 %all-reduce = s32[24]{0:T(128)S(1)} all-reduce(s32[24]{0:T(128)S(1)} %add_dynamic-update-slice_fusion), channel_id=2, replica_groups={{0,2,4,6},{8,10,12,14},{16,18,20,22},{24,26,28,30},{1,3,5,7},{9,11,13,1..., use_global_device_ids=true, to_apply=%add | all-reduce | flops 24 | bytes 192
  19.6 3.5 %all-to-all-start.1 = ((bf16[8,2,64,256]{3,2,1,0:T(8,128)(2,1)}), bf16[8,2,64,256]{3,2,1,0:T(8,128)(2,1)S(1)}, u32[]{:S(2)}, u32[]{:S(2)}) async-start(bf16[8,2,64,256]{3,2,1,0:T(8,128)(2,1)} %shard_map.83), calls=%async_computation.1 | async-start | bytes 1048576 | tf_op jit(solution)/shard_map/all_to_all | solution.py:176
  23.2 1.1 %or_select_fusion = f32[5,128,128]{2,1,0:T(8,128)} fusion(pred[128,128]{1,0:T(8,128)(4,1)S(1)} %get-tuple-element.30, pred[128,128]{1,0:T(8,128)(4,1)S(1)} %get-tuple-element.29, pred[128,128]{1,0:T(8,128)(4,1)S(1)} %get-tuple-element.28, pred[128,128]{1,0:T(8,128)(4,1)S(1)} %get-tuple-element.27, pred[128,128]{1,0:T(8,128)(4,1)S(1)} %get-tuple-element.26, ...), kind=kLoop, calls=%fused_computation | loop fusion | flops 1556480 | bytes 475181 | tf_op jit(solution)/shard_map/jit(_where)/select_n | solution.py:158
  24.3 3.6 %collective-permute-start.2 = (bf16[8,2,64,384]{3,2,1,0:T(8,128)(2,1)S(1)}, bf16[8,2,64,384]{3,2,1,0:T(8,128)(2,1)S(1)}, u32[]{:S(2)}, u32[]{:S(2)}) collective-permute-start(bf16[8,2,64,384]{3,2,1,0:T(8,128)(2,1)S(1)} %all-to-all-done.4.refs_3_), channel_id=1, source_target_pairs={{0,8},{2,10},{4,12},{6,14},{8,16},{10,18},{12,20},{14,22},{16,24},... | collective-permute-start | bytes 2359304 | tf_op jit(solution)/shard_map/ppermute | solution.py:180
  28.1 1.8 %shard_map.82 = bf16[8,1,64,256]{3,2,1,0:T(8,128)(2,1)} custom-call(bf16[64,5120]{1,0:T(8,128)(2,1)} %bitcast.45), custom_call_target="tpu_custom_call" | custom-call | tf_op jit(solution)/shard_map/pallas_call | solution.py:46
  29.9 2.0 %all-to-all-done.1.refs_3_ = bf16[8,2,64,256]{3,2,1,0:T(8,128)(2,1)S(1)} async-done(((bf16[8,2,64,256]{3,2,1,0:T(8,128)(2,1)}), bf16[8,2,64,256]{3,2,1,0:T(8,128)(2,1)S(1)}, u32[]{:S(2)}, u32[]{:S(2)}) %all-to-all-start.1) | async-done | bytes 524320 | tf_op jit(solution)/shard_map/all_to_all | solution.py:176
  31.9 3.4 %all-to-all-start = ((bf16[8,1,64,256]{3,2,1,0:T(8,128)(2,1)}), bf16[8,1,64,256]{3,2,1,0:T(8,128)(2,1)S(1)}, u32[]{:S(2)}, u32[]{:S(2)}) async-start(bf16[8,1,64,256]{3,2,1,0:T(8,128)(2,1)} %shard_map.82), calls=%async_computation | async-start | bytes 524288 | tf_op jit(solution)/shard_map/all_to_all | solution.py:176
  35.3 3.5 %collective-permute-start = (bf16[8,2,64,256]{3,2,1,0:T(8,128)(2,1)S(1)}, bf16[8,2,64,256]{3,2,1,0:T(8,128)(2,1)S(1)}, u32[]{:S(2)}, u32[]{:S(2)}) collective-permute-start(bf16[8,2,64,256]{3,2,1,0:T(8,128)(2,1)S(1)} %all-to-all-done.1.refs_3_), channel_id=1, source_target_pairs={{0,8},{2,10},{4,12},{6,14},{8,16},{10,18},{12,20},{14,22},{16,24},... | collective-permute-start | bytes 1572872 | tf_op jit(solution)/shard_map/ppermute | solution.py:180
  38.9 1.9 %shard_map.85 = bf16[8,1,64,384]{3,2,1,0:T(8,128)(2,1)} custom-call(bf16[64,5120]{1,0:T(8,128)(2,1)} %bitcast.46), custom_call_target="tpu_custom_call" | custom-call | tf_op jit(solution)/shard_map/pallas_call | solution.py:46
  41.2 3.6 %all-to-all-start.3 = ((bf16[8,1,64,384]{3,2,1,0:T(8,128)(2,1)}), bf16[8,1,64,384]{3,2,1,0:T(8,128)(2,1)S(1)}, u32[]{:S(2)}, u32[]{:S(2)}) async-start(bf16[8,1,64,384]{3,2,1,0:T(8,128)(2,1)} %shard_map.85), calls=%async_computation.3 | async-start | bytes 786432 | tf_op jit(solution)/shard_map/all_to_all | solution.py:176
  45.0 0.9 slice.88.refs_6_
  45.9 10.5 %collective-permute-done.refs_4_ = bf16[8,2,64,256]{3,2,1,0:T(8,128)(2,1)S(1)} collective-permute-done((bf16[8,2,64,256]{3,2,1,0:T(8,128)(2,1)S(1)}, bf16[8,2,64,256]{3,2,1,0:T(8,128)(2,1)S(1)}, u32[]{:S(2)}, u32[]{:S(2)}) %collective-permute-start) | collective-permute-done | bytes 524320 | tf_op jit(solution)/shard_map/ppermute | solution.py:180
  56.4 4.4 %collective-permute-start.1 = (bf16[2,2,64,256]{3,2,1,0:T(8,128)(2,1)S(1)}, bf16[2,2,64,256]{3,2,1,0:T(8,128)(2,1)S(1)}, u32[]{:S(2)}, u32[]{:S(2)}) collective-permute-start(bf16[2,2,64,256]{3,2,1,0:T(8,128)(2,1)S(1)} %slice.87), channel_id=1, source_target_pairs={{0,8},{2,10},{4,12},{6,14},{8,16},{10,18},{12,20},{14,22},{16,24},... | collective-permute-start | bytes 393224 | tf_op jit(solution)/shard_map/ppermute | solution.py:180
  60.8 0.7 slice.89
  61.5 3.5 %collective-permute-start.3 = (bf16[2,2,64,384]{3,2,1,0:T(8,128)(2,1)}, bf16[2,2,64,384]{3,2,1,0:T(8,128)(2,1)S(1)}, u32[]{:S(2)}, u32[]{:S(2)}) collective-permute-start(bf16[2,2,64,384]{3,2,1,0:T(8,128)(2,1)} %slice.89), channel_id=1, source_target_pairs={{0,8},{2,10},{4,12},{6,14},{8,16},{10,18},{12,20},{14,22},{16,24},... | collective-permute-start | bytes 589832 | tf_op jit(solution)/shard_map/ppermute | solution.py:180
  65.0 4.6 %shard_map.84 = bf16[8,64,256]{2,1,0:T(8,128)(2,1)} custom-call(f32[4,5]{1,0:T(4,128)S(1)} %fusion.6.refs_0_, f32[4,2]{1,0:T(4,128)S(1)} %bitcast.40, bf16[8,1,64,256]{3,2,1,0:T(8,128)(2,1)S(1)} %all-to-all-done.refs_2_, bf16[8,2,64,256]{3,2,1,0:T(8,128)(2,1)S(1)} %all-to-all-done.1.refs_3_, bf16[8,2,64,256]{3,2,1,0:T(8,128)(2,1)S(1)} %collective-permute-done.refs_4_, ...), custom_call_target="tpu_custom_call" | custom-call | flops 402653184 | bytes 1572864 | tf_op jit(solution)/shard_map/pallas_call | solution.py:131
  69.6 4.0 %all-to-all-start.2 = ((bf16[8,64,256]{2,1,0:T(8,128)(2,1)}), bf16[8,64,256]{2,1,0:T(8,128)(2,1)S(1)}, u32[]{:S(2)}, u32[]{:S(2)}) async-start(bf16[8,64,256]{2,1,0:T(8,128)(2,1)} %shard_map.84), calls=%async_computation.2 | async-start | bytes 524288 | tf_op jit(solution)/shard_map/all_to_all | solution.py:176
  73.7 5.4 %shard_map.87 = bf16[8,64,384]{2,1,0:T(8,128)(2,1)S(1)} custom-call(f32[4,5]{1,0:T(4,128)S(1)} %fusion.6.refs_0_, f32[4,3]{1,0:T(4,128)S(1)} %slice.84.refs_1_, bf16[8,1,64,384]{3,2,1,0:T(8,128)(2,1)S(1)} %all-to-all-done.3.refs_2_, bf16[8,2,64,384]{3,2,1,0:T(8,128)(2,1)S(1)} %all-to-all-done.4.refs_3_, ...), custom_call_target="tpu_custom_call" | custom-call | flops 603979776 | bytes 2359296 | tf_op jit(solution)/shard_map/pallas_call | solution.py:131
  79.6 11.4 %all_to_all.30.refs_1_ = bf16[8,64,384]{2,1,0:T(8,128)(2,1)} all-to-all(bf16[8,64,384]{2,1,0:T(8,128)(2,1)S(1)} %shard_map.87), channel_id=1, replica_groups={{0,1,2,3,4,5,6,7},{8,9,10,11,12,13,14,15},{16,17,18,19,20,21,22,23},{24..., dimensions={0} | all-to-all | bytes 786432 | tf_op jit(solution)/shard_map/all_to_all | solution.py:176
  91.0 2.0 %shard_map.88 = bf16[64,5120]{1,0:T(8,128)(2,1)} custom-call(bf16[8,64,256]{2,1,0:T(8,128)(2,1)} %copy-done.2, bf16[8,64,384]{2,1,0:T(8,128)(2,1)} %all_to_all.30.refs_1_), custom_call_target="tpu_custom_call" | custom-call | tf_op jit(solution)/shard_map/pallas_call | solution.py:64
  (34 shorter events, 2.7 us)
Async XLA Ops:
  0.0 38.8 %copy-start = (f32[4,40]{1,0:T(4,128)S(1)}, f32[4,40]{1,0:T(4,128)}, u32[]{:S(2)}) copy-start(f32[4,40]{1,0:T(4,128)} %param.15) | copy-start | bytes 1924
  2.2 17.3 %all-to-all-start.4 = ((bf16[8,2,64,384]{3,2,1,0:T(8,128)(2,1)}), bf16[8,2,64,384]{3,2,1,0:T(8,128)(2,1)S(1)}, u32[]{:S(2)}, u32[]{:S(2)}) async-start(bf16[8,2,64,384]{3,2,1,0:T(8,128)(2,1)} %shard_map.86), calls=%async_computation.4 | async-start | bytes 1572864 | tf_op jit(solution)/shard_map/all_to_all | solution.py:176
  10.2 0.7 copy-start.5
  12.2 0.7 copy-start.4
  19.6 3.5 %copy-start.3 = (s32[40,9]{0,1:T(8,128)S(1)}, s32[40,9]{0,1:T(8,128)}, u32[]{:S(2)}) copy-start(s32[40,9]{0,1:T(8,128)} %param.13) | copy-start | bytes 4324
  19.6 12.3 %all-to-all-start.1 = ((bf16[8,2,64,256]{3,2,1,0:T(8,128)(2,1)}), bf16[8,2,64,256]{3,2,1,0:T(8,128)(2,1)S(1)}, u32[]{:S(2)}, u32[]{:S(2)}) async-start(bf16[8,2,64,256]{3,2,1,0:T(8,128)(2,1)} %shard_map.83), calls=%async_computation.1 | async-start | bytes 1048576 | tf_op jit(solution)/shard_map/all_to_all | solution.py:176
  24.3 36.5 %collective-permute-start.2 = (bf16[8,2,64,384]{3,2,1,0:T(8,128)(2,1)S(1)}, bf16[8,2,64,384]{3,2,1,0:T(8,128)(2,1)S(1)}, u32[]{:S(2)}, u32[]{:S(2)}) collective-permute-start(bf16[8,2,64,384]{3,2,1,0:T(8,128)(2,1)S(1)} %all-to-all-done.4.refs_3_), channel_id=1, source_target_pairs={{0,8},{2,10},{4,12},{6,14},{8,16},{10,18},{12,20},{14,22},{16,24},... | collective-permute-start | bytes 2359304 | tf_op jit(solution)/shard_map/ppermute | solution.py:180
  31.9 9.4 %all-to-all-start = ((bf16[8,1,64,256]{3,2,1,0:T(8,128)(2,1)}), bf16[8,1,64,256]{3,2,1,0:T(8,128)(2,1)S(1)}, u32[]{:S(2)}, u32[]{:S(2)}) async-start(bf16[8,1,64,256]{3,2,1,0:T(8,128)(2,1)} %shard_map.82), calls=%async_computation | async-start | bytes 524288 | tf_op jit(solution)/shard_map/all_to_all | solution.py:176
  35.3 21.1 %collective-permute-start = (bf16[8,2,64,256]{3,2,1,0:T(8,128)(2,1)S(1)}, bf16[8,2,64,256]{3,2,1,0:T(8,128)(2,1)S(1)}, u32[]{:S(2)}, u32[]{:S(2)}) collective-permute-start(bf16[8,2,64,256]{3,2,1,0:T(8,128)(2,1)S(1)} %all-to-all-done.1.refs_3_), channel_id=1, source_target_pairs={{0,8},{2,10},{4,12},{6,14},{8,16},{10,18},{12,20},{14,22},{16,24},... | collective-permute-start | bytes 1572872 | tf_op jit(solution)/shard_map/ppermute | solution.py:180
  41.2 28.3 %all-to-all-start.3 = ((bf16[8,1,64,384]{3,2,1,0:T(8,128)(2,1)}), bf16[8,1,64,384]{3,2,1,0:T(8,128)(2,1)S(1)}, u32[]{:S(2)}, u32[]{:S(2)}) async-start(bf16[8,1,64,384]{3,2,1,0:T(8,128)(2,1)} %shard_map.85), calls=%async_computation.3 | async-start | bytes 786432 | tf_op jit(solution)/shard_map/all_to_all | solution.py:176
  56.4 8.6 %collective-permute-start.1 = (bf16[2,2,64,256]{3,2,1,0:T(8,128)(2,1)S(1)}, bf16[2,2,64,256]{3,2,1,0:T(8,128)(2,1)S(1)}, u32[]{:S(2)}, u32[]{:S(2)}) collective-permute-start(bf16[2,2,64,256]{3,2,1,0:T(8,128)(2,1)S(1)} %slice.87), channel_id=1, source_target_pairs={{0,8},{2,10},{4,12},{6,14},{8,16},{10,18},{12,20},{14,22},{16,24},... | collective-permute-start | bytes 393224 | tf_op jit(solution)/shard_map/ppermute | solution.py:180
  61.5 12.2 %collective-permute-start.3 = (bf16[2,2,64,384]{3,2,1,0:T(8,128)(2,1)}, bf16[2,2,64,384]{3,2,1,0:T(8,128)(2,1)S(1)}, u32[]{:S(2)}, u32[]{:S(2)}) collective-permute-start(bf16[2,2,64,384]{3,2,1,0:T(8,128)(2,1)} %slice.89), channel_id=1, source_target_pairs={{0,8},{2,10},{4,12},{6,14},{8,16},{10,18},{12,20},{14,22},{16,24},... | collective-permute-start | bytes 589832 | tf_op jit(solution)/shard_map/ppermute | solution.py:180
  69.6 4.1 %copy-start.1 = (f32[5,128,128]{2,1,0:T(8,128)S(1)}, f32[5,128,128]{2,1,0:T(8,128)}, u32[]{:S(2)}) copy-start(f32[5,128,128]{2,1,0:T(8,128)} %or_select_fusion) | copy-start | bytes 983044
  69.6 10.0 %all-to-all-start.2 = ((bf16[8,64,256]{2,1,0:T(8,128)(2,1)}), bf16[8,64,256]{2,1,0:T(8,128)(2,1)S(1)}, u32[]{:S(2)}, u32[]{:S(2)}) async-start(bf16[8,64,256]{2,1,0:T(8,128)(2,1)} %shard_map.84), calls=%async_computation.2 | async-start | bytes 524288 | tf_op jit(solution)/shard_map/all_to_all | solution.py:176
  79.6 11.4 %copy-start.2 = (bf16[8,64,256]{2,1,0:T(8,128)(2,1)}, bf16[8,64,256]{2,1,0:T(8,128)(2,1)S(1)}, u32[]{:S(2)}) copy-start(bf16[8,64,256]{2,1,0:T(8,128)(2,1)S(1)} %all-to-all-done.2.refs_0_) | copy-start | bytes 786436

commit v2 on v1

v2 whole, which is shorter than its diff:
```python
import functools
import math

import jax
import jax.numpy as jnp
from jax import lax
from jax.experimental import pallas as pl
from jax.experimental.pallas import tpu as pltpu
from jax.sharding import PartitionSpec as P

HEADS = 40
HD = 128
TH = 8
TW = 8
BLK = 4
WIN = 5
STEPS = 4

NEG_BIG = -1e30
FACT_ROWS = 8

VMEM = pl.BlockSpec(memory_space=pltpu.VMEM)
SMEM = pl.BlockSpec(memory_space=pltpu.SMEM)


def team_frames(frame_count, tile_count):
    return max(
        g
        for g in range(1, frame_count + 1)
        if frame_count % g == 0 and HEADS % (g * tile_count) == 0
    )


def first_needed(hop, group):
    return max(0, hop * group - WIN)


def partner(member, m, members):
    return member ^ m if members & (members - 1) == 0 else (member + m) % members


def sender(member, m, members):
    return member ^ m if members & (members - 1) == 0 else (member - m) % members


def here(group, tiles):
    return lax.rem(lax.axis_index("frame"), group) * tiles + lax.axis_index("tile")


def pack_kv(own_k, own_v, group, tiles, head_share):
    tokens = own_k.shape[0]
    width = head_share * HD
    members = group * tiles

    def body(k_ref, v_ref, own, *outs):
        for n in range(members):
            lanes = pl.ds(n * width, width)
            own[n, :, :width] = k_ref[:, lanes]
            own[n, :, width:] = v_ref[:, lanes]
        member = here(group, tiles)
        for m, out in enumerate(outs):
            out[...] = own[partner(member, m, members)]

    shape = (tokens, 2 * width)
    return pl.pallas_call(
        body,
        out_shape=[jax.ShapeDtypeStruct((members,) + shape, jnp.bfloat16)]
        + [jax.ShapeDtypeStruct(shape, jnp.bfloat16)] * members,
        in_specs=[VMEM] * 2,
        out_specs=[VMEM] * (1 + members),
    )(own_k, own_v)


def pack_queries(history, frame_index, step_index, own_q, members):
    tokens, channels = own_q.shape
    width = channels // members

    def body(history_ref, index_ref, step_ref, q_ref, out):
        row = lax.broadcasted_iota(jnp.int32, (tokens, HD), 0)
        block = jnp.where(row == WIN, step_ref[0], 0)
        for d in range(1, WIN + 1):
            usable = (
                (history_ref[0, d - 1] == 1)
                & (d <= index_ref[0])
                & (d <= lax.axis_index("frame"))
            )
            block = jnp.where(row == d - 1, usable.astype(jnp.int32), block)
        block = block.astype(jnp.float32).astype(jnp.bfloat16)
        for n in range(members):
            out[n, :, :width] = q_ref[:, n * width : (n + 1) * width]
            out[n, :, width:] = block

    return pl.pallas_call(
        body,
        out_shape=jax.ShapeDtypeStruct((members, tokens, width + HD), jnp.bfloat16),
        in_specs=[SMEM] * 3 + [VMEM],
        out_specs=VMEM,
    )(history, frame_index, step_index, own_q)


def unpack(parts, starts, head_share):
    members, tokens = parts[0].shape[:2]

    def body(*refs):
        out = refs[-1]
        for start, ref in zip(starts, refs[:-1]):
            for n in range(members):
                out[:, pl.ds((n * head_share + start) * HD, ref.shape[-1])] = ref[n]

    return pl.pallas_call(
        body,
        out_shape=jax.ShapeDtypeStruct((tokens, members * head_share * HD), jnp.bfloat16),
        in_specs=[VMEM] * len(parts),
        out_specs=VMEM,
    )(*parts)


FACTOR = math.log2(math.e) / math.sqrt(HD)


def frame_facts(asked_ref, row, frame_tok):
    facts = asked_ref[row, :16, asked_ref.shape[-1] - HD :].astype(jnp.float32)
    past = (facts[:FACT_ROWS] - 1.0) * -NEG_BIG
    past = [past[d : d + 1] for d in range(WIN) for _ in range(frame_tok // HD)]
    return jnp.concatenate(past, axis=1), facts[WIN : WIN + 1]


def head_gain(gain_ref, step, h):
    gain = jnp.zeros((1, HD), jnp.float32)
    for s in range(STEPS):
        gain = jnp.where(step == s, gain_ref[s, h], gain)
    return gain


def rows_of(ref, row, tiles, lane):
    return ref[row : row + tiles, :, lane : lane + HD].reshape(-1, HD)


def scores_of(q, k):
    return FACTOR * lax.dot_general(
        q, k, (((1,), (1,)), ((), ())), preferred_element_type=jnp.float32
    )


def cost(pairs, frame_tok):
    return pl.CostEstimate(
        flops=4 * pairs * frame_tok * frame_tok * HD,
        bytes_accessed=4 * pairs * frame_tok * HD,
        transcendentals=pairs * frame_tok * frame_tok,
    )


def attend_near(asked, team, ahead, bias, gains, group):
    members, tokens = team.shape[:2]
    tiles = members // group
    frame_tok = tiles * tokens
    width = team.shape[-1] // 2
    heads = width // HD
    unfinished = max(0, min(group, WIN - group))

    def body(gain_ref, bias_ref, asked_ref, team_ref, *refs):
        ahead_refs = refs[:members]
        out_ref, sum_ref, top_ref, norm_ref, before_ref = refs[members:]
        member = here(group, tiles)
        for m, ref in enumerate(ahead_refs):
            before_ref[sender(member, m, members)] = ref[...]
        lane_id = lax.broadcasted_iota(jnp.int32, (frame_tok, HD), 1)
        for j in range(group):
            past, step = frame_facts(asked_ref, j * tiles, frame_tok)
            near = min(WIN, j + group)
            frames = [(team_ref, j - d) if d <= j else (before_ref, j - d + group) for d in range(near + 1)]
            tops = norms = jnp.zeros((frame_tok, HD), jnp.float32)
            for h in range(heads):
                lane = h * HD
                q = rows_of(asked_ref, j * tiles, tiles, lane)
                k = jnp.concatenate([rows_of(r, f * tiles, tiles, lane) for r, f in frames])
                v = jnp.concatenate([rows_of(r, f * tiles, tiles, width + lane) for r, f in frames])
                scores = scores_of(q, k)
                scores = jnp.concatenate(
                    [
                        scores[:, :frame_tok] + bias_ref[h],
                        scores[:, frame_tok:] + past[:, : near * frame_tok],
                    ],
                    axis=1,
                )
                top = jnp.max(scores, axis=1, keepdims=True)
                p = jnp.exp2(scores - top)
                norm = jnp.sum(p, axis=1, keepdims=True)
                blended = jnp.dot(p.astype(jnp.bfloat16), v, preferred_element_type=jnp.float32)
                if j < unfinished:
                    sum_ref[j, :, lane : lane + HD] = blended
                    tops = jnp.where(lane_id == h, top, tops)
                    norms = jnp.where(lane_id == h, norm, norms)
                else:
                    result = (blended / norm * head_gain(gain_ref, step, h)).astype(jnp.bfloat16)
                    out_ref[j * tiles : (j + 1) * tiles, :, lane : lane + HD] = result.reshape(
                        tiles, tokens, HD
                    )
            if j < unfinished:
                top_ref[j] = tops
                norm_ref[j] = norms
                out_ref[j * tiles : (j + 1) * tiles] = jnp.zeros((tiles, tokens, width), jnp.bfloat16)

    parts = max(1, unfinished)
    return pl.pallas_call(
        body,
        out_shape=[
            jax.ShapeDtypeStruct((members, tokens, width), jnp.bfloat16),
            jax.ShapeDtypeStruct((parts, frame_tok, width), jnp.float32),
            jax.ShapeDtypeStruct((parts, frame_tok, HD), jnp.float32),
            jax.ShapeDtypeStruct((parts, frame_tok, HD), jnp.float32),
        ],
        in_specs=[SMEM] + [VMEM] * (3 + members),
        out_specs=[VMEM] * 4,
        scratch_shapes=[pltpu.VMEM((members, tokens, 2 * width), jnp.bfloat16)],
        cost_estimate=cost(group * heads * (WIN + 1), frame_tok),
        compiler_params=pltpu.CompilerParams(vmem_limit_bytes=48 * 1024 * 1024),
    )(gains, bias, asked, team, *ahead)


def attend_far(asked, far, state, gains, group):
    out, sums, tops, norms = state
    members, tokens, width = out.shape
    tiles = members // group
    frame_tok = tiles * tokens
    heads = width // HD
    unfinished = min(group, WIN - group)

    def body(gain_ref, asked_ref, sum_ref, top_ref, norm_ref, near_ref, *refs):
        far_refs, out_ref = refs[:-1], refs[-1]
        if unfinished < group:
            out_ref[unfinished * tiles :] = near_ref[unfinished * tiles :]
        for j in range(unfinished):
            past, step = frame_facts(asked_ref, j * tiles, frame_tok)
            frames = []
            for d in range(j + group + 1, WIN + 1):
                hop = -((j - d) // group)
                frames.append((far_refs[hop - 2], j - d + hop * group - first_needed(hop, group)))
            for h in range(heads):
                lane = h * HD
                q = rows_of(asked_ref, j * tiles, tiles, lane)
                k = jnp.concatenate([rows_of(r, f * tiles, tiles, lane) for r, f in frames])
                v = jnp.concatenate([rows_of(r, f * tiles, tiles, width + lane) for r, f in frames])
                scores = scores_of(q, k) + past[:, (j + group) * frame_tok :]
                top = top_ref[j, :, h : h + 1]
                both = jnp.maximum(top, jnp.max(scores, axis=1, keepdims=True))
                p = jnp.exp2(scores - both)
                kept = jnp.exp2(top - both)
                norm = norm_ref[j, :, h : h + 1] * kept + jnp.sum(p, axis=1, keepdims=True)
                blended = sum_ref[j, :, lane : lane + HD] * kept + jnp.dot(
                    p.astype(jnp.bfloat16), v, preferred_element_type=jnp.float32
                )
                result = (blended / norm * head_gain(gain_ref, step, h)).astype(jnp.bfloat16)
                out_ref[j * tiles : (j + 1) * tiles, :, lane : lane + HD] = result.reshape(
                    tiles, tokens, HD
                )

    return pl.pallas_call(
        body,
        out_shape=jax.ShapeDtypeStruct(out.shape, out.dtype),
        in_specs=[SMEM] + [VMEM] * (5 + len(far)),
        out_specs=VMEM,
        cost_estimate=cost(unfinished * heads, frame_tok),
        compiler_params=pltpu.CompilerParams(vmem_limit_bytes=48 * 1024 * 1024),
    )(gains, asked, sums, tops, norms, out, *far)


def window_bias(mask_rows, tile_count):
    tile_cols = min(tile_count, 4)
    pos = jnp.arange(tile_count * TH * TW, dtype=jnp.int32)
    tile, within = pos // (TH * TW), pos % (TH * TW)
    row = (tile // tile_cols * TH + within // TW) // BLK
    col = (tile % tile_cols * TW + within % TW) // BLK
    down = row[None, :] - row[:, None]
    across = col[None, :] - col[:, None]
    near = (jnp.abs(down) <= 1) & (jnp.abs(across) <= 1)
    code = jnp.where(near, (down + 1) * 3 + across + 1, -1)
    allowed = (code == 4)[None]
    for offset in range(9):
        allowed = allowed | (code == offset)[None] & (mask_rows[:, offset] == 1)[:, None, None]
    return jnp.where(allowed, 0.0, NEG_BIG).astype(jnp.float32)


def shards(queries, keys, values, step_index, frame_index, window_mask, history_mask, step_gain):
    tile_count = lax.axis_size("tile")
    frame_count = lax.axis_size("frame")
    group = team_frames(frame_count, tile_count)
    members = group * tile_count
    teams = frame_count // group
    head_share = HEADS // members
    hops = -(-WIN // group)
    both = ("frame", "tile")

    def exchange(block):
        return lax.all_to_all(
            block,
            both,
            0,
            0,
            axis_index_groups=[[t * members + n for n in range(members)] for t in range(teams)],
            tiled=True,
        )

    def team_permute(block, ahead, m):
        route = [
            (t * members + n, (t + ahead) % teams * members + partner(n, m, members))
            for t in range(teams)
            for n in range(members)
        ]
        return lax.ppermute(block, both, route)

    packed_kv, *ahead = pack_kv(keys[0, 0], values[0, 0], group, tile_count, head_share)
    ahead = [team_permute(block, 1, m) for m, block in enumerate(ahead)]
    team = exchange(packed_kv)
    team, ahead[:4] = lax.optimization_barrier((team, ahead[:4]))
    far = [
        team_permute(team[first_needed(hop, group) * tile_count :], hop, 0)
        for hop in range(2, hops + 1)
    ]
    asked = pack_queries(history_mask, frame_index, step_index, queries[0, 0], members)
    asked, ahead[2] = lax.optimization_barrier((asked, ahead[2]))
    asked = exchange(asked)

    share = here(group, tile_count) * head_share
    gains = lax.dynamic_slice(step_gain, (0, share), (STEPS, head_share))
    my_mask = lax.dynamic_slice(window_mask, (share, 0), (head_share, 9))
    bias = window_bias(my_mask, tile_count)
    state = attend_near(asked, team, ahead, bias, gains, group)
    out = attend_far(asked, far, state, gains, group) if far else state[0]
    return unpack([exchange(out)], [0], head_share)[None, None]


def solution(mesh):
    return jax.shard_map(
        shards,
        mesh=mesh,
        in_specs=(
            P("frame", "tile", None, None),
            P("frame", "tile", None, None),
            P("frame", "tile", None, None),
            P("frame"),
            P("frame"),
            P(),
            P("frame", None),
            P(),
        ),
        out_specs=P("frame", "tile", None, None),
        check_vma=False,
    )
```

time: 93.9 us -> 78.4 us (0.83)
  starting transfers between devices: 34.7 us -> 28.7 us
  blocking collectives: 17.6 us -> 13.7 us
  Pallas kernels: 20 us -> 16.9 us
  waiting for transfers between devices: 13.4 us -> 15.9 us
  local copies, waits for them, and re-layouts: 3.19 us -> 0.85 us
  other arithmetic: 1.89 us -> 0.72 us
    all_to_all x5 -> x2, waiting for transfers between devices: 2.93 us -> 12.3 us  [exchange(): lax.all_to_all(block, both, 0, 0, axis_index_groups=[[t * members + n for...]
    all_to_all x5 -> x2, starting transfers between devices: 19.7 us -> 11.3 us  [exchange(): lax.all_to_all(block, both, 0, 0, axis_index_groups=[[t * members + n for...]
    ppermute x4 -> x9, waiting for transfers between devices: 10.5 us -> 3.56 us  [team_permute(): return lax.ppermute(block, both, route)]
    unnamed x1 -> x0, blocking collectives: 6.23 us -> none
    pallas_call x6 -> x4, Pallas kernels: 18 us -> 14.9 us  [the longest x1 7.57 us: attend_near(): pl.pallas_call(body, out_shape=[jax.ShapeDtypeStruct((members, tokens, wi...]
    ppermute x4 -> x9, starting transfers between devices: 14.9 us -> 17.3 us  [team_permute(): return lax.ppermute(block, both, route)]
    all_to_all x1, blocking collectives: 11.4 us -> 13.7 us  [exchange(): lax.all_to_all(block, both, 0, 0, axis_index_groups=[[t * members + n for...]
    unnamed x14 -> x12, local copies, waits for them, and re-layouts: 1.33 us -> 0.02 us
  transfers between devices with their start and end apart: 9 -> 11, of which waited for: 4 -> 5; matrix products, arithmetic and copies ran while one was open for 5% -> 2% of each run, Pallas kernels for 17% -> 12%
where the time goes in v2:
time: 78.4 us; the launch traced here: 78 us
  starting transfers between devices  28.7 us (37%)
  Pallas kernels  16.9 us (22%)
  waiting for transfers between devices  15.9 us (20%)
  blocking collectives  13.7 us (17%)
  between operations  1.4 us (2%)
  local copies, waits for them, and re-layouts  0.85 us (1%)
    ppermute x9, starting transfers between devices, team_permute(): return lax.ppermute(block, both, route)  17.3 us
    all_to_all x1, blocking collectives, exchange(): lax.all_to_all(block, both, 0, 0, axis_index_groups=[[t * members + n for...  13.7 us
    all_to_all x2, waiting for transfers between devices, exchange(): lax.all_to_all(block, both, 0, 0, axis_index_groups=[[t * members + n for...  12.3 us
    all_to_all x2, starting transfers between devices, exchange(): lax.all_to_all(block, both, 0, 0, axis_index_groups=[[t * members + n for...  11.3 us
    pallas_call x1, Pallas kernels, attend_near(): pl.pallas_call(body, out_shape=[jax.ShapeDtypeStruct((members, tokens, wi...  7.57 us
    ppermute x9, waiting for transfers between devices, team_permute(): return lax.ppermute(block, both, route)  3.56 us
    pallas_call x1, Pallas kernels, pack_kv(): pl.pallas_call(body, out_shape=[jax.ShapeDtypeStruct((members,) + shape,...  2.88 us
    pallas_call x1, Pallas kernels, attend_far(): pl.pallas_call(body, out_shape=jax.ShapeDtypeStruct(out.shape, out.dtype)...  2.4 us
  transfers between devices with their start and end apart: 11, of which 5 were waited for; matrix products, arithmetic and copies ran while one was open for 2% of the time, Pallas kernels for 12%

profile of v2, /device:TPU:0, one launch (start us, length us, event | category | flops | bytes accessed | tf_op | source)
XLA Modules:
  0.0 78.0 jit_solution(3668350691703421478)
XLA Ops:
  0.0 2.9 %shard_map.83 = (bf16[8,64,1280]{2,1,0:T(8,128)(2,1)}, bf16[64,1280]{1,0:T(8,128)(2,1)}, bf16[64,1280]{1,0:T(8,128)(2,1)}, bf16[64,1280]{1,0:T(8,128)(2,1)}, bf1...) custom-call(bf16[64,5120]{1,0:T(8,128)(2,1)} %bitcast.22, ...), custom_call_target="tpu_custom_call" | custom-call | tf_op jit(solution)/shard_map/pallas_call | solution.py:65
  2.9 5.3 %all-to-all-start = ((bf16[8,64,1280]{2,1,0:T(8,128)(2,1)}), bf16[8,64,1280]{2,1,0:T(8,128)(2,1)S(1)}, u32[]{:S(2)}, u32[]{:S(2)}) async-start(bf16[8,64,1280]{2,1,0:T(8,128)(2,1)} %get-tuple-element.25), calls=%async_computation | async-start | bytes 2621440 | tf_op jit(solution)/shard_map/all_to_all | solution.py:295
  8.2 1.6 %collective-permute-start = (bf16[64,1280]{1,0:T(8,128)(2,1)S(1)}, bf16[64,1280]{1,0:T(8,128)(2,1)S(1)}, u32[]{:S(2)}, u32[]{:S(2)}) collective-permute-start(bf16[64,1280]{1,0:T(8,128)(2,1)S(1)} %copy-done.5), channel_id=1, source_target_pairs={{0,8},{1,9},{2,10},{3,11},{4,12},{5,13},{6,14},{7,15},{8,16},{9,17... | collective-permute-start | bytes 491528 | tf_op jit(solution)/shard_map/ppermute | solution.py:310
  9.9 3.0 %collective-permute-start.1 = (bf16[64,1280]{1,0:T(8,128)(2,1)S(1)}, bf16[64,1280]{1,0:T(8,128)(2,1)S(1)}, u32[]{:S(2)}, u32[]{:S(2)}) collective-permute-start(bf16[64,1280]{1,0:T(8,128)(2,1)S(1)} %copy-done.4), channel_id=1, source_target_pairs={{0,9},{1,8},{2,11},{3,10},{4,13},{5,12},{6,15},{7,14},{8,17},{9,16... | collective-permute-start | bytes 491528 | tf_op jit(solution)/shard_map/ppermute | solution.py:310
  12.9 0.8 collective-permute-start.2
  13.7 0.6 collective-permute-start.3
  14.2 2.6 %collective-permute-start.4 = (bf16[64,1280]{1,0:T(8,128)(2,1)}, bf16[64,1280]{1,0:T(8,128)(2,1)}, u32[]{:S(2)}, u32[]{:S(2)}) collective-permute-start(bf16[64,1280]{1,0:T(8,128)(2,1)} %get-tuple-element.37), channel_id=1, source_target_pairs={{0,12},{1,13},{2,14},{3,15},{4,8},{5,9},{6,10},{7,11},{8,20},{9,21... | collective-permute-start | bytes 491528 | tf_op jit(solution)/shard_map/ppermute | solution.py:310
  18.2 2.1 %shard_map.82 = bf16[8,64,768]{2,1,0:T(8,128)(2,1)} custom-call(s32[1,5]{1,0:T(1,128)} %history_ref.1, s32[1]{0:T(128)S(6)} %copy.10.index_ref, s32[1]{0:T(128)S(6)} %copy.9.step_ref, bf16[64,5120]{1,0:T(8,128)(2,1)} %bitcast.24), custom_call_target="tpu_custom_call" | custom-call | tf_op jit(solution)/shard_map/pallas_call | solution.py:93
  20.4 2.5 %collective-permute-start.5 = (bf16[64,1280]{1,0:T(8,128)(2,1)}, bf16[64,1280]{1,0:T(8,128)(2,1)}, u32[]{:S(2)}, u32[]{:S(2)}) collective-permute-start(bf16[64,1280]{1,0:T(8,128)(2,1)} %get-tuple-element.38), channel_id=1, source_target_pairs={{0,13},{1,12},{2,15},{3,14},{4,9},{5,8},{6,11},{7,10},{8,21},{9,20... | collective-permute-start | bytes 491528 | tf_op jit(solution)/shard_map/ppermute | solution.py:310
  22.9 0.5 collective-permute-done.1.refs_1_
  23.4 0.6 collective-permute-start.6
  24.0 2.0 %collective-permute-start.7 = (bf16[64,1280]{1,0:T(8,128)(2,1)}, bf16[64,1280]{1,0:T(8,128)(2,1)}, u32[]{:S(2)}, u32[]{:S(2)}) collective-permute-start(bf16[64,1280]{1,0:T(8,128)(2,1)} %get-tuple-element.40), channel_id=1, source_target_pairs={{0,15},{1,14},{2,13},{3,12},{4,11},{5,10},{6,9},{7,8},{8,23},{9,22... | collective-permute-start | bytes 491528 | tf_op jit(solution)/shard_map/ppermute | solution.py:310
  26.0 2.2 %collective-permute-done.3.refs_3_ = bf16[64,1280]{1,0:T(8,128)(2,1)S(1)} collective-permute-done((bf16[64,1280]{1,0:T(8,128)(2,1)S(1)}, bf16[64,1280]{1,0:T(8,128)(2,1)S(1)}, u32[]{:S(2)}, u32[]{:S(2)}) %collective-permute-start.3) | collective-permute-done | bytes 163872 | tf_op jit(solution)/shard_map/ppermute | solution.py:310
  28.2 3.9 %all-to-all-done.team_ref = bf16[8,64,1280]{2,1,0:T(8,128)(2,1)S(1)} async-done(((bf16[8,64,1280]{2,1,0:T(8,128)(2,1)}), bf16[8,64,1280]{2,1,0:T(8,128)(2,1)S(1)}, u32[]{:S(2)}, u32[]{:S(2)}) %all-to-all-start) | async-done | bytes 1310752 | tf_op jit(solution)/shard_map/all_to_all | solution.py:295
  32.0 6.0 %all-to-all-start.1 = ((bf16[8,64,768]{2,1,0:T(8,128)(2,1)}), bf16[8,64,768]{2,1,0:T(8,128)(2,1)S(1)}, u32[]{:S(2)}, u32[]{:S(2)}) async-start(bf16[8,64,768]{2,1,0:T(8,128)(2,1)} %shard_map.82), calls=%async_computation.1 | async-start | bytes 1572864 | tf_op jit(solution)/shard_map/all_to_all | solution.py:295
  38.3 0.7 slice.39
  39.0 3.6 %collective-permute-start.8 = (bf16[2,64,1280]{2,1,0:T(8,128)(2,1)}, bf16[2,64,1280]{2,1,0:T(8,128)(2,1)S(1)}, u32[]{:S(2)}, u32[]{:S(2)}) collective-permute-start(bf16[2,64,1280]{2,1,0:T(8,128)(2,1)} %slice.39), channel_id=1, source_target_pairs={{0,16},{1,17},{2,18},{3,19},{4,20},{5,21},{6,22},{7,23},{8,24},{9,... | collective-permute-start | bytes 983048 | tf_op jit(solution)/shard_map/ppermute | solution.py:310
  42.7 0.4 or_select_fusion.bias_ref
  43.2 0.8 %collective-permute-done.7.refs_7_ = bf16[64,1280]{1,0:T(8,128)(2,1)} collective-permute-done((bf16[64,1280]{1,0:T(8,128)(2,1)}, bf16[64,1280]{1,0:T(8,128)(2,1)}, u32[]{:S(2)}, u32[]{:S(2)}) %collective-permute-start.7) | collective-permute-done | bytes 163872 | tf_op jit(solution)/shard_map/ppermute | solution.py:310
  44.0 8.4 %all-to-all-done.1.asked_ref = bf16[8,64,768]{2,1,0:T(8,128)(2,1)S(1)} async-done(((bf16[8,64,768]{2,1,0:T(8,128)(2,1)}), bf16[8,64,768]{2,1,0:T(8,128)(2,1)S(1)}, u32[]{:S(2)}, u32[]{:S(2)}) %all-to-all-start.1) | async-done | bytes 786464 | tf_op jit(solution)/shard_map/all_to_all | solution.py:295
  52.4 7.6 %shard_map.84 = (bf16[8,64,640]{2,1,0:T(8,128)(2,1)S(1)}, f32[1,128,640]{2,1,0:T(8,128)S(1)}, f32[1,128,128]{2,1,0:T(8,128)S(1)}, f32[1,128,128]{2,1,0:T(8,128)S(1)}) custom-call(f32[4,5]{1,0:T(4,128)S(1)} %constant_dynamic-slice_fusion.gain_ref, f32[5,128,128]{2,1,0:T(8,128)S(1)} %or_select_fusion.bias_ref, ...), custom_call_target="tpu_custom_call" | custom-call | flops 1006632960 | bytes 7864320 | tf_op jit(solution)/shard_map/pallas_call | solution.py:205
  60.0 2.4 %shard_map.85 = bf16[8,64,640]{2,1,0:T(8,128)(2,1)S(1)} custom-call(f32[4,5]{1,0:T(4,128)S(1)} %constant_dynamic-slice_fusion.gain_ref, bf16[8,64,768]{2,1,0:T(8,128)(2,1)S(1)} %all-to-all-done.1.asked_ref, f32[1,128,640]{2,1,0:T(8,128)S(1)} %get-tuple-element.41.sum_ref, f32[1,128,128]{2,1,0:T(8,128)S(1)} %get-tuple-element.42.top_ref, ...), custom_call_target="tpu_custom_call" | custom-call | flops 41943040 | bytes 327680 | tf_op jit(solution)/shard_map/pallas_call | solution.py:258
  62.4 13.7 %all_to_all.15.refs_0_ = bf16[8,64,640]{2,1,0:T(8,128)(2,1)} all-to-all(bf16[8,64,640]{2,1,0:T(8,128)(2,1)S(1)} %shard_map.85), channel_id=1, replica_groups={{0,1,2,3,4,5,6,7},{8,9,10,11,12,13,14,15},{16,17,18,19,20,21,22,23},{24..., dimensions={0} | all-to-all | bytes 1310720 | tf_op jit(solution)/shard_map/all_to_all | solution.py:295
  76.1 2.0 %shard_map.86 = bf16[64,5120]{1,0:T(8,128)(2,1)} custom-call(bf16[8,64,640]{2,1,0:T(8,128)(2,1)} %all_to_all.15.refs_0_), custom_call_target="tpu_custom_call" | custom-call | tf_op jit(solution)/shard_map/pallas_call | solution.py:110
  (22 shorter events, 0.5 us)
Async XLA Ops:
  0.0 43.1 %copy-start = (f32[4,40]{1,0:T(4,128)S(1)}, f32[4,40]{1,0:T(4,128)}, u32[]{:S(2)}) copy-start(f32[4,40]{1,0:T(4,128)} %param.15) | copy-start | bytes 1924
  2.9 5.3 %copy-start.5 = (bf16[64,1280]{1,0:T(8,128)(2,1)S(1)}, bf16[64,1280]{1,0:T(8,128)(2,1)}, u32[]{:S(2)}) copy-start(bf16[64,1280]{1,0:T(8,128)(2,1)} %get-tuple-element.26) | copy-start | bytes 491524
  2.9 7.0 %copy-start.4 = (bf16[64,1280]{1,0:T(8,128)(2,1)S(1)}, bf16[64,1280]{1,0:T(8,128)(2,1)}, u32[]{:S(2)}) copy-start(bf16[64,1280]{1,0:T(8,128)(2,1)} %get-tuple-element.27) | copy-start | bytes 491524
  2.9 10.0 %copy-start.3 = (bf16[64,1280]{1,0:T(8,128)(2,1)S(1)}, bf16[64,1280]{1,0:T(8,128)(2,1)}, u32[]{:S(2)}) copy-start(bf16[64,1280]{1,0:T(8,128)(2,1)} %get-tuple-element.28) | copy-start | bytes 491524
  2.9 10.8 %copy-start.2 = (bf16[64,1280]{1,0:T(8,128)(2,1)S(1)}, bf16[64,1280]{1,0:T(8,128)(2,1)}, u32[]{:S(2)}) copy-start(bf16[64,1280]{1,0:T(8,128)(2,1)} %get-tuple-element.29) | copy-start | bytes 491524
  2.9 29.1 %all-to-all-start = ((bf16[8,64,1280]{2,1,0:T(8,128)(2,1)}), bf16[8,64,1280]{2,1,0:T(8,128)(2,1)S(1)}, u32[]{:S(2)}, u32[]{:S(2)}) async-start(bf16[8,64,1280]{2,1,0:T(8,128)(2,1)} %get-tuple-element.25), calls=%async_computation | async-start | bytes 2621440 | tf_op jit(solution)/shard_map/all_to_all | solution.py:295
  8.2 12.0 %copy-start.1 = (s32[40,9]{0,1:T(8,128)S(1)}, s32[40,9]{0,1:T(8,128)}, u32[]{:S(2)}) copy-start(s32[40,9]{0,1:T(8,128)} %param.13) | copy-start | bytes 4324
  8.2 12.1 %collective-permute-start = (bf16[64,1280]{1,0:T(8,128)(2,1)S(1)}, bf16[64,1280]{1,0:T(8,128)(2,1)S(1)}, u32[]{:S(2)}, u32[]{:S(2)}) collective-permute-start(bf16[64,1280]{1,0:T(8,128)(2,1)S(1)} %copy-done.5), channel_id=1, source_target_pairs={{0,8},{1,9},{2,10},{3,11},{4,12},{5,13},{6,14},{7,15},{8,16},{9,17... | collective-permute-start | bytes 491528 | tf_op jit(solution)/shard_map/ppermute | solution.py:310
  9.9 13.6 %collective-permute-start.1 = (bf16[64,1280]{1,0:T(8,128)(2,1)S(1)}, bf16[64,1280]{1,0:T(8,128)(2,1)S(1)}, u32[]{:S(2)}, u32[]{:S(2)}) collective-permute-start(bf16[64,1280]{1,0:T(8,128)(2,1)S(1)} %copy-done.4), channel_id=1, source_target_pairs={{0,9},{1,8},{2,11},{3,10},{4,13},{5,12},{6,15},{7,14},{8,17},{9,16... | collective-permute-start | bytes 491528 | tf_op jit(solution)/shard_map/ppermute | solution.py:310
  12.9 11.1 %collective-permute-start.2 = (bf16[64,1280]{1,0:T(8,128)(2,1)S(1)}, bf16[64,1280]{1,0:T(8,128)(2,1)S(1)}, u32[]{:S(2)}, u32[]{:S(2)}) collective-permute-start(bf16[64,1280]{1,0:T(8,128)(2,1)S(1)} %copy-done.3), channel_id=1, source_target_pairs={{0,10},{1,11},{2,8},{3,9},{4,14},{5,15},{6,12},{7,13},{8,18},{9,19... | collective-permute-start | bytes 491528 | tf_op jit(solution)/shard_map/ppermute | solution.py:310
  13.7 14.5 %collective-permute-start.3 = (bf16[64,1280]{1,0:T(8,128)(2,1)S(1)}, bf16[64,1280]{1,0:T(8,128)(2,1)S(1)}, u32[]{:S(2)}, u32[]{:S(2)}) collective-permute-start(bf16[64,1280]{1,0:T(8,128)(2,1)S(1)} %copy-done.2), channel_id=1, source_target_pairs={{0,11},{1,10},{2,9},{3,8},{4,15},{5,14},{6,13},{7,12},{8,19},{9,18... | collective-permute-start | bytes 491528 | tf_op jit(solution)/shard_map/ppermute | solution.py:310
  14.2 28.9 %collective-permute-start.4 = (bf16[64,1280]{1,0:T(8,128)(2,1)}, bf16[64,1280]{1,0:T(8,128)(2,1)}, u32[]{:S(2)}, u32[]{:S(2)}) collective-permute-start(bf16[64,1280]{1,0:T(8,128)(2,1)} %get-tuple-element.37), channel_id=1, source_target_pairs={{0,12},{1,13},{2,14},{3,15},{4,8},{5,9},{6,10},{7,11},{8,20},{9,21... | collective-permute-start | bytes 491528 | tf_op jit(solution)/shard_map/ppermute | solution.py:310
  20.4 22.8 %collective-permute-start.5 = (bf16[64,1280]{1,0:T(8,128)(2,1)}, bf16[64,1280]{1,0:T(8,128)(2,1)}, u32[]{:S(2)}, u32[]{:S(2)}) collective-permute-start(bf16[64,1280]{1,0:T(8,128)(2,1)} %get-tuple-element.38), channel_id=1, source_target_pairs={{0,13},{1,12},{2,15},{3,14},{4,9},{5,8},{6,11},{7,10},{8,21},{9,20... | collective-permute-start | bytes 491528 | tf_op jit(solution)/shard_map/ppermute | solution.py:310
  23.4 19.7 %collective-permute-start.6 = (bf16[64,1280]{1,0:T(8,128)(2,1)}, bf16[64,1280]{1,0:T(8,128)(2,1)}, u32[]{:S(2)}, u32[]{:S(2)}) collective-permute-start(bf16[64,1280]{1,0:T(8,128)(2,1)} %get-tuple-element.39), channel_id=1, source_target_pairs={{0,14},{1,15},{2,12},{3,13},{4,10},{5,11},{6,8},{7,9},{8,22},{9,23... | collective-permute-start | bytes 491528 | tf_op jit(solution)/shard_map/ppermute | solution.py:310
  24.0 19.9 %collective-permute-start.7 = (bf16[64,1280]{1,0:T(8,128)(2,1)}, bf16[64,1280]{1,0:T(8,128)(2,1)}, u32[]{:S(2)}, u32[]{:S(2)}) collective-permute-start(bf16[64,1280]{1,0:T(8,128)(2,1)} %get-tuple-element.40), channel_id=1, source_target_pairs={{0,15},{1,14},{2,13},{3,12},{4,11},{5,10},{6,9},{7,8},{8,23},{9,22... | collective-permute-start | bytes 491528 | tf_op jit(solution)/shard_map/ppermute | solution.py:310
  32.0 20.4 %all-to-all-start.1 = ((bf16[8,64,768]{2,1,0:T(8,128)(2,1)}), bf16[8,64,768]{2,1,0:T(8,128)(2,1)S(1)}, u32[]{:S(2)}, u32[]{:S(2)}) async-start(bf16[8,64,768]{2,1,0:T(8,128)(2,1)} %shard_map.82), calls=%async_computation.1 | async-start | bytes 1572864 | tf_op jit(solution)/shard_map/all_to_all | solution.py:295
  39.0 20.9 %collective-permute-start.8 = (bf16[2,64,1280]{2,1,0:T(8,128)(2,1)}, bf16[2,64,1280]{2,1,0:T(8,128)(2,1)S(1)}, u32[]{:S(2)}, u32[]{:S(2)}) collective-permute-start(bf16[2,64,1280]{2,1,0:T(8,128)(2,1)} %slice.39), channel_id=1, source_target_pairs={{0,16},{1,17},{2,18},{3,19},{4,20},{5,21},{6,22},{7,23},{8,24},{9,... | collective-permute-start | bytes 983048 | tf_op jit(solution)/shard_map/ppermute | solution.py:310

commit v3 on v2

--- a/solution.py
+++ b/solution.py
@@ -140,6 +140,12 @@
     return FACTOR * lax.dot_general(
         q, k, (((1,), (1,)), ((), ())), preferred_element_type=jnp.float32
     )
+
+
+def weigh(weights, v):
+    v = jnp.concatenate([v, jnp.ones(v.shape, v.dtype)], axis=1)
+    both = jnp.dot(weights.astype(jnp.bfloat16), v, preferred_element_type=jnp.float32)
+    return both[:, :HD], both[:, HD:]
 
 
 def cost(pairs, frame_tok):
@@ -185,8 +191,7 @@
                 )
                 top = jnp.max(scores, axis=1, keepdims=True)
                 p = jnp.exp2(scores - top)
-                norm = jnp.sum(p, axis=1, keepdims=True)
-                blended = jnp.dot(p.astype(jnp.bfloat16), v, preferred_element_type=jnp.float32)
+                blended, norm = weigh(p, v)
                 if j < unfinished:
                     sum_ref[j, :, lane : lane + HD] = blended
                     tops = jnp.where(lane_id == h, top, tops)
@@ -199,7 +204,6 @@
             if j < unfinished:
                 top_ref[j] = tops
                 norm_ref[j] = norms
-                out_ref[j * tiles : (j + 1) * tiles] = jnp.zeros((tiles, tokens, width), jnp.bfloat16)
 
     parts = max(1, unfinished)
     return pl.pallas_call(
@@ -228,8 +232,6 @@
 
     def body(gain_ref, asked_ref, sum_ref, top_ref, norm_ref, near_ref, *refs):
         far_refs, out_ref = refs[:-1], refs[-1]
-        if unfinished < group:
-            out_ref[unfinished * tiles :] = near_ref[unfinished * tiles :]
         for j in range(unfinished):
             past, step = frame_facts(asked_ref, j * tiles, frame_tok)
             frames = []
@@ -244,22 +246,28 @@
                 scores = scores_of(q, k) + past[:, (j + group) * frame_tok :]
                 top = top_ref[j, :, h : h + 1]
                 both = jnp.maximum(top, jnp.max(scores, axis=1, keepdims=True))
-                p = jnp.exp2(scores - both)
+                blended, norm = weigh(jnp.exp2(scores - both), v)
                 kept = jnp.exp2(top - both)
-                norm = norm_ref[j, :, h : h + 1] * kept + jnp.sum(p, axis=1, keepdims=True)
-                blended = sum_ref[j, :, lane : lane + HD] * kept + jnp.dot(
-                    p.astype(jnp.bfloat16), v, preferred_element_type=jnp.float32
-                )
+                blended += sum_ref[j, :, lane : lane + HD] * kept
+                norm += norm_ref[j, :, h : h + 1] * kept
                 result = (blended / norm * head_gain(gain_ref, step, h)).astype(jnp.bfloat16)
                 out_ref[j * tiles : (j + 1) * tiles, :, lane : lane + HD] = result.reshape(
                     tiles, tokens, HD
                 )
 
-    return pl.pallas_call(
-        body,
+    def leading(array):
+        return pl.BlockSpec((unfinished * tiles,) + array.shape[1:], lambda i: (0, 0, 0))
+
+    return pl.pallas_call(
+        body,
+        grid=(1,),
         out_shape=jax.ShapeDtypeStruct(out.shape, out.dtype),
-        in_specs=[SMEM] + [VMEM] * (5 + len(far)),
-        out_specs=VMEM,
+        in_specs=[SMEM, leading(asked)]
+        + [VMEM] * 3
+        + [pl.BlockSpec(memory_space=pl.ANY)]
+        + [VMEM] * len(far),
+        out_specs=leading(out),
+        input_output_aliases={5: 0},
         cost_estimate=cost(unfinished * heads, frame_tok),
         compiler_params=pltpu.CompilerParams(vmem_limit_bytes=48 * 1024 * 1024),
     )(gains, asked, sums, tops, norms, out, *far)
@@ -310,15 +318,23 @@
         return lax.ppermute(block, both, route)
 
     packed_kv, *ahead = pack_kv(keys[0, 0], values[0, 0], group, tile_count, head_share)
-    ahead = [team_permute(block, 1, m) for m, block in enumerate(ahead)]
+    sent = {}
+    for m in [0, 2, 1, 3, 4, 6, 5, 7]:
+        block = ahead[m]
+        sent[m] = team_permute(block, 1, m)
+    ahead = [sent[m] for m in range(members)]
     team = exchange(packed_kv)
-    team, ahead[:4] = lax.optimization_barrier((team, ahead[:4]))
+    team, *some = lax.optimization_barrier((team, *[ahead[m] for m in [0, 2, 1, 3]]))
+    for m, block in zip([0, 2, 1, 3], some):
+        ahead[m] = block
     far = [
         team_permute(team[first_needed(hop, group) * tile_count :], hop, 0)
         for hop in range(2, hops + 1)
     ]
     asked = pack_queries(history_mask, frame_index, step_index, queries[0, 0], members)
-    asked, ahead[2] = lax.optimization_barrier((asked, ahead[2]))
+    asked, *some = lax.optimization_barrier((asked, *[ahead[m] for m in [1]]))
+    for m, block in zip([1], some):
+        ahead[m] = block
     asked = exchange(asked)
 
     share = here(group, tile_count) * head_share

time: 78.4 us -> 75.5 us (0.963)
  waiting for transfers between devices: 15.9 us -> 21 us
  starting transfers between devices: 28.7 us -> 24 us
  Pallas kernels: 16.9 us -> 13.5 us
    ppermute x9, waiting for transfers between devices: 3.56 us -> 10.5 us  [team_permute(): return lax.ppermute(block, both, route)]
    pallas_call x1, Pallas kernels: 7.57 us -> 4.22 us  [attend_near(): pl.pallas_call(body, out_shape=[jax.ShapeDtypeStruct((members, tokens, wi...]
    all_to_all x2, starting transfers between devices: 11.3 us -> 8.86 us  [exchange(): lax.all_to_all(block, both, 0, 0, axis_index_groups=[[t * members + n for...]
    ppermute x9, starting transfers between devices: 17.3 us -> 15.2 us  [team_permute(): return lax.ppermute(block, both, route)]
    all_to_all x2, waiting for transfers between devices: 12.3 us -> 10.5 us  [exchange(): lax.all_to_all(block, both, 0, 0, axis_index_groups=[[t * members + n for...]
  transfers between devices with their start and end apart: 11 -> 11, of which waited for: 5 -> 6; matrix products, arithmetic and copies ran while one was open for 2% -> 2% of each run, Pallas kernels for 12% -> 8%
where the time goes in v3:
time: 75.5 us; the launch traced here: 75.1 us
  starting transfers between devices  24 us (32%)
  waiting for transfers between devices  21 us (28%)
  blocking collectives  13.7 us (18%)
  Pallas kernels  13.5 us (18%)
  between operations  1.4 us (2%)
  local copies, waits for them, and re-layouts  0.85 us (1%)
    ppermute x9, starting transfers between devices, team_permute(): return lax.ppermute(block, both, route)  15.2 us
    all_to_all x1, blocking collectives, exchange(): lax.all_to_all(block, both, 0, 0, axis_index_groups=[[t * members + n for...  13.7 us
    all_to_all x2, waiting for transfers between devices, exchange(): lax.all_to_all(block, both, 0, 0, axis_index_groups=[[t * members + n for...  10.5 us
    ppermute x9, waiting for transfers between devices, team_permute(): return lax.ppermute(block, both, route)  10.5 us
    all_to_all x2, starting transfers between devices, exchange(): lax.all_to_all(block, both, 0, 0, axis_index_groups=[[t * members + n for...  8.86 us
    pallas_call x1, Pallas kernels, attend_near(): pl.pallas_call(body, out_shape=[jax.ShapeDtypeStruct((members, tokens, wi...  4.22 us
    pallas_call x1, Pallas kernels, pack_kv(): pl.pallas_call(body, out_shape=[jax.ShapeDtypeStruct((members,) + shape,...  2.88 us
    pallas_call x1, Pallas kernels, attend_far(): pl.pallas_call(body, grid=(1,), out_shape=jax.ShapeDtypeStruct(out.shape,...  2.33 us
  transfers between devices with their start and end apart: 11, of which 6 were waited for; matrix products, arithmetic and copies ran while one was open for 2% of the time, Pallas kernels for 8%

profile of v3, /device:TPU:0, one launch (start us, length us, event | category | flops | bytes accessed | tf_op | source)
XLA Modules:
  0.0 75.1 jit_solution(16413235604507927947)
XLA Ops:
  0.0 2.9 %shard_map.83 = (bf16[8,64,1280]{2,1,0:T(8,128)(2,1)}, bf16[64,1280]{1,0:T(8,128)(2,1)}, bf16[64,1280]{1,0:T(8,128)(2,1)}, bf16[64,1280]{1,0:T(8,128)(2,1)}, bf1...) custom-call(bf16[64,5120]{1,0:T(8,128)(2,1)} %bitcast.22, ...), custom_call_target="tpu_custom_call" | custom-call | tf_op jit(solution)/shard_map/pallas_call | solution.py:65
  2.9 5.3 %all-to-all-start = ((bf16[8,64,1280]{2,1,0:T(8,128)(2,1)}), bf16[8,64,1280]{2,1,0:T(8,128)(2,1)S(1)}, u32[]{:S(2)}, u32[]{:S(2)}) async-start(bf16[8,64,1280]{2,1,0:T(8,128)(2,1)} %get-tuple-element.25), calls=%async_computation | async-start | bytes 2621440 | tf_op jit(solution)/shard_map/all_to_all | solution.py:303
  8.2 1.6 %collective-permute-start = (bf16[64,1280]{1,0:T(8,128)(2,1)S(1)}, bf16[64,1280]{1,0:T(8,128)(2,1)S(1)}, u32[]{:S(2)}, u32[]{:S(2)}) collective-permute-start(bf16[64,1280]{1,0:T(8,128)(2,1)S(1)} %copy-done.5), channel_id=1, source_target_pairs={{0,8},{1,9},{2,10},{3,11},{4,12},{5,13},{6,14},{7,15},{8,16},{9,17... | collective-permute-start | bytes 491528 | tf_op jit(solution)/shard_map/ppermute | solution.py:318
  9.9 1.4 %collective-permute-start.1 = (bf16[64,1280]{1,0:T(8,128)(2,1)S(1)}, bf16[64,1280]{1,0:T(8,128)(2,1)S(1)}, u32[]{:S(2)}, u32[]{:S(2)}) collective-permute-start(bf16[64,1280]{1,0:T(8,128)(2,1)S(1)} %copy-done.4), channel_id=1, source_target_pairs={{0,10},{1,11},{2,8},{3,9},{4,14},{5,15},{6,12},{7,13},{8,18},{9,19... | collective-permute-start | bytes 491528 | tf_op jit(solution)/shard_map/ppermute | solution.py:318
  11.3 2.7 %collective-permute-start.2 = (bf16[64,1280]{1,0:T(8,128)(2,1)S(1)}, bf16[64,1280]{1,0:T(8,128)(2,1)S(1)}, u32[]{:S(2)}, u32[]{:S(2)}) collective-permute-start(bf16[64,1280]{1,0:T(8,128)(2,1)S(1)} %copy-done.3), channel_id=1, source_target_pairs={{0,9},{1,8},{2,11},{3,10},{4,13},{5,12},{6,15},{7,14},{8,17},{9,16... | collective-permute-start | bytes 491528 | tf_op jit(solution)/shard_map/ppermute | solution.py:318
  13.9 0.3 collective-permute-start.3
  14.2 2.4 %collective-permute-start.4 = (bf16[64,1280]{1,0:T(8,128)(2,1)}, bf16[64,1280]{1,0:T(8,128)(2,1)}, u32[]{:S(2)}, u32[]{:S(2)}) collective-permute-start(bf16[64,1280]{1,0:T(8,128)(2,1)} %get-tuple-element.37), channel_id=1, source_target_pairs={{0,12},{1,13},{2,14},{3,15},{4,8},{5,9},{6,10},{7,11},{8,20},{9,21... | collective-permute-start | bytes 491528 | tf_op jit(solution)/shard_map/ppermute | solution.py:318
  17.9 2.1 %shard_map.82 = bf16[8,64,768]{2,1,0:T(8,128)(2,1)} custom-call(s32[1,5]{1,0:T(1,128)} %history_ref.1, s32[1]{0:T(128)S(6)} %copy.12.index_ref, s32[1]{0:T(128)S(6)} %copy.11.step_ref, bf16[64,5120]{1,0:T(8,128)(2,1)} %bitcast.24), custom_call_target="tpu_custom_call" | custom-call | tf_op jit(solution)/shard_map/pallas_call | solution.py:93
  20.1 2.5 %collective-permute-start.5 = (bf16[64,1280]{1,0:T(8,128)(2,1)}, bf16[64,1280]{1,0:T(8,128)(2,1)}, u32[]{:S(2)}, u32[]{:S(2)}) collective-permute-start(bf16[64,1280]{1,0:T(8,128)(2,1)} %get-tuple-element.38), channel_id=1, source_target_pairs={{0,13},{1,12},{2,15},{3,14},{4,9},{5,8},{6,11},{7,10},{8,21},{9,20... | collective-permute-start | bytes 491528 | tf_op jit(solution)/shard_map/ppermute | solution.py:318
  22.6 1.7 %collective-permute-start.6 = (bf16[64,1280]{1,0:T(8,128)(2,1)}, bf16[64,1280]{1,0:T(8,128)(2,1)}, u32[]{:S(2)}, u32[]{:S(2)}) collective-permute-start(bf16[64,1280]{1,0:T(8,128)(2,1)} %get-tuple-element.39), channel_id=1, source_target_pairs={{0,14},{1,15},{2,12},{3,13},{4,10},{5,11},{6,8},{7,9},{8,22},{9,23... | collective-permute-start | bytes 491528 | tf_op jit(solution)/shard_map/ppermute | solution.py:318
  24.3 3.0 %collective-permute-done.2.refs_1_ = bf16[64,1280]{1,0:T(8,128)(2,1)S(1)} collective-permute-done((bf16[64,1280]{1,0:T(8,128)(2,1)S(1)}, bf16[64,1280]{1,0:T(8,128)(2,1)S(1)}, u32[]{:S(2)}, u32[]{:S(2)}) %collective-permute-start.2) | collective-permute-done | bytes 163872 | tf_op jit(solution)/shard_map/ppermute | solution.py:318
  27.3 2.1 %collective-permute-done.3.refs_3_ = bf16[64,1280]{1,0:T(8,128)(2,1)S(1)} collective-permute-done((bf16[64,1280]{1,0:T(8,128)(2,1)S(1)}, bf16[64,1280]{1,0:T(8,128)(2,1)S(1)}, u32[]{:S(2)}, u32[]{:S(2)}) %collective-permute-start.3) | collective-permute-done | bytes 163872 | tf_op jit(solution)/shard_map/ppermute | solution.py:318
  29.3 2.7 %all-to-all-done.team_ref = bf16[8,64,1280]{2,1,0:T(8,128)(2,1)S(1)} async-done(((bf16[8,64,1280]{2,1,0:T(8,128)(2,1)}), bf16[8,64,1280]{2,1,0:T(8,128)(2,1)S(1)}, u32[]{:S(2)}, u32[]{:S(2)}) %all-to-all-start) | async-done | bytes 1310752 | tf_op jit(solution)/shard_map/all_to_all | solution.py:303
  32.0 3.5 %all-to-all-start.1 = ((bf16[8,64,768]{2,1,0:T(8,128)(2,1)}), bf16[8,64,768]{2,1,0:T(8,128)(2,1)S(1)}, u32[]{:S(2)}, u32[]{:S(2)}) async-start(bf16[8,64,768]{2,1,0:T(8,128)(2,1)} %shard_map.82), calls=%async_computation.1 | async-start | bytes 1572864 | tf_op jit(solution)/shard_map/all_to_all | solution.py:303
  35.8 0.7 slice.39
  36.6 2.6 %collective-permute-start.8 = (bf16[2,64,1280]{2,1,0:T(8,128)(2,1)}, bf16[2,64,1280]{2,1,0:T(8,128)(2,1)S(1)}, u32[]{:S(2)}, u32[]{:S(2)}) collective-permute-start(bf16[2,64,1280]{2,1,0:T(8,128)(2,1)} %slice.39), channel_id=1, source_target_pairs={{0,16},{1,17},{2,18},{3,19},{4,20},{5,21},{6,22},{7,23},{8,24},{9,... | collective-permute-start | bytes 983048 | tf_op jit(solution)/shard_map/ppermute | solution.py:318
  39.2 0.4 or_select_fusion.bias_ref
  39.7 3.9 %collective-permute-done.7.refs_7_ = bf16[64,1280]{1,0:T(8,128)(2,1)} collective-permute-done((bf16[64,1280]{1,0:T(8,128)(2,1)}, bf16[64,1280]{1,0:T(8,128)(2,1)}, u32[]{:S(2)}, u32[]{:S(2)}) %collective-permute-start.7) | collective-permute-done | bytes 163872 | tf_op jit(solution)/shard_map/ppermute | solution.py:318
  43.6 7.8 %all-to-all-done.1.asked_ref = bf16[8,64,768]{2,1,0:T(8,128)(2,1)S(1)} async-done(((bf16[8,64,768]{2,1,0:T(8,128)(2,1)}), bf16[8,64,768]{2,1,0:T(8,128)(2,1)S(1)}, u32[]{:S(2)}, u32[]{:S(2)}) %all-to-all-start.1) | async-done | bytes 786464 | tf_op jit(solution)/shard_map/all_to_all | solution.py:303
  51.4 4.2 %shard_map.84 = (bf16[8,64,640]{2,1,0:T(8,128)(2,1)S(1)}, f32[1,128,640]{2,1,0:T(8,128)S(1)}, f32[1,128,128]{2,1,0:T(8,128)S(1)}, f32[1,128,128]{2,1,0:T(8,128)S(1)}) custom-call(f32[4,5]{1,0:T(4,128)S(1)} %constant_dynamic-slice_fusion.gain_ref, f32[5,128,128]{2,1,0:T(8,128)S(1)} %or_select_fusion.bias_ref, ...), custom_call_target="tpu_custom_call" | custom-call | flops 1006632960 | bytes 7864320 | tf_op jit(solution)/shard_map/pallas_call | solution.py:209
  55.6 1.5 %collective-permute-done.8.refs_0_ = bf16[2,64,1280]{2,1,0:T(8,128)(2,1)S(1)} collective-permute-done((bf16[2,64,1280]{2,1,0:T(8,128)(2,1)}, bf16[2,64,1280]{2,1,0:T(8,128)(2,1)S(1)}, u32[]{:S(2)}, u32[]{:S(2)}) %collective-permute-start.8) | collective-permute-done | bytes 327712 | tf_op jit(solution)/shard_map/ppermute | solution.py:318
  57.2 2.3 %shard_map.85 = bf16[8,64,640]{2,1,0:T(8,128)(2,1)S(1)} custom-call(f32[4,5]{1,0:T(4,128)S(1)} %constant_dynamic-slice_fusion.gain_ref, bf16[8,64,768]{2,1,0:T(8,128)(2,1)S(1)} %all-to-all-done.1.asked_ref, f32[1,128,640]{2,1,0:T(8,128)S(1)} %get-tuple-element.41.sum_ref, ...), custom_call_target="tpu_custom_call", output_to_operand_aliasing={{}: (5, {})} | custom-call | flops 41943040 | bytes 327680 | tf_op jit(solution)/shard_map/pallas_call | solution.py:261
  59.5 13.7 %all_to_all.15.refs_0_ = bf16[8,64,640]{2,1,0:T(8,128)(2,1)} all-to-all(bf16[8,64,640]{2,1,0:T(8,128)(2,1)S(1)} %shard_map.85), channel_id=1, replica_groups={{0,1,2,3,4,5,6,7},{8,9,10,11,12,13,14,15},{16,17,18,19,20,21,22,23},{24..., dimensions={0} | all-to-all | bytes 1310720 | tf_op jit(solution)/shard_map/all_to_all | solution.py:303
  73.2 2.0 %shard_map.86 = bf16[64,5120]{1,0:T(8,128)(2,1)} custom-call(bf16[8,64,640]{2,1,0:T(8,128)(2,1)} %all_to_all.15.refs_0_), custom_call_target="tpu_custom_call" | custom-call | tf_op jit(solution)/shard_map/pallas_call | solution.py:110
  (22 shorter events, 0.4 us)
Async XLA Ops:
  0.0 39.6 %copy-start = (f32[4,40]{1,0:T(4,128)S(1)}, f32[4,40]{1,0:T(4,128)}, u32[]{:S(2)}) copy-start(f32[4,40]{1,0:T(4,128)} %param.15) | copy-start | bytes 1924
  2.9 5.3 %copy-start.5 = (bf16[64,1280]{1,0:T(8,128)(2,1)S(1)}, bf16[64,1280]{1,0:T(8,128)(2,1)}, u32[]{:S(2)}) copy-start(bf16[64,1280]{1,0:T(8,128)(2,1)} %get-tuple-element.26) | copy-start | bytes 491524
  2.9 7.0 %copy-start.4 = (bf16[64,1280]{1,0:T(8,128)(2,1)S(1)}, bf16[64,1280]{1,0:T(8,128)(2,1)}, u32[]{:S(2)}) copy-start(bf16[64,1280]{1,0:T(8,128)(2,1)} %get-tuple-element.27) | copy-start | bytes 491524
  2.9 8.4 %copy-start.3 = (bf16[64,1280]{1,0:T(8,128)(2,1)S(1)}, bf16[64,1280]{1,0:T(8,128)(2,1)}, u32[]{:S(2)}) copy-start(bf16[64,1280]{1,0:T(8,128)(2,1)} %get-tuple-element.28) | copy-start | bytes 491524
  2.9 11.0 %copy-start.2 = (bf16[64,1280]{1,0:T(8,128)(2,1)S(1)}, bf16[64,1280]{1,0:T(8,128)(2,1)}, u32[]{:S(2)}) copy-start(bf16[64,1280]{1,0:T(8,128)(2,1)} %get-tuple-element.29) | copy-start | bytes 491524
  2.9 29.1 %all-to-all-start = ((bf16[8,64,1280]{2,1,0:T(8,128)(2,1)}), bf16[8,64,1280]{2,1,0:T(8,128)(2,1)S(1)}, u32[]{:S(2)}, u32[]{:S(2)}) async-start(bf16[8,64,1280]{2,1,0:T(8,128)(2,1)} %get-tuple-element.25), calls=%async_computation | async-start | bytes 2621440 | tf_op jit(solution)/shard_map/all_to_all | solution.py:303
  8.2 11.8 %copy-start.1 = (s32[40,9]{0,1:T(8,128)S(1)}, s32[40,9]{0,1:T(8,128)}, u32[]{:S(2)}) copy-start(s32[40,9]{0,1:T(8,128)} %param.13) | copy-start | bytes 4324
  8.2 11.8 %collective-permute-start = (bf16[64,1280]{1,0:T(8,128)(2,1)S(1)}, bf16[64,1280]{1,0:T(8,128)(2,1)S(1)}, u32[]{:S(2)}, u32[]{:S(2)}) collective-permute-start(bf16[64,1280]{1,0:T(8,128)(2,1)S(1)} %copy-done.5), channel_id=1, source_target_pairs={{0,8},{1,9},{2,10},{3,11},{4,12},{5,13},{6,14},{7,15},{8,16},{9,17... | collective-permute-start | bytes 491528 | tf_op jit(solution)/shard_map/ppermute | solution.py:318
  9.9 12.7 %collective-permute-start.1 = (bf16[64,1280]{1,0:T(8,128)(2,1)S(1)}, bf16[64,1280]{1,0:T(8,128)(2,1)S(1)}, u32[]{:S(2)}, u32[]{:S(2)}) collective-permute-start(bf16[64,1280]{1,0:T(8,128)(2,1)S(1)} %copy-done.4), channel_id=1, source_target_pairs={{0,10},{1,11},{2,8},{3,9},{4,14},{5,15},{6,12},{7,13},{8,18},{9,19... | collective-permute-start | bytes 491528 | tf_op jit(solution)/shard_map/ppermute | solution.py:318
  11.3 16.0 %collective-permute-start.2 = (bf16[64,1280]{1,0:T(8,128)(2,1)S(1)}, bf16[64,1280]{1,0:T(8,128)(2,1)S(1)}, u32[]{:S(2)}, u32[]{:S(2)}) collective-permute-start(bf16[64,1280]{1,0:T(8,128)(2,1)S(1)} %copy-done.3), channel_id=1, source_target_pairs={{0,9},{1,8},{2,11},{3,10},{4,13},{5,12},{6,15},{7,14},{8,17},{9,16... | collective-permute-start | bytes 491528 | tf_op jit(solution)/shard_map/ppermute | solution.py:318
  13.9 15.4 %collective-permute-start.3 = (bf16[64,1280]{1,0:T(8,128)(2,1)S(1)}, bf16[64,1280]{1,0:T(8,128)(2,1)S(1)}, u32[]{:S(2)}, u32[]{:S(2)}) collective-permute-start(bf16[64,1280]{1,0:T(8,128)(2,1)S(1)} %copy-done.2), channel_id=1, source_target_pairs={{0,11},{1,10},{2,9},{3,8},{4,15},{5,14},{6,13},{7,12},{8,19},{9,18... | collective-permute-start | bytes 491528 | tf_op jit(solution)/shard_map/ppermute | solution.py:318
  14.2 25.4 %collective-permute-start.4 = (bf16[64,1280]{1,0:T(8,128)(2,1)}, bf16[64,1280]{1,0:T(8,128)(2,1)}, u32[]{:S(2)}, u32[]{:S(2)}) collective-permute-start(bf16[64,1280]{1,0:T(8,128)(2,1)} %get-tuple-element.37), channel_id=1, source_target_pairs={{0,12},{1,13},{2,14},{3,15},{4,8},{5,9},{6,10},{7,11},{8,20},{9,21... | collective-permute-start | bytes 491528 | tf_op jit(solution)/shard_map/ppermute | solution.py:318
  20.1 19.6 %collective-permute-start.5 = (bf16[64,1280]{1,0:T(8,128)(2,1)}, bf16[64,1280]{1,0:T(8,128)(2,1)}, u32[]{:S(2)}, u32[]{:S(2)}) collective-permute-start(bf16[64,1280]{1,0:T(8,128)(2,1)} %get-tuple-element.38), channel_id=1, source_target_pairs={{0,13},{1,12},{2,15},{3,14},{4,9},{5,8},{6,11},{7,10},{8,21},{9,20... | collective-permute-start | bytes 491528 | tf_op jit(solution)/shard_map/ppermute | solution.py:318
  22.6 17.0 %collective-permute-start.6 = (bf16[64,1280]{1,0:T(8,128)(2,1)}, bf16[64,1280]{1,0:T(8,128)(2,1)}, u32[]{:S(2)}, u32[]{:S(2)}) collective-permute-start(bf16[64,1280]{1,0:T(8,128)(2,1)} %get-tuple-element.39), channel_id=1, source_target_pairs={{0,14},{1,15},{2,12},{3,13},{4,10},{5,11},{6,8},{7,9},{8,22},{9,23... | collective-permute-start | bytes 491528 | tf_op jit(solution)/shard_map/ppermute | solution.py:318
  27.3 16.3 %collective-permute-start.7 = (bf16[64,1280]{1,0:T(8,128)(2,1)}, bf16[64,1280]{1,0:T(8,128)(2,1)}, u32[]{:S(2)}, u32[]{:S(2)}) collective-permute-start(bf16[64,1280]{1,0:T(8,128)(2,1)} %get-tuple-element.40), channel_id=1, source_target_pairs={{0,15},{1,14},{2,13},{3,12},{4,11},{5,10},{6,9},{7,8},{8,23},{9,22... | collective-permute-start | bytes 491528 | tf_op jit(solution)/shard_map/ppermute | solution.py:318
  32.0 19.4 %all-to-all-start.1 = ((bf16[8,64,768]{2,1,0:T(8,128)(2,1)}), bf16[8,64,768]{2,1,0:T(8,128)(2,1)S(1)}, u32[]{:S(2)}, u32[]{:S(2)}) async-start(bf16[8,64,768]{2,1,0:T(8,128)(2,1)} %shard_map.82), calls=%async_computation.1 | async-start | bytes 1572864 | tf_op jit(solution)/shard_map/all_to_all | solution.py:303
  36.6 20.6 %collective-permute-start.8 = (bf16[2,64,1280]{2,1,0:T(8,128)(2,1)}, bf16[2,64,1280]{2,1,0:T(8,128)(2,1)S(1)}, u32[]{:S(2)}, u32[]{:S(2)}) collective-permute-start(bf16[2,64,1280]{2,1,0:T(8,128)(2,1)} %slice.39), channel_id=1, source_target_pairs={{0,16},{1,17},{2,18},{3,19},{4,20},{5,21},{6,22},{7,23},{8,24},{9,... | collective-permute-start | bytes 983048 | tf_op jit(solution)/shard_map/ppermute | solution.py:318

commit v4 on v3

--- a/solution.py
+++ b/solution.py
@@ -98,21 +98,23 @@
     )(history, frame_index, step_index, own_q)
 
 
-def unpack(parts, starts, head_share):
-    members, tokens = parts[0].shape[:2]
+def unpack(blocks, group, tiles, order):
+    members = len(blocks)
+    tokens, width = blocks[0].shape
 
     def body(*refs):
-        out = refs[-1]
-        for start, ref in zip(starts, refs[:-1]):
-            for n in range(members):
-                out[:, pl.ds((n * head_share + start) * HD, ref.shape[-1])] = ref[n]
-
-    return pl.pallas_call(
-        body,
-        out_shape=jax.ShapeDtypeStruct((tokens, members * head_share * HD), jnp.bfloat16),
-        in_specs=[VMEM] * len(parts),
+        member = here(group, tiles)
+        for m, ref in zip(order, refs[:-1]):
+            lanes = pl.multiple_of(sender(member, m, members) * width, HD)
+            refs[-1][:, pl.ds(lanes, width)] = ref[...]
+
+    return pl.pallas_call(
+        body,
+        out_shape=jax.ShapeDtypeStruct((tokens, members * width), jnp.bfloat16),
+        in_specs=[VMEM] * members,
         out_specs=VMEM,
-    )(*parts)
+        compiler_params=pltpu.CompilerParams(vmem_limit_bytes=16 * 1024 * 1024),
+    )(*[blocks[m] for m in order])
 
 
 FACTOR = math.log2(math.e) / math.sqrt(HD)
@@ -156,121 +158,84 @@
     )
 
 
+def put_frame(out_ref, j, group, gain_ref, bias_ref, asked_ref, team_ref, before_ref, far_refs):
+    members, tokens, width = out_ref.shape
+    tiles = members // group
+    frame_tok = tiles * tokens
+    past, step = frame_facts(asked_ref, j * tiles, frame_tok)
+    frames = []
+    for d in range(WIN + 1):
+        hop = max(0, -((j - d) // group))
+        ref = (team_ref, before_ref, *far_refs)[hop]
+        skipped = first_needed(hop, group) if hop > 1 else 0
+        frames.append((ref, (j - d + hop * group - skipped) * tiles))
+    for h in range(width // HD):
+        lane = h * HD
+        q = rows_of(asked_ref, j * tiles, tiles, lane)
+        k = jnp.concatenate([rows_of(r, row, tiles, lane) for r, row in frames])
+        v = jnp.concatenate([rows_of(r, row, tiles, width + lane) for r, row in frames])
+        scores = scores_of(q, k)
+        scores = jnp.concatenate(
+            [scores[:, :frame_tok] + bias_ref[h], scores[:, frame_tok:] + past], axis=1
+        )
+        weights = jnp.exp2(scores - jnp.max(scores, axis=1, keepdims=True))
+        blended, norm = weigh(weights, v)
+        result = (blended / norm * head_gain(gain_ref, step, h)).astype(jnp.bfloat16)
+        out_ref[j * tiles : (j + 1) * tiles, :, lane : lane + HD] = result.reshape(
+            tiles, tokens, HD
+        )
+
+
 def attend_near(asked, team, ahead, bias, gains, group):
     members, tokens = team.shape[:2]
-    tiles = members // group
-    frame_tok = tiles * tokens
     width = team.shape[-1] // 2
-    heads = width // HD
-    unfinished = max(0, min(group, WIN - group))
 
     def body(gain_ref, bias_ref, asked_ref, team_ref, *refs):
-        ahead_refs = refs[:members]
-        out_ref, sum_ref, top_ref, norm_ref, before_ref = refs[members:]
-        member = here(group, tiles)
-        for m, ref in enumerate(ahead_refs):
+        out_ref, before_ref = refs[members:]
+        member = here(group, members // group)
+        for m, ref in enumerate(refs[:members]):
             before_ref[sender(member, m, members)] = ref[...]
-        lane_id = lax.broadcasted_iota(jnp.int32, (frame_tok, HD), 1)
-        for j in range(group):
-            past, step = frame_facts(asked_ref, j * tiles, frame_tok)
-            near = min(WIN, j + group)
-            frames = [(team_ref, j - d) if d <= j else (before_ref, j - d + group) for d in range(near + 1)]
-            tops = norms = jnp.zeros((frame_tok, HD), jnp.float32)
-            for h in range(heads):
-                lane = h * HD
-                q = rows_of(asked_ref, j * tiles, tiles, lane)
-                k = jnp.concatenate([rows_of(r, f * tiles, tiles, lane) for r, f in frames])
-                v = jnp.concatenate([rows_of(r, f * tiles, tiles, width + lane) for r, f in frames])
-                scores = scores_of(q, k)
-                scores = jnp.concatenate(
-                    [
-                        scores[:, :frame_tok] + bias_ref[h],
-                        scores[:, frame_tok:] + past[:, : near * frame_tok],
-                    ],
-                    axis=1,
-                )
-                top = jnp.max(scores, axis=1, keepdims=True)
-                p = jnp.exp2(scores - top)
-                blended, norm = weigh(p, v)
-                if j < unfinished:
-                    sum_ref[j, :, lane : lane + HD] = blended
-                    tops = jnp.where(lane_id == h, top, tops)
-                    norms = jnp.where(lane_id == h, norm, norms)
-                else:
-                    result = (blended / norm * head_gain(gain_ref, step, h)).astype(jnp.bfloat16)
-                    out_ref[j * tiles : (j + 1) * tiles, :, lane : lane + HD] = result.reshape(
-                        tiles, tokens, HD
-                    )
-            if j < unfinished:
-                top_ref[j] = tops
-                norm_ref[j] = norms
-
-    parts = max(1, unfinished)
+        for j in range(min(group, max(0, WIN - group)), group):
+            put_frame(out_ref, j, group, gain_ref, bias_ref, asked_ref, team_ref, before_ref, [])
+
     return pl.pallas_call(
         body,
         out_shape=[
             jax.ShapeDtypeStruct((members, tokens, width), jnp.bfloat16),
-            jax.ShapeDtypeStruct((parts, frame_tok, width), jnp.float32),
-            jax.ShapeDtypeStruct((parts, frame_tok, HD), jnp.float32),
-            jax.ShapeDtypeStruct((parts, frame_tok, HD), jnp.float32),
+            jax.ShapeDtypeStruct(team.shape, jnp.bfloat16),
         ],
         in_specs=[SMEM] + [VMEM] * (3 + members),
-        out_specs=[VMEM] * 4,
-        scratch_shapes=[pltpu.VMEM((members, tokens, 2 * width), jnp.bfloat16)],
-        cost_estimate=cost(group * heads * (WIN + 1), frame_tok),
+        out_specs=[VMEM] * 2,
+        cost_estimate=cost(group * width // HD * (WIN + 1), members // group * tokens),
         compiler_params=pltpu.CompilerParams(vmem_limit_bytes=48 * 1024 * 1024),
     )(gains, bias, asked, team, *ahead)
 
 
-def attend_far(asked, far, state, gains, group):
-    out, sums, tops, norms = state
-    members, tokens, width = out.shape
-    tiles = members // group
-    frame_tok = tiles * tokens
-    heads = width // HD
-    unfinished = min(group, WIN - group)
-
-    def body(gain_ref, asked_ref, sum_ref, top_ref, norm_ref, near_ref, *refs):
-        far_refs, out_ref = refs[:-1], refs[-1]
-        for j in range(unfinished):
-            past, step = frame_facts(asked_ref, j * tiles, frame_tok)
-            frames = []
-            for d in range(j + group + 1, WIN + 1):
-                hop = -((j - d) // group)
-                frames.append((far_refs[hop - 2], j - d + hop * group - first_needed(hop, group)))
-            for h in range(heads):
-                lane = h * HD
-                q = rows_of(asked_ref, j * tiles, tiles, lane)
-                k = jnp.concatenate([rows_of(r, f * tiles, tiles, lane) for r, f in frames])
-                v = jnp.concatenate([rows_of(r, f * tiles, tiles, width + lane) for r, f in frames])
-                scores = scores_of(q, k) + past[:, (j + group) * frame_tok :]
-                top = top_ref[j, :, h : h + 1]
-                both = jnp.maximum(top, jnp.max(scores, axis=1, keepdims=True))
-                blended, norm = weigh(jnp.exp2(scores - both), v)
-                kept = jnp.exp2(top - both)
-                blended += sum_ref[j, :, lane : lane + HD] * kept
-                norm += norm_ref[j, :, h : h + 1] * kept
-                result = (blended / norm * head_gain(gain_ref, step, h)).astype(jnp.bfloat16)
-                out_ref[j * tiles : (j + 1) * tiles, :, lane : lane + HD] = result.reshape(
-                    tiles, tokens, HD
-                )
-
-    def leading(array):
-        return pl.BlockSpec((unfinished * tiles,) + array.shape[1:], lambda i: (0, 0, 0))
-
-    return pl.pallas_call(
-        body,
-        grid=(1,),
-        out_shape=jax.ShapeDtypeStruct(out.shape, out.dtype),
-        in_specs=[SMEM, leading(asked)]
-        + [VMEM] * 3
-        + [pl.BlockSpec(memory_space=pl.ANY)]
-        + [VMEM] * len(far),
-        out_specs=leading(out),
-        input_output_aliases={5: 0},
-        cost_estimate=cost(unfinished * heads, frame_tok),
+def attend_far(asked, team, before, far, near, bias, gains, group):
+    members, tokens, width = near.shape
+    finished = min(group, max(0, WIN - group)) * members // group
+
+    def body(gain_ref, bias_ref, asked_ref, team_ref, before_ref, near_ref, *refs):
+        far_refs, outs, all_ref = refs[: len(far)], refs[len(far) : -1], refs[-1]
+        if finished < members:
+            all_ref[finished:] = near_ref[finished:]
+        for j in range(finished * group // members):
+            put_frame(
+                all_ref, j, group, gain_ref, bias_ref, asked_ref, team_ref, before_ref, far_refs
+            )
+        member = here(group, members // group)
+        for m, out in enumerate(outs):
+            out[...] = all_ref[partner(member, m, members)]
+
+    return pl.pallas_call(
+        body,
+        out_shape=[jax.ShapeDtypeStruct((tokens, width), near.dtype)] * members,
+        in_specs=[SMEM] + [VMEM] * (5 + len(far)),
+        out_specs=[VMEM] * members,
+        scratch_shapes=[pltpu.VMEM(near.shape, near.dtype)],
+        cost_estimate=cost(width // HD * (WIN + 1), members // group * tokens),
         compiler_params=pltpu.CompilerParams(vmem_limit_bytes=48 * 1024 * 1024),
-    )(gains, asked, sums, tops, norms, out, *far)
+    )(gains, bias, asked, team, before, near, *far)
 
 
 def window_bias(mask_rows, tile_count):
@@ -341,9 +306,11 @@
     gains = lax.dynamic_slice(step_gain, (0, share), (STEPS, head_share))
     my_mask = lax.dynamic_slice(window_mask, (share, 0), (head_share, 9))
     bias = window_bias(my_mask, tile_count)
-    state = attend_near(asked, team, ahead, bias, gains, group)
-    out = attend_far(asked, far, state, gains, group) if far else state[0]
-    return unpack([exchange(out)], [0], head_share)[None, None]
+    near, before = attend_near(asked, team, ahead, bias, gains, group)
+    out = attend_far(asked, team, before, far, near, bias, gains, group)
+    order = [4, 5, 6, 7, 1, 3, 2, 0]
+    back = {m: team_permute(out[m], 0, m) if m else out[m] for m in order}
+    return unpack(back, group, tile_count, order)[None, None]
 
 
 def solution(mesh):

time: 75.5 us -> 71.1 us (0.942)
  blocking collectives: 13.7 us -> 0 us
  starting transfers between devices: 24 us -> 30.2 us
  waiting for transfers between devices: 21 us -> 26.3 us
  Pallas kernels: 13.5 us -> 11.1 us
    all_to_all x1 -> x0, blocking collectives: 13.7 us -> none  [exchange(): lax.all_to_all(block, both, 0, 0, axis_index_groups=[[t * members + n for...]
    ppermute x9 -> x16, starting transfers between devices: 15.2 us -> 21.3 us  [team_permute(): return lax.ppermute(block, both, route)]
    ppermute x9 -> x16, waiting for transfers between devices: 10.5 us -> 15.7 us  [team_permute(): return lax.ppermute(block, both, route)]
    pallas_call x2, Pallas kernels: 4.31 us -> 2.63 us  [the longest x1 1.72 us: attend_far(): pl.pallas_call(body, out_shape=[jax.ShapeDtypeStruct((tokens, width), nea...]
  transfers between devices with their start and end apart: 11 -> 18, of which waited for: 6 -> 10; matrix products, arithmetic and copies ran while one was open for 2% -> 2% of each run, Pallas kernels for 8% -> 8%
where the time goes in v4:
time: 71.1 us; the launch traced here: 70.6 us
  starting transfers between devices  30.2 us (42%)
  waiting for transfers between devices  26.3 us (37%)
  Pallas kernels  11.1 us (16%)
  between operations  1.41 us (2%)
  local copies, waits for them, and re-layouts  0.85 us (1%)
  other arithmetic  0.72 us (1%)
    ppermute x16, starting transfers between devices, team_permute(): return lax.ppermute(block, both, route)  21.3 us
    ppermute x16, waiting for transfers between devices, team_permute(): return lax.ppermute(block, both, route)  15.7 us
    all_to_all x2, waiting for transfers between devices, exchange(): lax.all_to_all(block, both, 0, 0, axis_index_groups=[[t * members + n for...  10.5 us
    all_to_all x2, starting transfers between devices, exchange(): lax.all_to_all(block, both, 0, 0, axis_index_groups=[[t * members + n for...  8.86 us
    pallas_call x1, Pallas kernels, attend_near(): pl.pallas_call(body, out_shape=[jax.ShapeDtypeStruct((members, tokens, wi...  3.56 us
    pallas_call x1, Pallas kernels, pack_kv(): pl.pallas_call(body, out_shape=[jax.ShapeDtypeStruct((members,) + shape,...  2.87 us
    pallas_call x1, Pallas kernels, pack_queries(): pl.pallas_call(body, out_shape=jax.ShapeDtypeStruct((members, tokens, wid...  2.06 us
    pallas_call x1, Pallas kernels, attend_far(): pl.pallas_call(body, out_shape=[jax.ShapeDtypeStruct((tokens, width), nea...  1.72 us
  transfers between devices with their start and end apart: 18, of which 10 were waited for; matrix products, arithmetic and copies ran while one was open for 2% of the time, Pallas kernels for 8%

profile of v4, /device:TPU:0, one launch (start us, length us, event | category | flops | bytes accessed | tf_op | source)
XLA Modules:
  0.0 70.6 jit_solution(9622360918785433717)
XLA Ops:
  0.0 2.9 %shard_map.83 = (bf16[8,64,1280]{2,1,0:T(8,128)(2,1)}, bf16[64,1280]{1,0:T(8,128)(2,1)}, bf16[64,1280]{1,0:T(8,128)(2,1)}, bf16[64,1280]{1,0:T(8,128)(2,1)}, bf1...) custom-call(bf16[64,5120]{1,0:T(8,128)(2,1)} %bitcast.22, ...), custom_call_target="tpu_custom_call" | custom-call | tf_op jit(solution)/shard_map/pallas_call | solution.py:65
  2.9 5.3 %all-to-all-start = ((bf16[8,64,1280]{2,1,0:T(8,128)(2,1)}), bf16[8,64,1280]{2,1,0:T(8,128)(2,1)S(1)}, u32[]{:S(2)}, u32[]{:S(2)}) async-start(bf16[8,64,1280]{2,1,0:T(8,128)(2,1)} %get-tuple-element.31), calls=%async_computation | async-start | bytes 2621440 | tf_op jit(solution)/shard_map/all_to_all | solution.py:268
  8.2 1.6 %collective-permute-start = (bf16[64,1280]{1,0:T(8,128)(2,1)S(1)}, bf16[64,1280]{1,0:T(8,128)(2,1)S(1)}, u32[]{:S(2)}, u32[]{:S(2)}) collective-permute-start(bf16[64,1280]{1,0:T(8,128)(2,1)S(1)} %copy-done.5), channel_id=1, source_target_pairs={{0,8},{1,9},{2,10},{3,11},{4,12},{5,13},{6,14},{7,15},{8,16},{9,17... | collective-permute-start | bytes 491528 | tf_op jit(solution)/shard_map/ppermute | solution.py:283
  9.9 1.4 %collective-permute-start.1 = (bf16[64,1280]{1,0:T(8,128)(2,1)S(1)}, bf16[64,1280]{1,0:T(8,128)(2,1)S(1)}, u32[]{:S(2)}, u32[]{:S(2)}) collective-permute-start(bf16[64,1280]{1,0:T(8,128)(2,1)S(1)} %copy-done.4), channel_id=1, source_target_pairs={{0,10},{1,11},{2,8},{3,9},{4,14},{5,15},{6,12},{7,13},{8,18},{9,19... | collective-permute-start | bytes 491528 | tf_op jit(solution)/shard_map/ppermute | solution.py:283
  11.3 2.7 %collective-permute-start.2 = (bf16[64,1280]{1,0:T(8,128)(2,1)S(1)}, bf16[64,1280]{1,0:T(8,128)(2,1)S(1)}, u32[]{:S(2)}, u32[]{:S(2)}) collective-permute-start(bf16[64,1280]{1,0:T(8,128)(2,1)S(1)} %copy-done.3), channel_id=1, source_target_pairs={{0,9},{1,8},{2,11},{3,10},{4,13},{5,12},{6,15},{7,14},{8,17},{9,16... | collective-permute-start | bytes 491528 | tf_op jit(solution)/shard_map/ppermute | solution.py:283
  14.2 2.4 %collective-permute-start.4 = (bf16[64,1280]{1,0:T(8,128)(2,1)}, bf16[64,1280]{1,0:T(8,128)(2,1)}, u32[]{:S(2)}, u32[]{:S(2)}) collective-permute-start(bf16[64,1280]{1,0:T(8,128)(2,1)} %get-tuple-element.43), channel_id=1, source_target_pairs={{0,12},{1,13},{2,14},{3,15},{4,8},{5,9},{6,10},{7,11},{8,20},{9,21... | collective-permute-start | bytes 491528 | tf_op jit(solution)/shard_map/ppermute | solution.py:283
  17.9 2.1 %shard_map.82 = bf16[8,64,768]{2,1,0:T(8,128)(2,1)} custom-call(s32[1,5]{1,0:T(1,128)} %history_ref.1, s32[1]{0:T(128)S(6)} %copy.10.index_ref, s32[1]{0:T(128)S(6)} %copy.9.step_ref, bf16[64,5120]{1,0:T(8,128)(2,1)} %bitcast.24), custom_call_target="tpu_custom_call" | custom-call | tf_op jit(solution)/shard_map/pallas_call | solution.py:93
  20.1 2.5 %collective-permute-start.5 = (bf16[64,1280]{1,0:T(8,128)(2,1)}, bf16[64,1280]{1,0:T(8,128)(2,1)}, u32[]{:S(2)}, u32[]{:S(2)}) collective-permute-start(bf16[64,1280]{1,0:T(8,128)(2,1)} %get-tuple-element.44), channel_id=1, source_target_pairs={{0,13},{1,12},{2,15},{3,14},{4,9},{5,8},{6,11},{7,10},{8,21},{9,20... | collective-permute-start | bytes 491528 | tf_op jit(solution)/shard_map/ppermute | solution.py:283
  22.6 1.7 %collective-permute-start.6 = (bf16[64,1280]{1,0:T(8,128)(2,1)}, bf16[64,1280]{1,0:T(8,128)(2,1)}, u32[]{:S(2)}, u32[]{:S(2)}) collective-permute-start(bf16[64,1280]{1,0:T(8,128)(2,1)} %get-tuple-element.45), channel_id=1, source_target_pairs={{0,14},{1,15},{2,12},{3,13},{4,10},{5,11},{6,8},{7,9},{8,22},{9,23... | collective-permute-start | bytes 491528 | tf_op jit(solution)/shard_map/ppermute | solution.py:283
  24.3 3.0 %collective-permute-done.2.refs_1_ = bf16[64,1280]{1,0:T(8,128)(2,1)S(1)} collective-permute-done((bf16[64,1280]{1,0:T(8,128)(2,1)S(1)}, bf16[64,1280]{1,0:T(8,128)(2,1)S(1)}, u32[]{:S(2)}, u32[]{:S(2)}) %collective-permute-start.2) | collective-permute-done | bytes 163872 | tf_op jit(solution)/shard_map/ppermute | solution.py:283
  27.2 2.1 %collective-permute-done.3.refs_3_ = bf16[64,1280]{1,0:T(8,128)(2,1)S(1)} collective-permute-done((bf16[64,1280]{1,0:T(8,128)(2,1)S(1)}, bf16[64,1280]{1,0:T(8,128)(2,1)S(1)}, u32[]{:S(2)}, u32[]{:S(2)}) %collective-permute-start.3) | collective-permute-done | bytes 163872 | tf_op jit(solution)/shard_map/ppermute | solution.py:283
  29.3 2.7 %all-to-all-done.team_ref = bf16[8,64,1280]{2,1,0:T(8,128)(2,1)S(1)} async-done(((bf16[8,64,1280]{2,1,0:T(8,128)(2,1)}), bf16[8,64,1280]{2,1,0:T(8,128)(2,1)S(1)}, u32[]{:S(2)}, u32[]{:S(2)}) %all-to-all-start) | async-done | bytes 1310752 | tf_op jit(solution)/shard_map/all_to_all | solution.py:268
  32.0 3.5 %all-to-all-start.1 = ((bf16[8,64,768]{2,1,0:T(8,128)(2,1)}), bf16[8,64,768]{2,1,0:T(8,128)(2,1)S(1)}, u32[]{:S(2)}, u32[]{:S(2)}) async-start(bf16[8,64,768]{2,1,0:T(8,128)(2,1)} %shard_map.82), calls=%async_computation.1 | async-start | bytes 1572864 | tf_op jit(solution)/shard_map/all_to_all | solution.py:268
  36.6 2.6 %collective-permute-start.8 = (bf16[2,64,1280]{2,1,0:T(8,128)(2,1)}, bf16[2,64,1280]{2,1,0:T(8,128)(2,1)S(1)}, u32[]{:S(2)}, u32[]{:S(2)}) collective-permute-start(bf16[2,64,1280]{2,1,0:T(8,128)(2,1)} %slice.39), channel_id=1, source_target_pairs={{0,16},{1,17},{2,18},{3,19},{4,20},{5,21},{6,22},{7,23},{8,24},{9,... | collective-permute-start | bytes 983048 | tf_op jit(solution)/shard_map/ppermute | solution.py:283
  39.7 3.9 %collective-permute-done.7.refs_7_ = bf16[64,1280]{1,0:T(8,128)(2,1)} collective-permute-done((bf16[64,1280]{1,0:T(8,128)(2,1)}, bf16[64,1280]{1,0:T(8,128)(2,1)}, u32[]{:S(2)}, u32[]{:S(2)}) %collective-permute-start.7) | collective-permute-done | bytes 163872 | tf_op jit(solution)/shard_map/ppermute | solution.py:283
  43.6 7.8 %all-to-all-done.1.asked_ref = bf16[8,64,768]{2,1,0:T(8,128)(2,1)S(1)} async-done(((bf16[8,64,768]{2,1,0:T(8,128)(2,1)}), bf16[8,64,768]{2,1,0:T(8,128)(2,1)S(1)}, u32[]{:S(2)}, u32[]{:S(2)}) %all-to-all-start.1) | async-done | bytes 786464 | tf_op jit(solution)/shard_map/all_to_all | solution.py:268
  51.4 3.6 %shard_map.84 = (bf16[8,64,640]{2,1,0:T(8,128)(2,1)S(1)}, bf16[8,64,1280]{2,1,0:T(8,128)(2,1)S(1)}) custom-call(f32[4,5]{1,0:T(4,128)S(1)} %constant_dynamic-slice_fusion.gain_ref, f32[5,128,128]{2,1,0:T(8,128)S(1)} %or_select_fusion.bias_ref, bf16[8,64,768]{2,1,0:T(8,128)(2,1)S(1)} %all-to-all-done.1.asked_ref, ...), custom_call_target="tpu_custom_call" | custom-call | flops 1006632960 | bytes 7864320 | tf_op jit(solution)/shard_map/pallas_call | solution.py:201
  55.0 2.2 %collective-permute-done.8.refs_0_ = bf16[2,64,1280]{2,1,0:T(8,128)(2,1)S(1)} collective-permute-done((bf16[2,64,1280]{2,1,0:T(8,128)(2,1)}, bf16[2,64,1280]{2,1,0:T(8,128)(2,1)S(1)}, u32[]{:S(2)}, u32[]{:S(2)}) %collective-permute-start.8) | collective-permute-done | bytes 327712 | tf_op jit(solution)/shard_map/ppermute | solution.py:283
  57.2 1.7 %shard_map.85 = (bf16[64,640]{1,0:T(8,128)(2,1)S(1)}, bf16[64,640]{1,0:T(8,128)(2,1)S(1)}, bf16[64,640]{1,0:T(8,128)(2,1)S(1)}, bf16[64,640]{1,0:T(8,128)(2,1)S(...) custom-call(f32[4,5]{1,0:T(4,128)S(1)} %constant_dynamic-slice_fusio, ...), custom_call_target="tpu_custom_call" | custom-call | flops 251658240 | bytes 1966080 | tf_op jit(solution)/shard_map/pallas_call | solution.py:230
  58.9 1.5 %collective-permute-start.10 = (bf16[64,640]{1,0:T(8,128)(2,1)S(1)}, bf16[64,640]{1,0:T(8,128)(2,1)S(1)}, u32[]{:S(2)}, u32[]{:S(2)}) collective-permute-start(bf16[64,640]{1,0:T(8,128)(2,1)S(1)} %get-tuple-element.50), channel_id=1, source_target_pairs={{0,5},{1,4},{2,7},{3,6},{4,1},{5,0},{6,3},{7,2},{8,13},{9,12},{10,... | collective-permute-start | bytes 245768 | tf_op jit(solution)/shard_map/ppermute | solution.py:283
  62.0 1.7 %collective-permute-start.13 = (bf16[64,640]{1,0:T(8,128)(2,1)S(1)}, bf16[64,640]{1,0:T(8,128)(2,1)S(1)}, u32[]{:S(2)}, u32[]{:S(2)}) collective-permute-start(bf16[64,640]{1,0:T(8,128)(2,1)S(1)} %get-tuple-element.53), channel_id=1, source_target_pairs={{0,1},{1,0},{2,3},{3,2},{4,5},{5,4},{6,7},{7,6},{8,9},{9,8},{10,11... | collective-permute-start | bytes 245768 | tf_op jit(solution)/shard_map/ppermute | solution.py:283
  63.6 1.5 %collective-permute-done.10.refs_1_ = bf16[64,640]{1,0:T(8,128)(2,1)S(1)} collective-permute-done((bf16[64,640]{1,0:T(8,128)(2,1)S(1)}, bf16[64,640]{1,0:T(8,128)(2,1)S(1)}, u32[]{:S(2)}, u32[]{:S(2)}) %collective-permute-start.10) | collective-permute-done | bytes 81952 | tf_op jit(solution)/shard_map/ppermute | solution.py:283
  65.2 1.4 %collective-permute-start.9 = (bf16[64,640]{1,0:T(8,128)(2,1)S(1)}, bf16[64,640]{1,0:T(8,128)(2,1)S(1)}, u32[]{:S(2)}, u32[]{:S(2)}) collective-permute-start(bf16[64,640]{1,0:T(8,128)(2,1)S(1)} %get-tuple-element.49), channel_id=1, source_target_pairs={{0,4},{1,5},{2,6},{3,7},{4,0},{5,1},{6,2},{7,3},{8,12},{9,13},{10,... | collective-permute-start | bytes 245768 | tf_op jit(solution)/shard_map/ppermute | solution.py:283
  67.0 1.8 %collective-permute-done.13.refs_4_ = bf16[64,640]{1,0:T(8,128)(2,1)S(1)} collective-permute-done((bf16[64,640]{1,0:T(8,128)(2,1)S(1)}, bf16[64,640]{1,0:T(8,128)(2,1)S(1)}, u32[]{:S(2)}, u32[]{:S(2)}) %collective-permute-start.13) | collective-permute-done | bytes 81952 | tf_op jit(solution)/shard_map/ppermute | solution.py:283
  (35 shorter events, 5.6 us)
Async XLA Ops:
  0.0 39.6 %copy-start = (f32[4,40]{1,0:T(4,128)S(1)}, f32[4,40]{1,0:T(4,128)}, u32[]{:S(2)}) copy-start(f32[4,40]{1,0:T(4,128)} %param.15) | copy-start | bytes 1924
  2.9 5.3 %copy-start.5 = (bf16[64,1280]{1,0:T(8,128)(2,1)S(1)}, bf16[64,1280]{1,0:T(8,128)(2,1)}, u32[]{:S(2)}) copy-start(bf16[64,1280]{1,0:T(8,128)(2,1)} %get-tuple-element.32) | copy-start | bytes 491524
  2.9 7.0 %copy-start.4 = (bf16[64,1280]{1,0:T(8,128)(2,1)S(1)}, bf16[64,1280]{1,0:T(8,128)(2,1)}, u32[]{:S(2)}) copy-start(bf16[64,1280]{1,0:T(8,128)(2,1)} %get-tuple-element.33) | copy-start | bytes 491524
  2.9 8.4 %copy-start.3 = (bf16[64,1280]{1,0:T(8,128)(2,1)S(1)}, bf16[64,1280]{1,0:T(8,128)(2,1)}, u32[]{:S(2)}) copy-start(bf16[64,1280]{1,0:T(8,128)(2,1)} %get-tuple-element.34) | copy-start | bytes 491524
  2.9 11.0 %copy-start.2 = (bf16[64,1280]{1,0:T(8,128)(2,1)S(1)}, bf16[64,1280]{1,0:T(8,128)(2,1)}, u32[]{:S(2)}) copy-start(bf16[64,1280]{1,0:T(8,128)(2,1)} %get-tuple-element.35) | copy-start | bytes 491524
  2.9 29.1 %all-to-all-start = ((bf16[8,64,1280]{2,1,0:T(8,128)(2,1)}), bf16[8,64,1280]{2,1,0:T(8,128)(2,1)S(1)}, u32[]{:S(2)}, u32[]{:S(2)}) async-start(bf16[8,64,1280]{2,1,0:T(8,128)(2,1)} %get-tuple-element.31), calls=%async_computation | async-start | bytes 2621440 | tf_op jit(solution)/shard_map/all_to_all | solution.py:268
  8.2 11.7 %copy-start.1 = (s32[40,9]{0,1:T(8,128)S(1)}, s32[40,9]{0,1:T(8,128)}, u32[]{:S(2)}) copy-start(s32[40,9]{0,1:T(8,128)} %param.13) | copy-start | bytes 4324
  8.2 11.8 %collective-permute-start = (bf16[64,1280]{1,0:T(8,128)(2,1)S(1)}, bf16[64,1280]{1,0:T(8,128)(2,1)S(1)}, u32[]{:S(2)}, u32[]{:S(2)}) collective-permute-start(bf16[64,1280]{1,0:T(8,128)(2,1)S(1)} %copy-done.5), channel_id=1, source_target_pairs={{0,8},{1,9},{2,10},{3,11},{4,12},{5,13},{6,14},{7,15},{8,16},{9,17... | collective-permute-start | bytes 491528 | tf_op jit(solution)/shard_map/ppermute | solution.py:283
  9.9 12.7 %collective-permute-start.1 = (bf16[64,1280]{1,0:T(8,128)(2,1)S(1)}, bf16[64,1280]{1,0:T(8,128)(2,1)S(1)}, u32[]{:S(2)}, u32[]{:S(2)}) collective-permute-start(bf16[64,1280]{1,0:T(8,128)(2,1)S(1)} %copy-done.4), channel_id=1, source_target_pairs={{0,10},{1,11},{2,8},{3,9},{4,14},{5,15},{6,12},{7,13},{8,18},{9,19... | collective-permute-start | bytes 491528 | tf_op jit(solution)/shard_map/ppermute | solution.py:283
  11.3 16.0 %collective-permute-start.2 = (bf16[64,1280]{1,0:T(8,128)(2,1)S(1)}, bf16[64,1280]{1,0:T(8,128)(2,1)S(1)}, u32[]{:S(2)}, u32[]{:S(2)}) collective-permute-start(bf16[64,1280]{1,0:T(8,128)(2,1)S(1)} %copy-done.3), channel_id=1, source_target_pairs={{0,9},{1,8},{2,11},{3,10},{4,13},{5,12},{6,15},{7,14},{8,17},{9,16... | collective-permute-start | bytes 491528 | tf_op jit(solution)/shard_map/ppermute | solution.py:283
  13.9 15.4 %collective-permute-start.3 = (bf16[64,1280]{1,0:T(8,128)(2,1)S(1)}, bf16[64,1280]{1,0:T(8,128)(2,1)S(1)}, u32[]{:S(2)}, u32[]{:S(2)}) collective-permute-start(bf16[64,1280]{1,0:T(8,128)(2,1)S(1)} %copy-done.2), channel_id=1, source_target_pairs={{0,11},{1,10},{2,9},{3,8},{4,15},{5,14},{6,13},{7,12},{8,19},{9,18... | collective-permute-start | bytes 491528 | tf_op jit(solution)/shard_map/ppermute | solution.py:283
  14.2 25.4 %collective-permute-start.4 = (bf16[64,1280]{1,0:T(8,128)(2,1)}, bf16[64,1280]{1,0:T(8,128)(2,1)}, u32[]{:S(2)}, u32[]{:S(2)}) collective-permute-start(bf16[64,1280]{1,0:T(8,128)(2,1)} %get-tuple-element.43), channel_id=1, source_target_pairs={{0,12},{1,13},{2,14},{3,15},{4,8},{5,9},{6,10},{7,11},{8,20},{9,21... | collective-permute-start | bytes 491528 | tf_op jit(solution)/shard_map/ppermute | solution.py:283
  20.1 19.6 %collective-permute-start.5 = (bf16[64,1280]{1,0:T(8,128)(2,1)}, bf16[64,1280]{1,0:T(8,128)(2,1)}, u32[]{:S(2)}, u32[]{:S(2)}) collective-permute-start(bf16[64,1280]{1,0:T(8,128)(2,1)} %get-tuple-element.44), channel_id=1, source_target_pairs={{0,13},{1,12},{2,15},{3,14},{4,9},{5,8},{6,11},{7,10},{8,21},{9,20... | collective-permute-start | bytes 491528 | tf_op jit(solution)/shard_map/ppermute | solution.py:283
  22.6 17.0 %collective-permute-start.6 = (bf16[64,1280]{1,0:T(8,128)(2,1)}, bf16[64,1280]{1,0:T(8,128)(2,1)}, u32[]{:S(2)}, u32[]{:S(2)}) collective-permute-start(bf16[64,1280]{1,0:T(8,128)(2,1)} %get-tuple-element.45), channel_id=1, source_target_pairs={{0,14},{1,15},{2,12},{3,13},{4,10},{5,11},{6,8},{7,9},{8,22},{9,23... | collective-permute-start | bytes 491528 | tf_op jit(solution)/shard_map/ppermute | solution.py:283
  27.2 16.3 %collective-permute-start.7 = (bf16[64,1280]{1,0:T(8,128)(2,1)}, bf16[64,1280]{1,0:T(8,128)(2,1)}, u32[]{:S(2)}, u32[]{:S(2)}) collective-permute-start(bf16[64,1280]{1,0:T(8,128)(2,1)} %get-tuple-element.46), channel_id=1, source_target_pairs={{0,15},{1,14},{2,13},{3,12},{4,11},{5,10},{6,9},{7,8},{8,23},{9,22... | collective-permute-start | bytes 491528 | tf_op jit(solution)/shard_map/ppermute | solution.py:283
  32.0 19.4 %all-to-all-start.1 = ((bf16[8,64,768]{2,1,0:T(8,128)(2,1)}), bf16[8,64,768]{2,1,0:T(8,128)(2,1)S(1)}, u32[]{:S(2)}, u32[]{:S(2)}) async-start(bf16[8,64,768]{2,1,0:T(8,128)(2,1)} %shard_map.82), calls=%async_computation.1 | async-start | bytes 1572864 | tf_op jit(solution)/shard_map/all_to_all | solution.py:268
  36.6 20.6 %collective-permute-start.8 = (bf16[2,64,1280]{2,1,0:T(8,128)(2,1)}, bf16[2,64,1280]{2,1,0:T(8,128)(2,1)S(1)}, u32[]{:S(2)}, u32[]{:S(2)}) collective-permute-start(bf16[2,64,1280]{2,1,0:T(8,128)(2,1)} %slice.39), channel_id=1, source_target_pairs={{0,16},{1,17},{2,18},{3,19},{4,20},{5,21},{6,22},{7,23},{8,24},{9,... | collective-permute-start | bytes 983048 | tf_op jit(solution)/shard_map/ppermute | solution.py:283
  58.9 6.3 %collective-permute-start.10 = (bf16[64,640]{1,0:T(8,128)(2,1)S(1)}, bf16[64,640]{1,0:T(8,128)(2,1)S(1)}, u32[]{:S(2)}, u32[]{:S(2)}) collective-permute-start(bf16[64,640]{1,0:T(8,128)(2,1)S(1)} %get-tuple-element.50), channel_id=1, source_target_pairs={{0,5},{1,4},{2,7},{3,6},{4,1},{5,0},{6,3},{7,2},{8,13},{9,12},{10,... | collective-permute-start | bytes 245768 | tf_op jit(solution)/shard_map/ppermute | solution.py:283
  60.4 4.7 %collective-permute-start.11 = (bf16[64,640]{1,0:T(8,128)(2,1)S(1)}, bf16[64,640]{1,0:T(8,128)(2,1)S(1)}, u32[]{:S(2)}, u32[]{:S(2)}) collective-permute-start(bf16[64,640]{1,0:T(8,128)(2,1)S(1)} %get-tuple-element.51), channel_id=1, source_target_pairs={{0,6},{1,7},{2,4},{3,5},{4,2},{5,3},{6,0},{7,1},{8,14},{9,15},{10,... | collective-permute-start | bytes 245768 | tf_op jit(solution)/shard_map/ppermute | solution.py:283
  61.2 5.8 %collective-permute-start.12 = (bf16[64,640]{1,0:T(8,128)(2,1)S(1)}, bf16[64,640]{1,0:T(8,128)(2,1)S(1)}, u32[]{:S(2)}, u32[]{:S(2)}) collective-permute-start(bf16[64,640]{1,0:T(8,128)(2,1)S(1)} %get-tuple-element.52), channel_id=1, source_target_pairs={{0,7},{1,6},{2,5},{3,4},{4,3},{5,2},{6,1},{7,0},{8,15},{9,14},{10,... | collective-permute-start | bytes 245768 | tf_op jit(solution)/shard_map/ppermute | solution.py:283
  62.0 6.9 %collective-permute-start.13 = (bf16[64,640]{1,0:T(8,128)(2,1)S(1)}, bf16[64,640]{1,0:T(8,128)(2,1)S(1)}, u32[]{:S(2)}, u32[]{:S(2)}) collective-permute-start(bf16[64,640]{1,0:T(8,128)(2,1)S(1)} %get-tuple-element.53), channel_id=1, source_target_pairs={{0,1},{1,0},{2,3},{3,2},{4,5},{5,4},{6,7},{7,6},{8,9},{9,8},{10,11... | collective-permute-start | bytes 245768 | tf_op jit(solution)/shard_map/ppermute | solution.py:283
  63.6 6.0 %collective-permute-start.14 = (bf16[64,640]{1,0:T(8,128)(2,1)S(1)}, bf16[64,640]{1,0:T(8,128)(2,1)S(1)}, u32[]{:S(2)}, u32[]{:S(2)}) collective-permute-start(bf16[64,640]{1,0:T(8,128)(2,1)S(1)} %get-tuple-element.54), channel_id=1, source_target_pairs={{0,3},{1,2},{2,1},{3,0},{4,7},{5,6},{6,5},{7,4},{8,11},{9,10},{10,... | collective-permute-start | bytes 245768 | tf_op jit(solution)/shard_map/ppermute | solution.py:283
  65.1 4.5 %collective-permute-start.15 = (bf16[64,640]{1,0:T(8,128)(2,1)S(1)}, bf16[64,640]{1,0:T(8,128)(2,1)S(1)}, u32[]{:S(2)}, u32[]{:S(2)}) collective-permute-start(bf16[64,640]{1,0:T(8,128)(2,1)S(1)} %get-tuple-element.55), channel_id=1, source_target_pairs={{0,2},{1,3},{2,0},{3,1},{4,6},{5,7},{6,4},{7,5},{8,10},{9,11},{10,... | collective-permute-start | bytes 245768 | tf_op jit(solution)/shard_map/ppermute | solution.py:283
  65.2 4.5 %collective-permute-start.9 = (bf16[64,640]{1,0:T(8,128)(2,1)S(1)}, bf16[64,640]{1,0:T(8,128)(2,1)S(1)}, u32[]{:S(2)}, u32[]{:S(2)}) collective-permute-start(bf16[64,640]{1,0:T(8,128)(2,1)S(1)} %get-tuple-element.49), channel_id=1, source_target_pairs={{0,4},{1,5},{2,6},{3,7},{4,0},{5,1},{6,2},{7,3},{8,12},{9,13},{10,... | collective-permute-start | bytes 245768 | tf_op jit(solution)/shard_map/ppermute | solution.py:283

commit v5 on v4

--- a/solution.py
+++ b/solution.py
@@ -18,6 +18,7 @@
 
 NEG_BIG = -1e30
 FACT_ROWS = 8
+STRAIGHT = 3
 
 VMEM = pl.BlockSpec(memory_space=pltpu.VMEM)
 SMEM = pl.BlockSpec(memory_space=pltpu.SMEM)
@@ -53,10 +54,13 @@
     members = group * tiles
 
     def body(k_ref, v_ref, own, *outs):
+        cut = STRAIGHT * HD
         for n in range(members):
-            lanes = pl.ds(n * width, width)
-            own[n, :, :width] = k_ref[:, lanes]
-            own[n, :, width:] = v_ref[:, lanes]
+            first, last = n * width, (n + 1) * width
+            own[n, :, :cut] = k_ref[:, first : first + cut]
+            own[n, :, cut : 2 * cut] = v_ref[:, first : first + cut]
+            own[n, :, 2 * cut : width + cut] = k_ref[:, first + cut : last]
+            own[n, :, width + cut :] = v_ref[:, first + cut : last]
         member = here(group, tiles)
         for m, out in enumerate(outs):
             out[...] = own[partner(member, m, members)]
@@ -71,12 +75,36 @@
     )(own_k, own_v)
 
 
+def pick_tail(blocks, group, tiles):
+    members = len(blocks)
+    needed = first_needed(2, group) * tiles
+    cut = 2 * STRAIGHT * HD
+
+    def body(*refs):
+        member = here(group, tiles)
+        for m, ref in enumerate(refs[:-1]):
+            place = sender(member, m, members) - needed
+
+            @pl.when(place >= 0)
+            def _():
+                refs[-1][place] = ref[:, cut:]
+
+    tokens, width = blocks[0].shape
+    return pl.pallas_call(
+        body,
+        out_shape=jax.ShapeDtypeStruct((members - needed, tokens, width - cut), jnp.bfloat16),
+        in_specs=[VMEM] * members,
+        out_specs=VMEM,
+        compiler_params=pltpu.CompilerParams(vmem_limit_bytes=16 * 1024 * 1024),
+    )(*blocks)
+
+
 def pack_queries(history, frame_index, step_index, own_q, members):
     tokens, channels = own_q.shape
     width = channels // members
 
-    def body(history_ref, index_ref, step_ref, q_ref, out):
-        row = lax.broadcasted_iota(jnp.int32, (tokens, HD), 0)
+    def body(history_ref, index_ref, step_ref, q_ref, out, fact_ref):
+        row = lax.broadcasted_iota(jnp.int32, fact_ref.shape, 0)
         block = jnp.where(row == WIN, step_ref[0], 0)
         for d in range(1, WIN + 1):
             usable = (
@@ -85,16 +113,18 @@
                 & (d <= lax.axis_index("frame"))
             )
             block = jnp.where(row == d - 1, usable.astype(jnp.int32), block)
-        block = block.astype(jnp.float32).astype(jnp.bfloat16)
+        fact_ref[...] = block.astype(jnp.float32)
         for n in range(members):
-            out[n, :, :width] = q_ref[:, n * width : (n + 1) * width]
-            out[n, :, width:] = block
-
-    return pl.pallas_call(
-        body,
-        out_shape=jax.ShapeDtypeStruct((members, tokens, width + HD), jnp.bfloat16),
+            out[n] = q_ref[:, n * width : (n + 1) * width]
+
+    return pl.pallas_call(
+        body,
+        out_shape=[
+            jax.ShapeDtypeStruct((members, tokens, width), jnp.bfloat16),
+            jax.ShapeDtypeStruct((FACT_ROWS, HD), jnp.float32),
+        ],
         in_specs=[SMEM] * 3 + [VMEM],
-        out_specs=VMEM,
+        out_specs=[VMEM] * 2,
     )(history, frame_index, step_index, own_q)
 
 
@@ -120,9 +150,8 @@
 FACTOR = math.log2(math.e) / math.sqrt(HD)
 
 
-def frame_facts(asked_ref, row, frame_tok):
-    facts = asked_ref[row, :16, asked_ref.shape[-1] - HD :].astype(jnp.float32)
-    past = (facts[:FACT_ROWS] - 1.0) * -NEG_BIG
+def frame_facts(facts, frame_tok):
+    past = (facts - 1.0) * -NEG_BIG
     past = [past[d : d + 1] for d in range(WIN) for _ in range(frame_tok // HD)]
     return jnp.concatenate(past, axis=1), facts[WIN : WIN + 1]
 
@@ -132,6 +161,12 @@
     for s in range(STEPS):
         gain = jnp.where(step == s, gain_ref[s, h], gain)
     return gain
+
+
+def kv_lanes(h, heads, straight=STRAIGHT):
+    if h < straight:
+        return h * HD, (straight + h) * HD
+    return (straight + h) * HD, (heads + h) * HD
 
 
 def rows_of(ref, row, tiles, lane):
@@ -158,22 +193,30 @@
     )
 
 
-def put_frame(out_ref, j, group, gain_ref, bias_ref, asked_ref, team_ref, before_ref, far_refs):
+def put_frame(
+    out_ref, j, group, gain_ref, bias_ref, fact_ref, asked_ref, team_ref, before_ref, far_refs
+):
     members, tokens, width = out_ref.shape
     tiles = members // group
     frame_tok = tiles * tokens
-    past, step = frame_facts(asked_ref, j * tiles, frame_tok)
+    past, step = frame_facts(fact_ref[j], frame_tok)
     frames = []
     for d in range(WIN + 1):
         hop = max(0, -((j - d) // group))
-        ref = (team_ref, before_ref, *far_refs)[hop]
         skipped = first_needed(hop, group) if hop > 1 else 0
-        frames.append((ref, (j - d + hop * group - skipped) * tiles))
+        frames.append((hop, (j - d + hop * group - skipped) * tiles))
     for h in range(width // HD):
         lane = h * HD
         q = rows_of(asked_ref, j * tiles, tiles, lane)
-        k = jnp.concatenate([rows_of(r, row, tiles, lane) for r, row in frames])
-        v = jnp.concatenate([rows_of(r, row, tiles, width + lane) for r, row in frames])
+        straight = h < STRAIGHT
+        refs = [team_ref, before_ref, *far_refs[int(not straight) :: 2]]
+        shift = 0 if straight else 2 * STRAIGHT * HD
+        k, v = (
+            jnp.concatenate(
+                [rows_of(refs[hop], row, tiles, at - shift * (hop > 1)) for hop, row in frames]
+            )
+            for at in kv_lanes(h, width // HD)
+        )
         scores = scores_of(q, k)
         scores = jnp.concatenate(
             [scores[:, :frame_tok] + bias_ref[h], scores[:, frame_tok:] + past], axis=1
@@ -186,42 +229,58 @@
         )
 
 
-def attend_near(asked, team, ahead, bias, gains, group):
+def attend_near(facts, asked, team, ahead, bias, gains, group):
     members, tokens = team.shape[:2]
     width = team.shape[-1] // 2
 
+    tiles = members // group
+
     def body(gain_ref, bias_ref, asked_ref, team_ref, *refs):
-        out_ref, before_ref = refs[members:]
-        member = here(group, members // group)
+        out_ref, before_ref, fact_ref = refs[members + group :]
+        member = here(group, tiles)
         for m, ref in enumerate(refs[:members]):
             before_ref[sender(member, m, members)] = ref[...]
+        for i, ref in enumerate(refs[members : members + group]):
+            fact_ref[lax.div(sender(member, i * tiles, members), tiles)] = ref[...]
         for j in range(min(group, max(0, WIN - group)), group):
-            put_frame(out_ref, j, group, gain_ref, bias_ref, asked_ref, team_ref, before_ref, [])
+            put_frame(
+                out_ref, j, group, gain_ref, bias_ref, fact_ref, asked_ref, team_ref, before_ref, []
+            )
 
     return pl.pallas_call(
         body,
         out_shape=[
             jax.ShapeDtypeStruct((members, tokens, width), jnp.bfloat16),
             jax.ShapeDtypeStruct(team.shape, jnp.bfloat16),
+            jax.ShapeDtypeStruct((group,) + facts[0].shape, jnp.float32),
         ],
-        in_specs=[SMEM] + [VMEM] * (3 + members),
-        out_specs=[VMEM] * 2,
+        in_specs=[SMEM] + [VMEM] * (3 + members + group),
+        out_specs=[VMEM] * 3,
         cost_estimate=cost(group * width // HD * (WIN + 1), members // group * tokens),
         compiler_params=pltpu.CompilerParams(vmem_limit_bytes=48 * 1024 * 1024),
-    )(gains, bias, asked, team, *ahead)
-
-
-def attend_far(asked, team, before, far, near, bias, gains, group):
+    )(gains, bias, asked, team, *ahead, *facts)
+
+
+def attend_far(facts, asked, team, before, far, near, bias, gains, group):
     members, tokens, width = near.shape
     finished = min(group, max(0, WIN - group)) * members // group
 
-    def body(gain_ref, bias_ref, asked_ref, team_ref, before_ref, near_ref, *refs):
+    def body(gain_ref, bias_ref, fact_ref, asked_ref, team_ref, before_ref, near_ref, *refs):
         far_refs, outs, all_ref = refs[: len(far)], refs[len(far) : -1], refs[-1]
         if finished < members:
             all_ref[finished:] = near_ref[finished:]
         for j in range(finished * group // members):
             put_frame(
-                all_ref, j, group, gain_ref, bias_ref, asked_ref, team_ref, before_ref, far_refs
+                all_ref,
+                j,
+                group,
+                gain_ref,
+                bias_ref,
+                fact_ref,
+                asked_ref,
+                team_ref,
+                before_ref,
+                far_refs,
             )
         member = here(group, members // group)
         for m, out in enumerate(outs):
@@ -230,12 +289,12 @@
     return pl.pallas_call(
         body,
         out_shape=[jax.ShapeDtypeStruct((tokens, width), near.dtype)] * members,
-        in_specs=[SMEM] + [VMEM] * (5 + len(far)),
+        in_specs=[SMEM] + [VMEM] * (6 + len(far)),
         out_specs=[VMEM] * members,
         scratch_shapes=[pltpu.VMEM(near.shape, near.dtype)],
         cost_estimate=cost(width // HD * (WIN + 1), members // group * tokens),
         compiler_params=pltpu.CompilerParams(vmem_limit_bytes=48 * 1024 * 1024),
-    )(gains, bias, asked, team, before, near, *far)
+    )(gains, bias, facts, asked, team, before, near, *far)
 
 
 def window_bias(mask_rows, tile_count):
@@ -274,10 +333,10 @@
             tiled=True,
         )
 
-    def team_permute(block, ahead, m):
+    def team_permute(block, ahead, m, around=True):
         route = [
             (t * members + n, (t + ahead) % teams * members + partner(n, m, members))
-            for t in range(teams)
+            for t in range(teams if around else teams - ahead)
             for n in range(members)
         ]
         return lax.ppermute(block, both, route)
@@ -292,23 +351,29 @@
     team, *some = lax.optimization_barrier((team, *[ahead[m] for m in [0, 2, 1, 3]]))
     for m, block in zip([0, 2, 1, 3], some):
         ahead[m] = block
-    far = [
-        team_permute(team[first_needed(hop, group) * tile_count :], hop, 0)
-        for hop in range(2, hops + 1)
-    ]
-    asked = pack_queries(history_mask, frame_index, step_index, queries[0, 0], members)
+    far, first = [], first_needed(2, group)
+    for hop in range(2, hops + 1):
+        needed = first_needed(hop, group)
+        tail = team[needed * tile_count :, :, : 2 * STRAIGHT * HD]
+        block = far[-1][(needed - first) * tile_count :] if far else pick_tail(ahead, group, tile_count)
+        far += [team_permute(tail, hop, 0, False), team_permute(block, 1, 0, True)]
+        first = needed
+    asked, fact = pack_queries(history_mask, frame_index, step_index, queries[0, 0], members)
     asked, *some = lax.optimization_barrier((asked, *[ahead[m] for m in [1]]))
     for m, block in zip([1], some):
         ahead[m] = block
     asked = exchange(asked)
+    fact, ahead[6] = lax.optimization_barrier((fact, ahead[6]))
+    facts = [fact] + [team_permute(fact, 0, i * tile_count) for i in range(1, group)]
 
     share = here(group, tile_count) * head_share
     gains = lax.dynamic_slice(step_gain, (0, share), (STEPS, head_share))
     my_mask = lax.dynamic_slice(window_mask, (share, 0), (head_share, 9))
     bias = window_bias(my_mask, tile_count)
-    near, before = attend_near(asked, team, ahead, bias, gains, group)
-    out = attend_far(asked, team, before, far, near, bias, gains, group)
-    order = [4, 5, 6, 7, 1, 3, 2, 0]
+    team, far[0] = lax.optimization_barrier((team, far[0]))
+    near, before, facts = attend_near(facts, asked, team, ahead, bias, gains, group)
+    out = attend_far(facts, asked, team, before, far, near, bias, gains, group)
+    order = [5, 4, 7, 6, 1, 3, 2, 0]
     back = {m: team_permute(out[m], 0, m) if m else out[m] for m in order}
     return unpack(back, group, tile_count, order)[None, None]
 

time: 71.1 us -> 69.3 us (0.975)
  waiting for transfers between devices: 26.3 us -> 14.5 us
  starting transfers between devices: 30.2 us -> 39.2 us
  Pallas kernels: 11.1 us -> 12.9 us
  local copies, waits for them, and re-layouts: 0.85 us -> 0.12 us
    ppermute x16 -> x20, starting transfers between devices: 21.3 us -> 30.3 us  [team_permute(): return lax.ppermute(block, both, route)]
    all_to_all x2, waiting for transfers between devices: 10.5 us -> 2.71 us  [exchange(): lax.all_to_all(block, both, 0, 0, axis_index_groups=[[t * members + n for...]
    ppermute x16 -> x20, waiting for transfers between devices: 15.7 us -> 11.8 us  [team_permute(): return lax.ppermute(block, both, route)]
    pallas_call x1 -> x2, Pallas kernels: 2.06 us -> 3.64 us  [the longest x1 1.99 us: pack_queries(): pl.pallas_call(body, out_shape=[jax.ShapeDtypeStruct((members, tokens, wi...]
    slice x1, local copies, waits for them, and re-layouts: 0.75 us -> 0.01 us  [shards(): tail = team[needed * tile_count:, :, :2 * STRAIGHT * HD]]
  transfers between devices with their start and end apart: 18 -> 22, of which waited for: 10 -> 10; matrix products, arithmetic and copies ran while one was open for 2% -> 1% of each run, Pallas kernels for 8% -> 10%
where the time goes in v5:
time: 69.3 us; the launch traced here: 68.9 us
  starting transfers between devices  39.2 us (57%)
  waiting for transfers between devices  14.5 us (21%)
  Pallas kernels  12.9 us (19%)
  between operations  1.45 us (2%)
  other arithmetic  0.72 us (1%)
    ppermute x20, starting transfers between devices, team_permute(): return lax.ppermute(block, both, route)  30.3 us
    ppermute x20, waiting for transfers between devices, team_permute(): return lax.ppermute(block, both, route)  11.8 us
    all_to_all x2, starting transfers between devices, exchange(): lax.all_to_all(block, both, 0, 0, axis_index_groups=[[t * members + n for...  8.86 us
    pallas_call x1, Pallas kernels, attend_near(): pl.pallas_call(body, out_shape=[jax.ShapeDtypeStruct((members, tokens, wi...  3.43 us
    pallas_call x1, Pallas kernels, pack_kv(): pl.pallas_call(body, out_shape=[jax.ShapeDtypeStruct((members,) + shape,...  2.88 us
    all_to_all x2, waiting for transfers between devices, exchange(): lax.all_to_all(block, both, 0, 0, axis_index_groups=[[t * members + n for...  2.71 us
    pallas_call x1, Pallas kernels, attend_far(): pl.pallas_call(body, out_shape=[jax.ShapeDtypeStruct((tokens, width), nea...  2.08 us
    pallas_call x1, Pallas kernels, pack_queries(): pl.pallas_call(body, out_shape=[jax.ShapeDtypeStruct((members, tokens, wi...  1.99 us
  transfers between devices with their start and end apart: 22, of which 10 were waited for; matrix products, arithmetic and copies ran while one was open for 1% of the time, Pallas kernels for 10%

profile of v5, /device:TPU:0, one launch (start us, length us, event | category | flops | bytes accessed | tf_op | source)
XLA Modules:
  0.0 68.9 jit_solution(11634479325290017624)
XLA Ops:
  0.0 2.9 %shard_map.83 = (bf16[8,64,1280]{2,1,0:T(8,128)(2,1)}, bf16[64,1280]{1,0:T(8,128)(2,1)}, bf16[64,1280]{1,0:T(8,128)(2,1)}, bf16[64,1280]{1,0:T(8,128)(2,1)}, bf1...) custom-call(bf16[64,5120]{1,0:T(8,128)(2,1)} %bitcast.22, ...), custom_call_target="tpu_custom_call" | custom-call | tf_op jit(solution)/shard_map/pallas_call | solution.py:69
  2.9 5.3 %all-to-all-start = ((bf16[8,64,1280]{2,1,0:T(8,128)(2,1)}), bf16[8,64,1280]{2,1,0:T(8,128)(2,1)S(1)}, u32[]{:S(2)}, u32[]{:S(2)}) async-start(bf16[8,64,1280]{2,1,0:T(8,128)(2,1)} %get-tuple-element.39), calls=%async_computation | async-start | bytes 2621440 | tf_op jit(solution)/shard_map/all_to_all | solution.py:327
  8.2 1.6 %collective-permute-start = (bf16[64,1280]{1,0:T(8,128)(2,1)S(1)}, bf16[64,1280]{1,0:T(8,128)(2,1)S(1)}, u32[]{:S(2)}, u32[]{:S(2)}) collective-permute-start(bf16[64,1280]{1,0:T(8,128)(2,1)S(1)} %copy-done.6), channel_id=1, source_target_pairs={{0,8},{1,9},{2,10},{3,11},{4,12},{5,13},{6,14},{7,15},{8,16},{9,17... | collective-permute-start | bytes 491528 | tf_op jit(solution)/shard_map/ppermute | solution.py:342
  9.9 1.4 %collective-permute-start.1 = (bf16[64,1280]{1,0:T(8,128)(2,1)S(1)}, bf16[64,1280]{1,0:T(8,128)(2,1)S(1)}, u32[]{:S(2)}, u32[]{:S(2)}) collective-permute-start(bf16[64,1280]{1,0:T(8,128)(2,1)S(1)} %copy-done.5), channel_id=1, source_target_pairs={{0,10},{1,11},{2,8},{3,9},{4,14},{5,15},{6,12},{7,13},{8,18},{9,19... | collective-permute-start | bytes 491528 | tf_op jit(solution)/shard_map/ppermute | solution.py:342
  11.2 2.7 %collective-permute-start.2 = (bf16[64,1280]{1,0:T(8,128)(2,1)S(1)}, bf16[64,1280]{1,0:T(8,128)(2,1)S(1)}, u32[]{:S(2)}, u32[]{:S(2)}) collective-permute-start(bf16[64,1280]{1,0:T(8,128)(2,1)S(1)} %copy-done.4), channel_id=1, source_target_pairs={{0,9},{1,8},{2,11},{3,10},{4,13},{5,12},{6,15},{7,14},{8,17},{9,16... | collective-permute-start | bytes 491528 | tf_op jit(solution)/shard_map/ppermute | solution.py:342
  14.2 2.4 %collective-permute-start.5 = (bf16[64,1280]{1,0:T(8,128)(2,1)}, bf16[64,1280]{1,0:T(8,128)(2,1)S(1)}, u32[]{:S(2)}, u32[]{:S(2)}) collective-permute-start(bf16[64,1280]{1,0:T(8,128)(2,1)} %get-tuple-element.52), channel_id=1, source_target_pairs={{0,12},{1,13},{2,14},{3,15},{4,8},{5,9},{6,10},{7,11},{8,20},{9,21... | collective-permute-start | bytes 491528 | tf_op jit(solution)/shard_map/ppermute | solution.py:342
  17.9 2.0 %shard_map.82 = (bf16[8,64,640]{2,1,0:T(8,128)(2,1)}, f32[8,128]{1,0:T(8,128)}) custom-call(s32[1,5]{1,0:T(1,128)} %history_ref.1, s32[1]{0:T(128)S(6)} %copy.10.index_ref, s32[1]{0:T(128)S(6)} %copy.9.step_ref, bf16[64,5120]{1,0:T(8,128)(2,1)} %bitcast.24), custom_call_target="tpu_custom_call" | custom-call | tf_op jit(solution)/shard_map/pallas_call | solution.py:120
  20.0 2.5 %collective-permute-start.6 = (bf16[64,1280]{1,0:T(8,128)(2,1)}, bf16[64,1280]{1,0:T(8,128)(2,1)S(1)}, u32[]{:S(2)}, u32[]{:S(2)}) collective-permute-start(bf16[64,1280]{1,0:T(8,128)(2,1)} %get-tuple-element.53), channel_id=1, source_target_pairs={{0,13},{1,12},{2,15},{3,14},{4,9},{5,8},{6,11},{7,10},{8,21},{9,20... | collective-permute-start | bytes 491528 | tf_op jit(solution)/shard_map/ppermute | solution.py:342
  22.5 1.7 %collective-permute-start.7 = (bf16[64,1280]{1,0:T(8,128)(2,1)}, bf16[64,1280]{1,0:T(8,128)(2,1)}, u32[]{:S(2)}, u32[]{:S(2)}) collective-permute-start(bf16[64,1280]{1,0:T(8,128)(2,1)} %get-tuple-element.55), channel_id=1, source_target_pairs={{0,14},{1,15},{2,12},{3,13},{4,10},{5,11},{6,8},{7,9},{8,22},{9,23... | collective-permute-start | bytes 491528 | tf_op jit(solution)/shard_map/ppermute | solution.py:342
  24.2 3.1 %collective-permute-done.2.refs_1_ = bf16[64,1280]{1,0:T(8,128)(2,1)S(1)} collective-permute-done((bf16[64,1280]{1,0:T(8,128)(2,1)S(1)}, bf16[64,1280]{1,0:T(8,128)(2,1)S(1)}, u32[]{:S(2)}, u32[]{:S(2)}) %collective-permute-start.2) | collective-permute-done | bytes 163872 | tf_op jit(solution)/shard_map/ppermute | solution.py:342
  27.3 2.1 %collective-permute-done.3.refs_3_ = bf16[64,1280]{1,0:T(8,128)(2,1)S(1)} collective-permute-done((bf16[64,1280]{1,0:T(8,128)(2,1)S(1)}, bf16[64,1280]{1,0:T(8,128)(2,1)S(1)}, u32[]{:S(2)}, u32[]{:S(2)}) %collective-permute-start.3) | collective-permute-done | bytes 163872 | tf_op jit(solution)/shard_map/ppermute | solution.py:342
  29.3 2.7 %all-to-all-done.team_ref = bf16[8,64,1280]{2,1,0:T(8,128)(2,1)S(1)} async-done(((bf16[8,64,1280]{2,1,0:T(8,128)(2,1)}), bf16[8,64,1280]{2,1,0:T(8,128)(2,1)S(1)}, u32[]{:S(2)}, u32[]{:S(2)}) %all-to-all-start) | async-done | bytes 1310752 | tf_op jit(solution)/shard_map/all_to_all | solution.py:327
  32.0 3.5 %all-to-all-start.1 = ((bf16[8,64,640]{2,1,0:T(8,128)(2,1)}), bf16[8,64,640]{2,1,0:T(8,128)(2,1)S(1)}, u32[]{:S(2)}, u32[]{:S(2)}) async-start(bf16[8,64,640]{2,1,0:T(8,128)(2,1)} %get-tuple-element.45), calls=%async_computation.1 | async-start | bytes 1310720 | tf_op jit(solution)/shard_map/all_to_all | solution.py:327
  35.8 4.5 %collective-permute-start.4 = (bf16[2,64,768]{2,1,0:T(8,128)(2,1)S(1)}, bf16[2,64,768]{2,1,0:T(8,128)(2,1)S(1)}, u32[]{:S(2)}, u32[]{:S(2)}) collective-permute-start(bf16[2,64,768]{2,1,0:T(8,128)(2,1)S(1)} %slice.39), channel_id=1, source_target_pairs={{0,16},{1,17},{2,18},{3,19},{4,20},{5,21},{6,22},{7,23},{8,24},{9,... | collective-permute-start | bytes 589832 | tf_op jit(solution)/shard_map/ppermute | solution.py:342
  41.1 2.0 %collective-permute-start.10 = (f32[8,128]{1,0:T(8,128)S(1)}, f32[8,128]{1,0:T(8,128)S(1)}, u32[]{:S(2)}, u32[]{:S(2)}) collective-permute-start(f32[8,128]{1,0:T(8,128)S(1)} %copy-done.1), channel_id=1, source_target_pairs={{0,4},{1,5},{2,6},{3,7},{4,0},{5,1},{6,2},{7,3},{8,12},{9,13},{10,... | collective-permute-start | bytes 12296 | tf_op jit(solution)/shard_map/ppermute | solution.py:342
  43.6 1.7 %shard_map.85 = bf16[2,64,512]{2,1,0:T(8,128)(2,1)} custom-call(bf16[64,1280]{1,0:T(8,128)(2,1)S(1)} %collective-permute-done.refs_0_, bf16[64,1280]{1,0:T(8,128)(2,1)S(1)} %collective-permute-done.2.refs_1_, bf16[64,1280]{1,0:T(8,128)(2,1)S(1)} %collective-permute-done.1.refs_2_, bf16[64,1280]{1,0:T(8,128)(2,1)S(1)} %collective-permute-done.3.refs_3_, ...), custom_call_target="tpu_custom_call" | custom-call | tf_op jit(solution)/shard_map/pallas_call | solution.py:93
  45.2 4.4 %collective-permute-start.12 = (bf16[2,64,512]{2,1,0:T(8,128)(2,1)}, bf16[2,64,512]{2,1,0:T(8,128)(2,1)}, u32[]{:S(2)}, u32[]{:S(2)}) collective-permute-start(bf16[2,64,512]{2,1,0:T(8,128)(2,1)} %shard_map.85), channel_id=1, source_target_pairs={{0,8},{1,9},{2,10},{3,11},{4,12},{5,13},{6,14},{7,15},{8,16},{9,17... | collective-permute-start | bytes 393224 | tf_op jit(solution)/shard_map/ppermute | solution.py:342
  50.1 3.4 %shard_map.84 = (bf16[8,64,640]{2,1,0:T(8,128)(2,1)S(1)}, bf16[8,64,1280]{2,1,0:T(8,128)(2,1)S(1)}, f32[4,8,128]{2,1,0:T(8,128)S(1)}) custom-call(f32[4,5]{1,0:T(4,128)S(1)} %constant_dynamic-slice_fusion.gain_ref, f32[5,128,128]{2,1,0:T(8,128)S(1)} %or_select_fusion.bias_ref, bf16[8,64,640]{2,1,0:T(8,128)(2,1)S(1)} %all-to-all-done.1.asked_ref, ...), custom_call_target="tpu_custom_call" | custom-call | flops 1006632960 | bytes 7864320 | tf_op jit(solution)/shard_map/pallas_call | solution.py:250
  53.5 2.1 %shard_map.86 = (bf16[64,640]{1,0:T(8,128)(2,1)S(1)}, bf16[64,640]{1,0:T(8,128)(2,1)S(1)}, bf16[64,640]{1,0:T(8,128)(2,1)S(1)}, bf16[64,640]{1,0:T(8,128)(2,1)S(...) custom-call(f32[4,5]{1,0:T(4,128)S(1)} %constant_dynamic-slice_fusio, ...), custom_call_target="tpu_custom_call" | custom-call | flops 251658240 | bytes 1966080 | tf_op jit(solution)/shard_map/pallas_call | solution.py:289
  55.6 2.7 %collective-permute-start.13 = (bf16[64,640]{1,0:T(8,128)(2,1)S(1)}, bf16[64,640]{1,0:T(8,128)(2,1)S(1)}, u32[]{:S(2)}, u32[]{:S(2)}) collective-permute-start(bf16[64,640]{1,0:T(8,128)(2,1)S(1)} %get-tuple-element.63), channel_id=1, source_target_pairs={{0,5},{1,4},{2,7},{3,6},{4,1},{5,0},{6,3},{7,2},{8,13},{9,12},{10,... | collective-permute-start | bytes 245768 | tf_op jit(solution)/shard_map/ppermute | solution.py:342
  60.4 1.7 %collective-permute-start.17 = (bf16[64,640]{1,0:T(8,128)(2,1)S(1)}, bf16[64,640]{1,0:T(8,128)(2,1)S(1)}, u32[]{:S(2)}, u32[]{:S(2)}) collective-permute-start(bf16[64,640]{1,0:T(8,128)(2,1)S(1)} %get-tuple-element.67), channel_id=1, source_target_pairs={{0,1},{1,0},{2,3},{3,2},{4,5},{5,4},{6,7},{7,6},{8,9},{9,8},{10,11... | collective-permute-start | bytes 245768 | tf_op jit(solution)/shard_map/ppermute | solution.py:342
  62.0 1.6 %collective-permute-done.14.refs_1_ = bf16[64,640]{1,0:T(8,128)(2,1)S(1)} collective-permute-done((bf16[64,640]{1,0:T(8,128)(2,1)S(1)}, bf16[64,640]{1,0:T(8,128)(2,1)S(1)}, u32[]{:S(2)}, u32[]{:S(2)}) %collective-permute-start.14) | collective-permute-done | bytes 81952 | tf_op jit(solution)/shard_map/ppermute | solution.py:342
  64.6 1.3 %collective-permute-done.16.refs_3_ = bf16[64,640]{1,0:T(8,128)(2,1)S(1)} collective-permute-done((bf16[64,640]{1,0:T(8,128)(2,1)S(1)}, bf16[64,640]{1,0:T(8,128)(2,1)S(1)}, u32[]{:S(2)}, u32[]{:S(2)}) %collective-permute-start.16) | collective-permute-done | bytes 81952 | tf_op jit(solution)/shard_map/ppermute | solution.py:342
  66.4 1.6 %collective-permute-done.18.refs_5_ = bf16[64,640]{1,0:T(8,128)(2,1)S(1)} collective-permute-done((bf16[64,640]{1,0:T(8,128)(2,1)S(1)}, bf16[64,640]{1,0:T(8,128)(2,1)S(1)}, u32[]{:S(2)}, u32[]{:S(2)}) %collective-permute-start.18) | collective-permute-done | bytes 81952 | tf_op jit(solution)/shard_map/ppermute | solution.py:342
  (46 shorter events, 6.8 us)
Async XLA Ops:
  0.0 49.6 %copy-start = (f32[4,40]{1,0:T(4,128)S(1)}, f32[4,40]{1,0:T(4,128)}, u32[]{:S(2)}) copy-start(f32[4,40]{1,0:T(4,128)} %param.15) | copy-start | bytes 1924
  2.9 29.1 %all-to-all-start = ((bf16[8,64,1280]{2,1,0:T(8,128)(2,1)}), bf16[8,64,1280]{2,1,0:T(8,128)(2,1)S(1)}, u32[]{:S(2)}, u32[]{:S(2)}) async-start(bf16[8,64,1280]{2,1,0:T(8,128)(2,1)} %get-tuple-element.39), calls=%async_computation | async-start | bytes 2621440 | tf_op jit(solution)/shard_map/all_to_all | solution.py:327
  8.2 11.8 %collective-permute-start = (bf16[64,1280]{1,0:T(8,128)(2,1)S(1)}, bf16[64,1280]{1,0:T(8,128)(2,1)S(1)}, u32[]{:S(2)}, u32[]{:S(2)}) collective-permute-start(bf16[64,1280]{1,0:T(8,128)(2,1)S(1)} %copy-done.6), channel_id=1, source_target_pairs={{0,8},{1,9},{2,10},{3,11},{4,12},{5,13},{6,14},{7,15},{8,16},{9,17... | collective-permute-start | bytes 491528 | tf_op jit(solution)/shard_map/ppermute | solution.py:342
  9.9 12.7 %collective-permute-start.1 = (bf16[64,1280]{1,0:T(8,128)(2,1)S(1)}, bf16[64,1280]{1,0:T(8,128)(2,1)S(1)}, u32[]{:S(2)}, u32[]{:S(2)}) collective-permute-start(bf16[64,1280]{1,0:T(8,128)(2,1)S(1)} %copy-done.5), channel_id=1, source_target_pairs={{0,10},{1,11},{2,8},{3,9},{4,14},{5,15},{6,12},{7,13},{8,18},{9,19... | collective-permute-start | bytes 491528 | tf_op jit(solution)/shard_map/ppermute | solution.py:342
  11.2 16.0 %collective-permute-start.2 = (bf16[64,1280]{1,0:T(8,128)(2,1)S(1)}, bf16[64,1280]{1,0:T(8,128)(2,1)S(1)}, u32[]{:S(2)}, u32[]{:S(2)}) collective-permute-start(bf16[64,1280]{1,0:T(8,128)(2,1)S(1)} %copy-done.4), channel_id=1, source_target_pairs={{0,9},{1,8},{2,11},{3,10},{4,13},{5,12},{6,15},{7,14},{8,17},{9,16... | collective-permute-start | bytes 491528 | tf_op jit(solution)/shard_map/ppermute | solution.py:342
  13.9 15.4 %collective-permute-start.3 = (bf16[64,1280]{1,0:T(8,128)(2,1)S(1)}, bf16[64,1280]{1,0:T(8,128)(2,1)S(1)}, u32[]{:S(2)}, u32[]{:S(2)}) collective-permute-start(bf16[64,1280]{1,0:T(8,128)(2,1)S(1)} %copy-done.3), channel_id=1, source_target_pairs={{0,11},{1,10},{2,9},{3,8},{4,15},{5,14},{6,13},{7,12},{8,19},{9,18... | collective-permute-start | bytes 491528 | tf_op jit(solution)/shard_map/ppermute | solution.py:342
  14.2 26.9 %collective-permute-start.5 = (bf16[64,1280]{1,0:T(8,128)(2,1)}, bf16[64,1280]{1,0:T(8,128)(2,1)S(1)}, u32[]{:S(2)}, u32[]{:S(2)}) collective-permute-start(bf16[64,1280]{1,0:T(8,128)(2,1)} %get-tuple-element.52), channel_id=1, source_target_pairs={{0,12},{1,13},{2,14},{3,15},{4,8},{5,9},{6,10},{7,11},{8,20},{9,21... | collective-permute-start | bytes 491528 | tf_op jit(solution)/shard_map/ppermute | solution.py:342
  19.9 20.9 %copy-start.1 = (f32[8,128]{1,0:T(8,128)S(1)}, f32[8,128]{1,0:T(8,128)}, u32[]{:S(2)}) copy-start(f32[8,128]{1,0:T(8,128)} %get-tuple-element.58.refs_8_) | copy-start | bytes 12292
  20.0 23.1 %collective-permute-start.6 = (bf16[64,1280]{1,0:T(8,128)(2,1)}, bf16[64,1280]{1,0:T(8,128)(2,1)S(1)}, u32[]{:S(2)}, u32[]{:S(2)}) collective-permute-start(bf16[64,1280]{1,0:T(8,128)(2,1)} %get-tuple-element.53), channel_id=1, source_target_pairs={{0,13},{1,12},{2,15},{3,14},{4,9},{5,8},{6,11},{7,10},{8,21},{9,20... | collective-permute-start | bytes 491528 | tf_op jit(solution)/shard_map/ppermute | solution.py:342
  22.5 18.2 %collective-permute-start.7 = (bf16[64,1280]{1,0:T(8,128)(2,1)}, bf16[64,1280]{1,0:T(8,128)(2,1)}, u32[]{:S(2)}, u32[]{:S(2)}) collective-permute-start(bf16[64,1280]{1,0:T(8,128)(2,1)} %get-tuple-element.55), channel_id=1, source_target_pairs={{0,14},{1,15},{2,12},{3,13},{4,10},{5,11},{6,8},{7,9},{8,22},{9,23... | collective-permute-start | bytes 491528 | tf_op jit(solution)/shard_map/ppermute | solution.py:342
  27.3 16.3 %collective-permute-start.8 = (bf16[64,1280]{1,0:T(8,128)(2,1)}, bf16[64,1280]{1,0:T(8,128)(2,1)}, u32[]{:S(2)}, u32[]{:S(2)}) collective-permute-start(bf16[64,1280]{1,0:T(8,128)(2,1)} %get-tuple-element.57), channel_id=1, source_target_pairs={{0,15},{1,14},{2,13},{3,12},{4,11},{5,10},{6,9},{7,8},{8,23},{9,22... | collective-permute-start | bytes 491528 | tf_op jit(solution)/shard_map/ppermute | solution.py:342
  32.0 18.1 %all-to-all-start.1 = ((bf16[8,64,640]{2,1,0:T(8,128)(2,1)}), bf16[8,64,640]{2,1,0:T(8,128)(2,1)S(1)}, u32[]{:S(2)}, u32[]{:S(2)}) async-start(bf16[8,64,640]{2,1,0:T(8,128)(2,1)} %get-tuple-element.45), calls=%async_computation.1 | async-start | bytes 1310720 | tf_op jit(solution)/shard_map/all_to_all | solution.py:327
  35.8 13.9 %collective-permute-start.4 = (bf16[2,64,768]{2,1,0:T(8,128)(2,1)S(1)}, bf16[2,64,768]{2,1,0:T(8,128)(2,1)S(1)}, u32[]{:S(2)}, u32[]{:S(2)}) collective-permute-start(bf16[2,64,768]{2,1,0:T(8,128)(2,1)S(1)} %slice.39), channel_id=1, source_target_pairs={{0,16},{1,17},{2,18},{3,19},{4,20},{5,21},{6,22},{7,23},{8,24},{9,... | collective-permute-start | bytes 589832 | tf_op jit(solution)/shard_map/ppermute | solution.py:342
  40.8 8.9 %collective-permute-start.9 = (f32[8,128]{1,0:T(8,128)S(1)}, f32[8,128]{1,0:T(8,128)S(1)}, u32[]{:S(2)}, u32[]{:S(2)}) collective-permute-start(f32[8,128]{1,0:T(8,128)S(1)} %copy-done.1), channel_id=1, source_target_pairs={{0,2},{1,3},{2,0},{3,1},{4,6},{5,7},{6,4},{7,5},{8,10},{9,11},{10,... | collective-permute-start | bytes 12296 | tf_op jit(solution)/shard_map/ppermute | solution.py:342
  41.1 9.0 %collective-permute-start.10 = (f32[8,128]{1,0:T(8,128)S(1)}, f32[8,128]{1,0:T(8,128)S(1)}, u32[]{:S(2)}, u32[]{:S(2)}) collective-permute-start(f32[8,128]{1,0:T(8,128)S(1)} %copy-done.1), channel_id=1, source_target_pairs={{0,4},{1,5},{2,6},{3,7},{4,0},{5,1},{6,2},{7,3},{8,12},{9,13},{10,... | collective-permute-start | bytes 12296 | tf_op jit(solution)/shard_map/ppermute | solution.py:342
  43.1 7.0 %collective-permute-start.11 = (f32[8,128]{1,0:T(8,128)S(1)}, f32[8,128]{1,0:T(8,128)S(1)}, u32[]{:S(2)}, u32[]{:S(2)}) collective-permute-start(f32[8,128]{1,0:T(8,128)S(1)} %copy-done.1), channel_id=1, source_target_pairs={{0,6},{1,7},{2,4},{3,5},{4,2},{5,3},{6,0},{7,1},{8,14},{9,15},{10,... | collective-permute-start | bytes 12296 | tf_op jit(solution)/shard_map/ppermute | solution.py:342
  45.2 8.3 %collective-permute-start.12 = (bf16[2,64,512]{2,1,0:T(8,128)(2,1)}, bf16[2,64,512]{2,1,0:T(8,128)(2,1)}, u32[]{:S(2)}, u32[]{:S(2)}) collective-permute-start(bf16[2,64,512]{2,1,0:T(8,128)(2,1)} %shard_map.85), channel_id=1, source_target_pairs={{0,8},{1,9},{2,10},{3,11},{4,12},{5,13},{6,14},{7,15},{8,16},{9,17... | collective-permute-start | bytes 393224 | tf_op jit(solution)/shard_map/ppermute | solution.py:342
  55.6 6.4 %collective-permute-start.13 = (bf16[64,640]{1,0:T(8,128)(2,1)S(1)}, bf16[64,640]{1,0:T(8,128)(2,1)S(1)}, u32[]{:S(2)}, u32[]{:S(2)}) collective-permute-start(bf16[64,640]{1,0:T(8,128)(2,1)S(1)} %get-tuple-element.63), channel_id=1, source_target_pairs={{0,5},{1,4},{2,7},{3,6},{4,1},{5,0},{6,3},{7,2},{8,13},{9,12},{10,... | collective-permute-start | bytes 245768 | tf_op jit(solution)/shard_map/ppermute | solution.py:342
  58.3 5.3 %collective-permute-start.14 = (bf16[64,640]{1,0:T(8,128)(2,1)S(1)}, bf16[64,640]{1,0:T(8,128)(2,1)S(1)}, u32[]{:S(2)}, u32[]{:S(2)}) collective-permute-start(bf16[64,640]{1,0:T(8,128)(2,1)S(1)} %get-tuple-element.64), channel_id=1, source_target_pairs={{0,4},{1,5},{2,6},{3,7},{4,0},{5,1},{6,2},{7,3},{8,12},{9,13},{10,... | collective-permute-start | bytes 245768 | tf_op jit(solution)/shard_map/ppermute | solution.py:342
  58.8 5.8 %collective-permute-start.15 = (bf16[64,640]{1,0:T(8,128)(2,1)S(1)}, bf16[64,640]{1,0:T(8,128)(2,1)S(1)}, u32[]{:S(2)}, u32[]{:S(2)}) collective-permute-start(bf16[64,640]{1,0:T(8,128)(2,1)S(1)} %get-tuple-element.65), channel_id=1, source_target_pairs={{0,7},{1,6},{2,5},{3,4},{4,3},{5,2},{6,1},{7,0},{8,15},{9,14},{10,... | collective-permute-start | bytes 245768 | tf_op jit(solution)/shard_map/ppermute | solution.py:342
  59.5 6.4 %collective-permute-start.16 = (bf16[64,640]{1,0:T(8,128)(2,1)S(1)}, bf16[64,640]{1,0:T(8,128)(2,1)S(1)}, u32[]{:S(2)}, u32[]{:S(2)}) collective-permute-start(bf16[64,640]{1,0:T(8,128)(2,1)S(1)} %get-tuple-element.66), channel_id=1, source_target_pairs={{0,6},{1,7},{2,4},{3,5},{4,2},{5,3},{6,0},{7,1},{8,14},{9,15},{10,... | collective-permute-start | bytes 245768 | tf_op jit(solution)/shard_map/ppermute | solution.py:342
  60.4 6.0 %collective-permute-start.17 = (bf16[64,640]{1,0:T(8,128)(2,1)S(1)}, bf16[64,640]{1,0:T(8,128)(2,1)S(1)}, u32[]{:S(2)}, u32[]{:S(2)}) collective-permute-start(bf16[64,640]{1,0:T(8,128)(2,1)S(1)} %get-tuple-element.67), channel_id=1, source_target_pairs={{0,1},{1,0},{2,3},{3,2},{4,5},{5,4},{6,7},{7,6},{8,9},{9,8},{10,11... | collective-permute-start | bytes 245768 | tf_op jit(solution)/shard_map/ppermute | solution.py:342
  62.0 6.0 %collective-permute-start.18 = (bf16[64,640]{1,0:T(8,128)(2,1)S(1)}, bf16[64,640]{1,0:T(8,128)(2,1)S(1)}, u32[]{:S(2)}, u32[]{:S(2)}) collective-permute-start(bf16[64,640]{1,0:T(8,128)(2,1)S(1)} %get-tuple-element.68), channel_id=1, source_target_pairs={{0,3},{1,2},{2,1},{3,0},{4,7},{5,6},{6,5},{7,4},{8,11},{9,10},{10,... | collective-permute-start | bytes 245768 | tf_op jit(solution)/shard_map/ppermute | solution.py:342
  63.6 4.4 %collective-permute-start.19 = (bf16[64,640]{1,0:T(8,128)(2,1)S(1)}, bf16[64,640]{1,0:T(8,128)(2,1)S(1)}, u32[]{:S(2)}, u32[]{:S(2)}) collective-permute-start(bf16[64,640]{1,0:T(8,128)(2,1)S(1)} %get-tuple-element.69), channel_id=1, source_target_pairs={{0,2},{1,3},{2,0},{3,1},{4,6},{5,7},{6,4},{7,5},{8,10},{9,11},{10,... | collective-permute-start | bytes 245768 | tf_op jit(solution)/shard_map/ppermute | solution.py:342
  (5 other events, 48.7 us)

commit v6 on v5

--- a/solution.py
+++ b/solution.py
@@ -333,10 +333,10 @@
             tiled=True,
         )
 
-    def team_permute(block, ahead, m, around=True):
+    def team_permute(block, ahead, m):
         route = [
             (t * members + n, (t + ahead) % teams * members + partner(n, m, members))
-            for t in range(teams if around else teams - ahead)
+            for t in range(teams - ahead)
             for n in range(members)
         ]
         return lax.ppermute(block, both, route)
@@ -356,7 +356,7 @@
         needed = first_needed(hop, group)
         tail = team[needed * tile_count :, :, : 2 * STRAIGHT * HD]
         block = far[-1][(needed - first) * tile_count :] if far else pick_tail(ahead, group, tile_count)
-        far += [team_permute(tail, hop, 0, False), team_permute(block, 1, 0, True)]
+        far += [team_permute(tail, hop, 0), team_permute(block, 1, 0)]
         first = needed
     asked, fact = pack_queries(history_mask, frame_index, step_index, queries[0, 0], members)
     asked, *some = lax.optimization_barrier((asked, *[ahead[m] for m in [1]]))

time: 69.3 us -> 70.9 us (1.023)
  starting transfers between devices: 39.2 us -> 49.6 us
  waiting for transfers between devices: 14.5 us -> 4.86 us
    ppermute x20, starting transfers between devices: 30.3 us -> 40.7 us  [team_permute(): return lax.ppermute(block, both, route)]
    ppermute x20, waiting for transfers between devices: 11.8 us -> 4.85 us  [team_permute(): return lax.ppermute(block, both, route)]
    all_to_all x2, waiting for transfers between devices: 2.71 us -> 0.01 us  [exchange(): lax.all_to_all(block, both, 0, 0, axis_index_groups=[[t * members + n for...]
  transfers between devices with their start and end apart: 22 -> 22, of which waited for: 10 -> 4; matrix products, arithmetic and copies ran while one was open for 1% -> 1% of each run, Pallas kernels for 10% -> 10%
where the time goes in v6:
time: 70.9 us; the launch traced here: 69.8 us
  starting transfers between devices  49.6 us (70%)
  Pallas kernels  13 us (18%)
  waiting for transfers between devices  4.86 us (7%)
  between operations  1.55 us (2%)
  other arithmetic  0.72 us (1%)
    ppermute x20, starting transfers between devices, team_permute(): return lax.ppermute(block, both, route)  40.7 us
    all_to_all x2, starting transfers between devices, exchange(): lax.all_to_all(block, both, 0, 0, axis_index_groups=[[t * members + n for...  8.95 us
    ppermute x20, waiting for transfers between devices, team_permute(): return lax.ppermute(block, both, route)  4.85 us
    pallas_call x1, Pallas kernels, attend_near(): pl.pallas_call(body, out_shape=[jax.ShapeDtypeStruct((members, tokens, wi...  3.44 us
    pallas_call x1, Pallas kernels, pack_kv(): pl.pallas_call(body, out_shape=[jax.ShapeDtypeStruct((members,) + shape,...  2.88 us
    pallas_call x1, Pallas kernels, attend_far(): pl.pallas_call(body, out_shape=[jax.ShapeDtypeStruct((tokens, width), nea...  2.08 us
    pallas_call x1, Pallas kernels, pack_queries(): pl.pallas_call(body, out_shape=[jax.ShapeDtypeStruct((members, tokens, wi...  1.99 us
    pallas_call x1, Pallas kernels, pick_tail(): pl.pallas_call(body, out_shape=jax.ShapeDtypeStruct((members - needed, to...  1.65 us
  transfers between devices with their start and end apart: 22, of which 4 were waited for; matrix products, arithmetic and copies ran while one was open for 1% of the time, Pallas kernels for 10%

profile of v6, /device:TPU:0, one launch (start us, length us, event | category | flops | bytes accessed | tf_op | source)
XLA Modules:
  0.0 69.8 jit_solution(4932053353051321169)
XLA Ops:
  0.0 2.9 %shard_map.83 = (bf16[8,64,1280]{2,1,0:T(8,128)(2,1)}, bf16[64,1280]{1,0:T(8,128)(2,1)}, bf16[64,1280]{1,0:T(8,128)(2,1)}, bf16[64,1280]{1,0:T(8,128)(2,1)}, bf1...) custom-call(bf16[64,5120]{1,0:T(8,128)(2,1)} %bitcast.22, ...), custom_call_target="tpu_custom_call" | custom-call | tf_op jit(solution)/shard_map/pallas_call | solution.py:69
  2.9 5.3 %all-to-all-start = ((bf16[8,64,1280]{2,1,0:T(8,128)(2,1)}), bf16[8,64,1280]{2,1,0:T(8,128)(2,1)S(1)}, u32[]{:S(2)}, u32[]{:S(2)}) async-start(bf16[8,64,1280]{2,1,0:T(8,128)(2,1)} %get-tuple-element.39), calls=%async_computation | async-start | bytes 2621440 | tf_op jit(solution)/shard_map/all_to_all | solution.py:327
  8.2 3.5 %collective-permute-start = (bf16[64,1280]{1,0:T(8,128)(2,1)S(1)}, bf16[64,1280]{1,0:T(8,128)(2,1)S(1)}, u32[]{:S(2)}, u32[]{:S(2)}) collective-permute-start(bf16[64,1280]{1,0:T(8,128)(2,1)S(1)} %copy-done.6), channel_id=1, source_target_pairs={{0,8},{1,9},{2,10},{3,11},{4,12},{5,13},{6,14},{7,15},{8,16},{9,17... | collective-permute-start | bytes 491528 | tf_op jit(solution)/shard_map/ppermute | solution.py:342
  11.7 3.3 %collective-permute-start.1 = (bf16[64,1280]{1,0:T(8,128)(2,1)S(1)}, bf16[64,1280]{1,0:T(8,128)(2,1)S(1)}, u32[]{:S(2)}, u32[]{:S(2)}) collective-permute-start(bf16[64,1280]{1,0:T(8,128)(2,1)S(1)} %copy-done.5), channel_id=1, source_target_pairs={{0,10},{1,11},{2,8},{3,9},{4,14},{5,15},{6,12},{7,13},{8,18},{9,19... | collective-permute-start | bytes 491528 | tf_op jit(solution)/shard_map/ppermute | solution.py:342
  15.1 4.6 %collective-permute-start.2 = (bf16[64,1280]{1,0:T(8,128)(2,1)S(1)}, bf16[64,1280]{1,0:T(8,128)(2,1)S(1)}, u32[]{:S(2)}, u32[]{:S(2)}) collective-permute-start(bf16[64,1280]{1,0:T(8,128)(2,1)S(1)} %copy-done.4), channel_id=1, source_target_pairs={{0,9},{1,8},{2,11},{3,10},{4,13},{5,12},{6,15},{7,14},{8,17},{9,16... | collective-permute-start | bytes 491528 | tf_op jit(solution)/shard_map/ppermute | solution.py:342
  19.7 2.2 %collective-permute-start.3 = (bf16[64,1280]{1,0:T(8,128)(2,1)S(1)}, bf16[64,1280]{1,0:T(8,128)(2,1)S(1)}, u32[]{:S(2)}, u32[]{:S(2)}) collective-permute-start(bf16[64,1280]{1,0:T(8,128)(2,1)S(1)} %copy-done.3), channel_id=1, source_target_pairs={{0,11},{1,10},{2,9},{3,8},{4,15},{5,14},{6,13},{7,12},{8,19},{9,18... | collective-permute-start | bytes 491528 | tf_op jit(solution)/shard_map/ppermute | solution.py:342
  21.8 3.1 %collective-permute-start.5 = (bf16[64,1280]{1,0:T(8,128)(2,1)}, bf16[64,1280]{1,0:T(8,128)(2,1)S(1)}, u32[]{:S(2)}, u32[]{:S(2)}) collective-permute-start(bf16[64,1280]{1,0:T(8,128)(2,1)} %get-tuple-element.52), channel_id=1, source_target_pairs={{0,12},{1,13},{2,14},{3,15},{4,8},{5,9},{6,10},{7,11},{8,20},{9,21... | collective-permute-start | bytes 491528 | tf_op jit(solution)/shard_map/ppermute | solution.py:342
  26.3 2.0 %shard_map.82 = (bf16[8,64,640]{2,1,0:T(8,128)(2,1)}, f32[8,128]{1,0:T(8,128)}) custom-call(s32[1,5]{1,0:T(1,128)} %history_ref.1, s32[1]{0:T(128)S(6)} %copy.10.index_ref, s32[1]{0:T(128)S(6)} %copy.9.step_ref, bf16[64,5120]{1,0:T(8,128)(2,1)} %bitcast.24), custom_call_target="tpu_custom_call" | custom-call | tf_op jit(solution)/shard_map/pallas_call | solution.py:120
  28.4 1.9 %collective-permute-start.6 = (bf16[64,1280]{1,0:T(8,128)(2,1)}, bf16[64,1280]{1,0:T(8,128)(2,1)S(1)}, u32[]{:S(2)}, u32[]{:S(2)}) collective-permute-start(bf16[64,1280]{1,0:T(8,128)(2,1)} %get-tuple-element.53), channel_id=1, source_target_pairs={{0,13},{1,12},{2,15},{3,14},{4,9},{5,8},{6,11},{7,10},{8,21},{9,20... | collective-permute-start | bytes 491528 | tf_op jit(solution)/shard_map/ppermute | solution.py:342
  30.3 2.3 %collective-permute-start.7 = (bf16[64,1280]{1,0:T(8,128)(2,1)}, bf16[64,1280]{1,0:T(8,128)(2,1)}, u32[]{:S(2)}, u32[]{:S(2)}) collective-permute-start(bf16[64,1280]{1,0:T(8,128)(2,1)} %get-tuple-element.55), channel_id=1, source_target_pairs={{0,14},{1,15},{2,12},{3,13},{4,10},{5,11},{6,8},{7,9},{8,22},{9,23... | collective-permute-start | bytes 491528 | tf_op jit(solution)/shard_map/ppermute | solution.py:342
  32.6 2.0 %collective-permute-start.8 = (bf16[64,1280]{1,0:T(8,128)(2,1)}, bf16[64,1280]{1,0:T(8,128)(2,1)}, u32[]{:S(2)}, u32[]{:S(2)}) collective-permute-start(bf16[64,1280]{1,0:T(8,128)(2,1)} %get-tuple-element.57), channel_id=1, source_target_pairs={{0,15},{1,14},{2,13},{3,12},{4,11},{5,10},{6,9},{7,8},{8,23},{9,22... | collective-permute-start | bytes 491528 | tf_op jit(solution)/shard_map/ppermute | solution.py:342
  34.6 3.6 %all-to-all-start.1 = ((bf16[8,64,640]{2,1,0:T(8,128)(2,1)}), bf16[8,64,640]{2,1,0:T(8,128)(2,1)S(1)}, u32[]{:S(2)}, u32[]{:S(2)}) async-start(bf16[8,64,640]{2,1,0:T(8,128)(2,1)} %get-tuple-element.45), calls=%async_computation.1 | async-start | bytes 1310720 | tf_op jit(solution)/shard_map/all_to_all | solution.py:327
  38.4 1.9 %collective-permute-start.4 = (bf16[2,64,768]{2,1,0:T(8,128)(2,1)S(1)}, bf16[2,64,768]{2,1,0:T(8,128)(2,1)S(1)}, u32[]{:S(2)}, u32[]{:S(2)}) collective-permute-start(bf16[2,64,768]{2,1,0:T(8,128)(2,1)S(1)} %slice.39), channel_id=1, source_target_pairs={{0,16},{1,17},{2,18},{3,19},{4,20},{5,21},{6,22},{7,23},{8,24},{9,... | collective-permute-start | bytes 589832 | tf_op jit(solution)/shard_map/ppermute | solution.py:342
  41.0 1.8 %collective-permute-start.10 = (f32[8,128]{1,0:T(8,128)S(1)}, f32[8,128]{1,0:T(8,128)S(1)}, u32[]{:S(2)}, u32[]{:S(2)}) collective-permute-start(f32[8,128]{1,0:T(8,128)S(1)} %copy-done.1), channel_id=1, source_target_pairs={{0,4},{1,5},{2,6},{3,7},{4,0},{5,1},{6,2},{7,3},{8,12},{9,13},{10,... | collective-permute-start | bytes 12296 | tf_op jit(solution)/shard_map/ppermute | solution.py:342
  43.0 1.7 %shard_map.85 = bf16[2,64,512]{2,1,0:T(8,128)(2,1)} custom-call(bf16[64,1280]{1,0:T(8,128)(2,1)S(1)} %collective-permute-done.refs_0_, bf16[64,1280]{1,0:T(8,128)(2,1)S(1)} %collective-permute-done.2.refs_1_, bf16[64,1280]{1,0:T(8,128)(2,1)S(1)} %collective-permute-done.1.refs_2_, bf16[64,1280]{1,0:T(8,128)(2,1)S(1)} %collective-permute-done.3.refs_3_, ...), custom_call_target="tpu_custom_call" | custom-call | tf_op jit(solution)/shard_map/pallas_call | solution.py:93
  44.6 8.1 %collective-permute-start.12 = (bf16[2,64,512]{2,1,0:T(8,128)(2,1)}, bf16[2,64,512]{2,1,0:T(8,128)(2,1)}, u32[]{:S(2)}, u32[]{:S(2)}) collective-permute-start(bf16[2,64,512]{2,1,0:T(8,128)(2,1)} %shard_map.85), channel_id=1, source_target_pairs={{0,8},{1,9},{2,10},{3,11},{4,12},{5,13},{6,14},{7,15},{8,16},{9,17... | collective-permute-start | bytes 393224 | tf_op jit(solution)/shard_map/ppermute | solution.py:342
  52.8 3.4 %shard_map.84 = (bf16[8,64,640]{2,1,0:T(8,128)(2,1)S(1)}, bf16[8,64,1280]{2,1,0:T(8,128)(2,1)S(1)}, f32[4,8,128]{2,1,0:T(8,128)S(1)}) custom-call(f32[4,5]{1,0:T(4,128)S(1)} %constant_dynamic-slice_fusion.gain_ref, f32[5,128,128]{2,1,0:T(8,128)S(1)} %or_select_fusion.bias_ref, bf16[8,64,640]{2,1,0:T(8,128)(2,1)S(1)} %all-to-all-done.1.asked_ref, ...), custom_call_target="tpu_custom_call" | custom-call | flops 1006632960 | bytes 7864320 | tf_op jit(solution)/shard_map/pallas_call | solution.py:250
  56.2 2.1 %shard_map.86 = (bf16[64,640]{1,0:T(8,128)(2,1)S(1)}, bf16[64,640]{1,0:T(8,128)(2,1)S(1)}, bf16[64,640]{1,0:T(8,128)(2,1)S(1)}, bf16[64,640]{1,0:T(8,128)(2,1)S(...) custom-call(f32[4,5]{1,0:T(4,128)S(1)} %constant_dynamic-slice_fusio, ...), custom_call_target="tpu_custom_call" | custom-call | flops 251658240 | bytes 1966080 | tf_op jit(solution)/shard_map/pallas_call | solution.py:289
  59.0 4.1 %collective-permute-start.16 = (bf16[64,640]{1,0:T(8,128)(2,1)S(1)}, bf16[64,640]{1,0:T(8,128)(2,1)S(1)}, u32[]{:S(2)}, u32[]{:S(2)}) collective-permute-start(bf16[64,640]{1,0:T(8,128)(2,1)S(1)} %get-tuple-element.66), channel_id=1, source_target_pairs={{0,6},{1,7},{2,4},{3,5},{4,2},{5,3},{6,0},{7,1},{8,14},{9,15},{10,... | collective-permute-start | bytes 245768 | tf_op jit(solution)/shard_map/ppermute | solution.py:342
  63.1 1.1 %collective-permute-done.13.refs_0_ = bf16[64,640]{1,0:T(8,128)(2,1)S(1)} collective-permute-done((bf16[64,640]{1,0:T(8,128)(2,1)S(1)}, bf16[64,640]{1,0:T(8,128)(2,1)S(1)}, u32[]{:S(2)}, u32[]{:S(2)}) %collective-permute-start.13) | collective-permute-done | bytes 81952 | tf_op jit(solution)/shard_map/ppermute | solution.py:342
  64.2 1.0 %collective-permute-start.19 = (bf16[64,640]{1,0:T(8,128)(2,1)S(1)}, bf16[64,640]{1,0:T(8,128)(2,1)S(1)}, u32[]{:S(2)}, u32[]{:S(2)}) collective-permute-start(bf16[64,640]{1,0:T(8,128)(2,1)S(1)} %get-tuple-element.69), channel_id=1, source_target_pairs={{0,2},{1,3},{2,0},{3,1},{4,6},{5,7},{6,4},{7,5},{8,10},{9,11},{10,... | collective-permute-start | bytes 245768 | tf_op jit(solution)/shard_map/ppermute | solution.py:342
  65.2 1.7 %collective-permute-done.16.refs_3_ = bf16[64,640]{1,0:T(8,128)(2,1)S(1)} collective-permute-done((bf16[64,640]{1,0:T(8,128)(2,1)S(1)}, bf16[64,640]{1,0:T(8,128)(2,1)S(1)}, u32[]{:S(2)}, u32[]{:S(2)}) %collective-permute-start.16) | collective-permute-done | bytes 81952 | tf_op jit(solution)/shard_map/ppermute | solution.py:342
  66.9 1.3 %collective-permute-done.17.refs_4_ = bf16[64,640]{1,0:T(8,128)(2,1)S(1)} collective-permute-done((bf16[64,640]{1,0:T(8,128)(2,1)S(1)}, bf16[64,640]{1,0:T(8,128)(2,1)S(1)}, u32[]{:S(2)}, u32[]{:S(2)}) %collective-permute-start.17) | collective-permute-done | bytes 81952 | tf_op jit(solution)/shard_map/ppermute | solution.py:342
  68.9 0.9 %shard_map.87 = bf16[64,5120]{1,0:T(8,128)(2,1)} custom-call(bf16[64,640]{1,0:T(8,128)(2,1)S(1)} %collective-permute-done.13.refs_0_, bf16[64,640]{1,0:T(8,128)(2,1)S(1)} %collective-permute-done.14.refs_1_, bf16[64,640]{1,0:T(8,128)(2,1)S(1)} %collective-permute-done.15.refs_2_, bf16[64,640]{1,0:T(8,128)(2,1)S(1)} %collective-permute-done.16.refs_3_, ...), custom_call_target="tpu_custom_call" | custom-call | tf_op jit(solution)/shard_map/pallas_call | solution.py:141
  (46 shorter events, 2.5 us)
Async XLA Ops:
  0.0 52.7 %copy-start = (f32[4,40]{1,0:T(4,128)S(1)}, f32[4,40]{1,0:T(4,128)}, u32[]{:S(2)}) copy-start(f32[4,40]{1,0:T(4,128)} %param.15) | copy-start | bytes 1924
  2.9 25.4 %copy-start.2 = (s32[40,9]{0,1:T(8,128)S(1)}, s32[40,9]{0,1:T(8,128)}, u32[]{:S(2)}) copy-start(s32[40,9]{0,1:T(8,128)} %param.13) | copy-start | bytes 4324
  2.9 31.7 %all-to-all-start = ((bf16[8,64,1280]{2,1,0:T(8,128)(2,1)}), bf16[8,64,1280]{2,1,0:T(8,128)(2,1)S(1)}, u32[]{:S(2)}, u32[]{:S(2)}) async-start(bf16[8,64,1280]{2,1,0:T(8,128)(2,1)} %get-tuple-element.39), calls=%async_computation | async-start | bytes 2621440 | tf_op jit(solution)/shard_map/all_to_all | solution.py:327
  8.2 20.1 %collective-permute-start = (bf16[64,1280]{1,0:T(8,128)(2,1)S(1)}, bf16[64,1280]{1,0:T(8,128)(2,1)S(1)}, u32[]{:S(2)}, u32[]{:S(2)}) collective-permute-start(bf16[64,1280]{1,0:T(8,128)(2,1)S(1)} %copy-done.6), channel_id=1, source_target_pairs={{0,8},{1,9},{2,10},{3,11},{4,12},{5,13},{6,14},{7,15},{8,16},{9,17... | collective-permute-start | bytes 491528 | tf_op jit(solution)/shard_map/ppermute | solution.py:342
  11.7 18.6 %collective-permute-start.1 = (bf16[64,1280]{1,0:T(8,128)(2,1)S(1)}, bf16[64,1280]{1,0:T(8,128)(2,1)S(1)}, u32[]{:S(2)}, u32[]{:S(2)}) collective-permute-start(bf16[64,1280]{1,0:T(8,128)(2,1)S(1)} %copy-done.5), channel_id=1, source_target_pairs={{0,10},{1,11},{2,8},{3,9},{4,14},{5,15},{6,12},{7,13},{8,18},{9,19... | collective-permute-start | bytes 491528 | tf_op jit(solution)/shard_map/ppermute | solution.py:342
  15.1 17.6 %collective-permute-start.2 = (bf16[64,1280]{1,0:T(8,128)(2,1)S(1)}, bf16[64,1280]{1,0:T(8,128)(2,1)S(1)}, u32[]{:S(2)}, u32[]{:S(2)}) collective-permute-start(bf16[64,1280]{1,0:T(8,128)(2,1)S(1)} %copy-done.4), channel_id=1, source_target_pairs={{0,9},{1,8},{2,11},{3,10},{4,13},{5,12},{6,15},{7,14},{8,17},{9,16... | collective-permute-start | bytes 491528 | tf_op jit(solution)/shard_map/ppermute | solution.py:342
  19.7 14.9 %collective-permute-start.3 = (bf16[64,1280]{1,0:T(8,128)(2,1)S(1)}, bf16[64,1280]{1,0:T(8,128)(2,1)S(1)}, u32[]{:S(2)}, u32[]{:S(2)}) collective-permute-start(bf16[64,1280]{1,0:T(8,128)(2,1)S(1)} %copy-done.3), channel_id=1, source_target_pairs={{0,11},{1,10},{2,9},{3,8},{4,15},{5,14},{6,13},{7,12},{8,19},{9,18... | collective-permute-start | bytes 491528 | tf_op jit(solution)/shard_map/ppermute | solution.py:342
  21.8 19.2 %collective-permute-start.5 = (bf16[64,1280]{1,0:T(8,128)(2,1)}, bf16[64,1280]{1,0:T(8,128)(2,1)S(1)}, u32[]{:S(2)}, u32[]{:S(2)}) collective-permute-start(bf16[64,1280]{1,0:T(8,128)(2,1)} %get-tuple-element.52), channel_id=1, source_target_pairs={{0,12},{1,13},{2,14},{3,15},{4,8},{5,9},{6,10},{7,11},{8,20},{9,21... | collective-permute-start | bytes 491528 | tf_op jit(solution)/shard_map/ppermute | solution.py:342
  28.4 14.5 %collective-permute-start.6 = (bf16[64,1280]{1,0:T(8,128)(2,1)}, bf16[64,1280]{1,0:T(8,128)(2,1)S(1)}, u32[]{:S(2)}, u32[]{:S(2)}) collective-permute-start(bf16[64,1280]{1,0:T(8,128)(2,1)} %get-tuple-element.53), channel_id=1, source_target_pairs={{0,13},{1,12},{2,15},{3,14},{4,9},{5,8},{6,11},{7,10},{8,21},{9,20... | collective-permute-start | bytes 491528 | tf_op jit(solution)/shard_map/ppermute | solution.py:342
  30.3 10.4 %collective-permute-start.7 = (bf16[64,1280]{1,0:T(8,128)(2,1)}, bf16[64,1280]{1,0:T(8,128)(2,1)}, u32[]{:S(2)}, u32[]{:S(2)}) collective-permute-start(bf16[64,1280]{1,0:T(8,128)(2,1)} %get-tuple-element.55), channel_id=1, source_target_pairs={{0,14},{1,15},{2,12},{3,13},{4,10},{5,11},{6,8},{7,9},{8,22},{9,23... | collective-permute-start | bytes 491528 | tf_op jit(solution)/shard_map/ppermute | solution.py:342
  32.6 10.4 %collective-permute-start.8 = (bf16[64,1280]{1,0:T(8,128)(2,1)}, bf16[64,1280]{1,0:T(8,128)(2,1)}, u32[]{:S(2)}, u32[]{:S(2)}) collective-permute-start(bf16[64,1280]{1,0:T(8,128)(2,1)} %get-tuple-element.57), channel_id=1, source_target_pairs={{0,15},{1,14},{2,13},{3,12},{4,11},{5,10},{6,9},{7,8},{8,23},{9,22... | collective-permute-start | bytes 491528 | tf_op jit(solution)/shard_map/ppermute | solution.py:342
  34.6 18.2 %all-to-all-start.1 = ((bf16[8,64,640]{2,1,0:T(8,128)(2,1)}), bf16[8,64,640]{2,1,0:T(8,128)(2,1)S(1)}, u32[]{:S(2)}, u32[]{:S(2)}) async-start(bf16[8,64,640]{2,1,0:T(8,128)(2,1)} %get-tuple-element.45), calls=%async_computation.1 | async-start | bytes 1310720 | tf_op jit(solution)/shard_map/all_to_all | solution.py:327
  38.4 14.3 %collective-permute-start.4 = (bf16[2,64,768]{2,1,0:T(8,128)(2,1)S(1)}, bf16[2,64,768]{2,1,0:T(8,128)(2,1)S(1)}, u32[]{:S(2)}, u32[]{:S(2)}) collective-permute-start(bf16[2,64,768]{2,1,0:T(8,128)(2,1)S(1)} %slice.39), channel_id=1, source_target_pairs={{0,16},{1,17},{2,18},{3,19},{4,20},{5,21},{6,22},{7,23},{8,24},{9,... | collective-permute-start | bytes 589832 | tf_op jit(solution)/shard_map/ppermute | solution.py:342
  40.8 12.0 %collective-permute-start.9 = (f32[8,128]{1,0:T(8,128)S(1)}, f32[8,128]{1,0:T(8,128)S(1)}, u32[]{:S(2)}, u32[]{:S(2)}) collective-permute-start(f32[8,128]{1,0:T(8,128)S(1)} %copy-done.1), channel_id=1, source_target_pairs={{0,2},{1,3},{2,0},{3,1},{4,6},{5,7},{6,4},{7,5},{8,10},{9,11},{10,... | collective-permute-start | bytes 12296 | tf_op jit(solution)/shard_map/ppermute | solution.py:342
  41.0 11.7 %collective-permute-start.10 = (f32[8,128]{1,0:T(8,128)S(1)}, f32[8,128]{1,0:T(8,128)S(1)}, u32[]{:S(2)}, u32[]{:S(2)}) collective-permute-start(f32[8,128]{1,0:T(8,128)S(1)} %copy-done.1), channel_id=1, source_target_pairs={{0,4},{1,5},{2,6},{3,7},{4,0},{5,1},{6,2},{7,3},{8,12},{9,13},{10,... | collective-permute-start | bytes 12296 | tf_op jit(solution)/shard_map/ppermute | solution.py:342
  42.9 9.9 %collective-permute-start.11 = (f32[8,128]{1,0:T(8,128)S(1)}, f32[8,128]{1,0:T(8,128)S(1)}, u32[]{:S(2)}, u32[]{:S(2)}) collective-permute-start(f32[8,128]{1,0:T(8,128)S(1)} %copy-done.1), channel_id=1, source_target_pairs={{0,6},{1,7},{2,4},{3,5},{4,2},{5,3},{6,0},{7,1},{8,14},{9,15},{10,... | collective-permute-start | bytes 12296 | tf_op jit(solution)/shard_map/ppermute | solution.py:342
  44.6 11.6 %collective-permute-start.12 = (bf16[2,64,512]{2,1,0:T(8,128)(2,1)}, bf16[2,64,512]{2,1,0:T(8,128)(2,1)}, u32[]{:S(2)}, u32[]{:S(2)}) collective-permute-start(bf16[2,64,512]{2,1,0:T(8,128)(2,1)} %shard_map.85), channel_id=1, source_target_pairs={{0,8},{1,9},{2,10},{3,11},{4,12},{5,13},{6,14},{7,15},{8,16},{9,17... | collective-permute-start | bytes 393224 | tf_op jit(solution)/shard_map/ppermute | solution.py:342
  58.3 5.9 %collective-permute-start.13 = (bf16[64,640]{1,0:T(8,128)(2,1)S(1)}, bf16[64,640]{1,0:T(8,128)(2,1)S(1)}, u32[]{:S(2)}, u32[]{:S(2)}) collective-permute-start(bf16[64,640]{1,0:T(8,128)(2,1)S(1)} %get-tuple-element.63), channel_id=1, source_target_pairs={{0,5},{1,4},{2,7},{3,6},{4,1},{5,0},{6,3},{7,2},{8,13},{9,12},{10,... | collective-permute-start | bytes 245768 | tf_op jit(solution)/shard_map/ppermute | solution.py:342
  58.4 5.8 %collective-permute-start.14 = (bf16[64,640]{1,0:T(8,128)(2,1)S(1)}, bf16[64,640]{1,0:T(8,128)(2,1)S(1)}, u32[]{:S(2)}, u32[]{:S(2)}) collective-permute-start(bf16[64,640]{1,0:T(8,128)(2,1)S(1)} %get-tuple-element.64), channel_id=1, source_target_pairs={{0,4},{1,5},{2,6},{3,7},{4,0},{5,1},{6,2},{7,3},{8,12},{9,13},{10,... | collective-permute-start | bytes 245768 | tf_op jit(solution)/shard_map/ppermute | solution.py:342
  58.5 6.7 %collective-permute-start.15 = (bf16[64,640]{1,0:T(8,128)(2,1)S(1)}, bf16[64,640]{1,0:T(8,128)(2,1)S(1)}, u32[]{:S(2)}, u32[]{:S(2)}) collective-permute-start(bf16[64,640]{1,0:T(8,128)(2,1)S(1)} %get-tuple-element.65), channel_id=1, source_target_pairs={{0,7},{1,6},{2,5},{3,4},{4,3},{5,2},{6,1},{7,0},{8,15},{9,14},{10,... | collective-permute-start | bytes 245768 | tf_op jit(solution)/shard_map/ppermute | solution.py:342
  59.0 8.0 %collective-permute-start.16 = (bf16[64,640]{1,0:T(8,128)(2,1)S(1)}, bf16[64,640]{1,0:T(8,128)(2,1)S(1)}, u32[]{:S(2)}, u32[]{:S(2)}) collective-permute-start(bf16[64,640]{1,0:T(8,128)(2,1)S(1)} %get-tuple-element.66), channel_id=1, source_target_pairs={{0,6},{1,7},{2,4},{3,5},{4,2},{5,3},{6,0},{7,1},{8,14},{9,15},{10,... | collective-permute-start | bytes 245768 | tf_op jit(solution)/shard_map/ppermute | solution.py:342
  63.1 5.2 %collective-permute-start.17 = (bf16[64,640]{1,0:T(8,128)(2,1)S(1)}, bf16[64,640]{1,0:T(8,128)(2,1)S(1)}, u32[]{:S(2)}, u32[]{:S(2)}) collective-permute-start(bf16[64,640]{1,0:T(8,128)(2,1)S(1)} %get-tuple-element.67), channel_id=1, source_target_pairs={{0,1},{1,0},{2,3},{3,2},{4,5},{5,4},{6,7},{7,6},{8,9},{9,8},{10,11... | collective-permute-start | bytes 245768 | tf_op jit(solution)/shard_map/ppermute | solution.py:342
  64.2 4.7 %collective-permute-start.18 = (bf16[64,640]{1,0:T(8,128)(2,1)S(1)}, bf16[64,640]{1,0:T(8,128)(2,1)S(1)}, u32[]{:S(2)}, u32[]{:S(2)}) collective-permute-start(bf16[64,640]{1,0:T(8,128)(2,1)S(1)} %get-tuple-element.68), channel_id=1, source_target_pairs={{0,3},{1,2},{2,1},{3,0},{4,7},{5,6},{6,5},{7,4},{8,11},{9,10},{10,... | collective-permute-start | bytes 245768 | tf_op jit(solution)/shard_map/ppermute | solution.py:342
  64.2 4.7 %collective-permute-start.19 = (bf16[64,640]{1,0:T(8,128)(2,1)S(1)}, bf16[64,640]{1,0:T(8,128)(2,1)S(1)}, u32[]{:S(2)}, u32[]{:S(2)}) collective-permute-start(bf16[64,640]{1,0:T(8,128)(2,1)S(1)} %get-tuple-element.69), channel_id=1, source_target_pairs={{0,2},{1,3},{2,0},{3,1},{4,6},{5,7},{6,4},{7,5},{8,10},{9,11},{10,... | collective-permute-start | bytes 245768 | tf_op jit(solution)/shard_map/ppermute | solution.py:342
  (5 other events, 55.6 us)
